TPU v7x, 256 devices: a whole 4x4x8 slice. The times are simulated.
256 devices in a mesh: blk: 64 (over z, x, y_hi), inner: 4 (over y_lo, core).
Axes of the slice: x: 4, y: 4 (y_hi: 2, y_lo: 2; y = y_hi * 2 + y_lo), z: 8, core: 2. Of those that a mesh axis runs over, the one named last changes fastest.
Arguments:
- image_embeds: bfloat16 [81920, 1152], P(('blk', 'inner')), may hold values from -0.59765625 to 0.59765625
- text_embeds: bfloat16 [81920, 1152], P(('blk', 'inner')), may hold values from -0.59765625 to 0.59765625
- positive: int32 [81920], P(('blk', 'inner')), may hold values from 0 to 1279, as said below
- logit_scale: float32 [1], replicated, may hold values from 2 to 4
- logit_bias: float32 [1], replicated, may hold values from -2 to -0.5
Outputs:
- grad_images: float32 [81920, 1152], P(('blk', 'inner'))
- grad_texts: float32 [81920, 1152], P(('blk', 'inner'))
Inputs may be any that keep to these rules, and one draw needn't show every extreme that they name: `positive`: within each aligned block of 1280 entries every value 0 .. 1279 appears exactly once.
All inputs are finite; a program needn't handle non-finite values.
Results may differ from a plain program's by a relative error of at most 0.0024.
Values may be sent and summed in bfloat16 or wider, within the bound.
No kernel may reach another device: no remote copies, remote signals or barrier semaphores. Data moves between devices by JAX's collectives and lax.ppermute only.
A program may use at most 64 MiB of HBM per device.

v0:
```python
import jax
import jax.numpy as jnp
from jax import lax
from jax.sharding import PartitionSpec as P

STEPS = 3


def passed_along(block, axis, distance):
    devices = range(lax.axis_size(axis))
    route = [((i - distance) % len(devices), i) for i in devices]
    return lax.ppermute(block, axis, route)


def tile_grads(image_rows, text_rows, onehot, scale_value, bias_value):
    raw_scores = lax.dot_general(
        image_rows, text_rows, (((1,), (1,)), ((), ())), preferred_element_type=jnp.float32
    )
    sigmoid_term = jax.nn.sigmoid(scale_value * raw_scores + bias_value)
    if onehot is not None:
        sigmoid_term = sigmoid_term - onehot
    tile_bf = (scale_value * sigmoid_term).astype(jnp.bfloat16)
    grad_left = jnp.dot(tile_bf, text_rows, preferred_element_type=jnp.float32)
    grad_right = lax.dot_general(
        tile_bf, image_rows, (((0,), (0,)), ((), ())), preferred_element_type=jnp.float32
    )
    return (grad_left, grad_right)


def local(image_embeds, text_embeds, positive, logit_scale, logit_bias):
    scale_value = logit_scale[0]
    bias_value = logit_bias[0]
    group_text = lax.all_gather(text_embeds, "inner", axis=0, tiled=True)
    group_rows = group_text.shape[0]
    onehot = (positive[:, None] == jnp.arange(group_rows, dtype=jnp.int32)[None, :]).astype(
        jnp.float32
    )
    grad_images = jnp.zeros(image_embeds.shape, jnp.float32)
    moving = group_text
    carried = jnp.zeros(group_text.shape, jnp.float32)
    for cycle_step in range(STEPS):
        first_table = onehot if cycle_step == 0 else None
        grad_left, grad_right = tile_grads(
            image_embeds, moving, first_table, scale_value, bias_value
        )
        grad_images = grad_images + grad_left
        carried = carried + grad_right
        if cycle_step + 1 < STEPS:
            moving = passed_along(moving, "blk", 1)
            carried = passed_along(carried, "blk", 1)
    group_grad = passed_along(carried, "blk", -(STEPS - 1))
    grad_texts = lax.psum_scatter(group_grad, "inner", scatter_dimension=0, tiled=True)
    return (grad_images, grad_texts)


def solution(mesh):
    placed = (P(("blk", "inner"), None), P(("blk", "inner"), None), P(("blk", "inner")), P(), P())
    return jax.shard_map(
        local,
        mesh=mesh,
        in_specs=placed,
        out_specs=(P(("blk", "inner"), None), P(("blk", "inner"), None)),
        check_vma=False,
    )
```

profile of v0, /device:TPU:1, one launch (start us, length us, event | category | flops | bytes accessed | tf_op | source)
XLA Modules:
  0.0 658.3 jit_solution(1708254320749448249)
XLA Ops:
  7.2 0.0 copy-start
  7.2 0.0 all-gather.2.cloned.1.call-start
  7.2 0.7 all-gather.2.cloned.1.call-update
  7.9 0.0 reduce-scatter.2.cloned.1.call-start
  9.2 43.6 %all-gather.2.cloned.1.call-done = bf16[1280,1152]{1,0:T(8,128)(2,1)} async-done(((bf16[320,1152]{1,0:T(8,128)(2,1)}), bf16[1280,1152]{1,0:T(8,128)(2,1)}) %all-gather.2.cloned.1.call-update) | async-done | bytes 2949136 | tf_op jit(solution)/shard_map/all_gather | solution.py:33
  52.8 0.0 copy-done
  52.8 3.2 fusion.19
  56.1 0.0 copy-start.1
  56.1 1.8 fusion.23
  57.9 2.5 collective-permute-start.2
  60.4 0.0 copy-done.1
  60.4 1.4 collective-permute-start
  61.9 194.0 %collective-permute-done = bf16[1280,1152]{1,0:T(8,128)(2,1)S(1)} collective-permute-done((bf16[1280,1152]{1,0:T(8,128)(2,1)S(1)}, bf16[1280,1152]{1,0:T(8,128)(2,1)S(1)}, u32[]{:S(2)}, u32[]{:S(2)}) %collective-permute-start) | collective-permute-done | bytes 2949152 | tf_op jit(solution)/shard_map/ppermute | solution.py:12
  255.9 1.3 fusion.21
  257.2 0.0 collective-permute-done.2
  257.2 1.9 convolution_add_fusion
  259.1 0.1 collective-permute-start.3
  259.2 0.4 collective-permute-start.1
  259.6 196.5 %collective-permute-done.1 = bf16[1280,1152]{1,0:T(8,128)(2,1)S(1)} collective-permute-done((bf16[1280,1152]{1,0:T(8,128)(2,1)S(1)}, bf16[1280,1152]{1,0:T(8,128)(2,1)S(1)}, u32[]{:S(2)}, u32[]{:S(2)}) %collective-permute-start.1) | collective-permute-done | bytes 2949152 | tf_op jit(solution)/shard_map/ppermute | solution.py:12
  456.1 1.3 fusion.20
  457.4 0.3 copy-done.4
  457.7 1.8 fusion.24
  459.6 0.0 collective-permute-done.3
  459.6 3.4 add.47
  463.0 0.1 collective-permute-start.4
  463.1 127.1 %collective-permute-done.4 = f32[1280,1152]{1,0:T(8,128)} collective-permute-done((f32[1280,1152]{1,0:T(8,128)S(1)}, f32[1280,1152]{1,0:T(8,128)}, u32[]{:S(2)}, u32[]{:S(2)}) %collective-permute-start.4) | collective-permute-done | bytes 5898272 | tf_op jit(solution)/shard_map/ppermute | solution.py:12
  590.2 0.0 reduce-scatter.2.cloned.1.call-update
  590.3 3.2 fusion.22
  593.5 1.3 convolution_add_fusion.2
  594.8 0.5 copy-done.5
  595.3 2.4 convolution_add_fusion.1
  597.7 53.8 %reduce-scatter.2.cloned.1.call-done = f32[320,1152]{1,0:T(8,128)} async-done(((f32[1280,1152]{1,0:T(8,128)}), f32[320,1152]{1,0:T(8,128)}) %reduce-scatter.2.cloned.1.call-update) | async-done | bytes 1474576 | tf_op jit(solution)/shard_map/reduce_scatter | solution.py:52
  (6 shorter events, 0.0 us)
Async XLA Ops:
  7.2 45.7 %copy-start = (bf16[320,1152]{1,0:T(8,128)(2,1)S(1)}, bf16[320,1152]{1,0:T(8,128)(2,1)}, u32[]{:S(2)}) copy-start(bf16[320,1152]{1,0:T(8,128)(2,1)} %param.5) | copy-start | bytes 2211844
  7.2 45.6 %all-gather.2.cloned.1.call-start = ((), (), s32[]{:S(2)}) async-start(), calls=%async_computation.1 | async-start | bytes 3686400 | tf_op jit(solution)/shard_map/all_gather | solution.py:33
  7.9 643.6 %reduce-scatter.2.cloned.1.call-start = ((), (), s32[]{:S(2)}) async-start(), calls=%async_computation.2 | async-start | bytes 7372800 | tf_op jit(solution)/shard_map/reduce_scatter | solution.py:52
  56.1 4.4 copy-start.1
  57.9 199.3 %collective-permute-start.2 = (f32[1280,1152]{1,0:T(8,128)S(1)}, f32[1280,1152]{1,0:T(8,128)S(1)}, u32[]{:S(2)}, u32[]{:S(2)}) collective-permute-start(f32[1280,1152]{1,0:T(8,128)S(1)} %fusion.23), channel_id=1, source_target_pairs={{252,0},{0,4},{4,8},{8,12},{12,16},{16,20},{20,24},{24,28},{28,32}... | collective-permute-start | bytes 17694728 | tf_op jit(solution)/shard_map/ppermute | solution.py:12
  60.4 195.4 %collective-permute-start = (bf16[1280,1152]{1,0:T(8,128)(2,1)S(1)}, bf16[1280,1152]{1,0:T(8,128)(2,1)S(1)}, u32[]{:S(2)}, u32[]{:S(2)}) collective-permute-start(bf16[1280,1152]{1,0:T(8,128)(2,1)S(1)} %copy-done.1), channel_id=1, source_target_pairs={{252,0},{0,4},{4,8},{8,12},{12,16},{16,20},{20,24},{24,28},{28,32}... | collective-permute-start | bytes 8847368 | tf_op jit(solution)/shard_map/ppermute | solution.py:12
  255.9 3.3 copy-start.2
  259.1 200.5 %collective-permute-start.3 = (f32[1280,1152]{1,0:T(8,128)S(1)}, f32[1280,1152]{1,0:T(8,128)}, u32[]{:S(2)}, u32[]{:S(2)}) collective-permute-start(f32[1280,1152]{1,0:T(8,128)S(1)} %convolution_add_fusion), channel_id=1, source_target_pairs={{252,0},{0,4},{4,8},{8,12},{12,16},{16,20},{20,24},{24,28},{28,32}... | collective-permute-start | bytes 17694728 | tf_op jit(solution)/shard_map/ppermute | solution.py:12
  259.2 196.9 %collective-permute-start.1 = (bf16[1280,1152]{1,0:T(8,128)(2,1)S(1)}, bf16[1280,1152]{1,0:T(8,128)(2,1)S(1)}, u32[]{:S(2)}, u32[]{:S(2)}) collective-permute-start(bf16[1280,1152]{1,0:T(8,128)(2,1)S(1)} %collective-permute-done), channel_id=1, source_target_pairs={{252,0},{0,4},{4,8},{8,12},{12,16},{16,20},{20,24},{24,28},{28,32}... | collective-permute-start | bytes 8847368 | tf_op jit(solution)/shard_map/ppermute | solution.py:12
  456.1 1.7 copy-start.4
  463.0 127.2 %collective-permute-start.4 = (f32[1280,1152]{1,0:T(8,128)S(1)}, f32[1280,1152]{1,0:T(8,128)}, u32[]{:S(2)}, u32[]{:S(2)}) collective-permute-start(f32[1280,1152]{1,0:T(8,128)S(1)} %add.47), channel_id=1, source_target_pairs={{8,0},{12,4},{16,8},{20,12},{24,16},{28,20},{32,24},{36,28},{40,32... | collective-permute-start | bytes 17694728 | tf_op jit(solution)/shard_map/ppermute | solution.py:12
  590.3 3.2 copy-start.3
  593.5 1.8 copy-start.5
Sparse Core Ops, SparseCore 0:
  9.8 42.9 all-gather.1
  590.4 61.0 reduce-scatter.1
where the time goes:
time: 659 us; the launch traced here: 658 us
  waiting for transfers between devices  616 us (93%)
  matrix products  18.3 us (3%)
  between operations  15.5 us (2%)
    ppermute x5, waiting for transfers between devices, passed_along(): return lax.ppermute(block, axis, route)  518 us
    reduce_scatter x1, waiting for transfers between devices, local(): lax.psum_scatter(group_grad, 'inner', scatter_dimension=0, tiled=True)  53.8 us
    all_gather x1, waiting for transfers between devices, local(): group_text = lax.all_gather(text_embeds, 'inner', axis=0, tiled=True)  43.6 us
  transfers between devices with their start and end apart: 7, of which 5 were waited for; matrix products, arithmetic and copies ran while one was open for 2% of the time, Pallas kernels for 0%

commit v1 on v0

v1 whole, which is shorter than its diff:
```python
import jax
import jax.numpy as jnp
from jax import lax
from jax.sharding import PartitionSpec as P

AXES = ("blk", "inner")
BF = jnp.bfloat16
F32 = jnp.float32
CHUNKS = 2


def routes(nblk, ninner):
    def route(place):
        out = []
        for blk in range(nblk):
            for inner in range(ninner):
                col, half, low, core = blk // 2, blk % 2, inner // 2, inner % 2
                c, h, l, k = place(col, half, low, core)
                out.append((blk * ninner + inner, ((c % (nblk // 2)) * 2 + h) * ninner + l * 2 + k))
        return out

    return {
        "core": route(lambda c, h, l, k: (c, h, l, 1 - k)),
        "pair": route(lambda c, h, l, k: (c, h, 1 - l, k)),
        "mirror": route(lambda c, h, l, k: (c, 1 - h, 1 - l, k)),
        "next": route(lambda c, h, l, k: (c + 1, h, l, k)),
        "prev": route(lambda c, h, l, k: (c - 1, h, l, k)),
    }


def nt(a, b):
    return lax.dot_general(a, b, (((1,), (1,)), ((), ())), preferred_element_type=F32)


def tn(a, b):
    return lax.dot_general(a, b, (((0,), (0,)), ((), ())), preferred_element_type=F32)


def nn(a, b):
    return jnp.dot(a, b, preferred_element_type=F32)


def local(image, text, positive, logit_scale, logit_bias):
    nblk, ninner = lax.axis_size("blk"), lax.axis_size("inner")
    way = routes(nblk, ninner)
    move = lambda v, name: lax.ppermute(v, AXES, way[name])
    scale, bias = logit_scale[0], logit_bias[0]
    upper = (lax.axis_index("blk") % 2) == 1
    rows = text.shape[0]
    cut = rows // CHUNKS
    parts = [slice(i * cut, (i + 1) * cut) for i in range(CHUNKS)]

    text_x = [move(text[p], "next") for p in parts]
    image_n = move(image, "pair")
    image_c = move(image, "core")
    pos_c = move(positive, "core")
    pos_n = move(jnp.concatenate([positive, pos_c]), "pair")
    pos = jnp.concatenate([positive, pos_c, pos_n])
    text_m = [move(jnp.where(upper, t, text[p]), "mirror") for t, p in zip(text_x, parts)]
    image_nc = move(image_n, "core")
    images = jnp.concatenate([image, image_c, image_n, image_nc])
    at = pos - lax.axis_index("inner") * rows

    def tile(texts, first):
        s = jax.nn.sigmoid(scale * nt(texts, images) + bias)
        if first:
            s = s - (jnp.arange(rows, dtype=jnp.int32)[:, None] == at[None, :]).astype(F32)
        return (scale * s).astype(BF)

    tile0 = tile(text, True)
    tile_x = [tile(t, False) for t in text_x]
    grad_t = nn(tile0, images)
    grad_x = [nn(t, images) for t in tile_x]
    grad_i = tn(tile0, text) + sum(tn(a, b) for a, b in zip(tile_x, text_x))
    tile_m = [tile(t, False) for t in text_m]
    grad_m = [nn(t, images).astype(BF) for t in tile_m]
    back_m = [move(g, "mirror") for g in grad_m]
    send_x = [(g + jnp.where(upper, b.astype(F32), 0.0)).astype(BF) for g, b in zip(grad_x, back_m)]
    back_x = [move(g, "prev") for g in send_x]
    grad_i = grad_i + sum(tn(a, b) for a, b in zip(tile_m, text_m))
    core_nc = move(grad_i[3 * rows :].astype(BF), "core")
    pair_n = move((grad_i[2 * rows : 3 * rows] + core_nc.astype(F32)).astype(BF), "pair")
    core_c = move(grad_i[rows : 2 * rows].astype(BF), "core")
    grad_images = grad_i[:rows] + core_c.astype(F32) + pair_n.astype(F32)
    back_m = jnp.concatenate(back_m).astype(F32)
    grad_texts = grad_t + jnp.where(upper, 0.0, back_m) + jnp.concatenate(back_x).astype(F32)
    return grad_images, grad_texts


def solution(mesh):
    rows, flat = P(AXES, None), P(AXES)
    return jax.shard_map(
        local,
        mesh=mesh,
        in_specs=(rows, rows, flat, P(), P()),
        out_specs=(rows, rows),
        check_vma=False,
    )
```

time: 659 us -> 101 us (0.15)
  waiting for transfers between devices: 616 us -> 39.8 us
  starting transfers between devices: 4.56 us -> 25.7 us
  between operations: 15.5 us -> 2.16 us
    ppermute x5 -> x16, waiting for transfers between devices: 518 us -> 39.8 us  [local(): move = lambda v, name: lax.ppermute(v, AXES, way[name])]
    reduce_scatter x1 -> x0, waiting for transfers between devices: 53.8 us -> none  [local(): lax.psum_scatter(group_grad, 'inner', scatter_dimension=0, tiled=True)]
    all_gather x1 -> x0, waiting for transfers between devices: 43.6 us -> none  [local(): group_text = lax.all_gather(text_embeds, 'inner', axis=0, tiled=True)]
    ppermute x5 -> x16, starting transfers between devices: 4.49 us -> 25.7 us  [local(): move = lambda v, name: lax.ppermute(v, AXES, way[name])]
    dot_general x9 -> x15, matrix products: 18.3 us -> 21.5 us  [the longest x5 8.05 us: nn(): return jnp.dot(a, b, preferred_element_type=F32)]
  transfers between devices with their start and end apart: 7 -> 16, of which waited for: 5 -> 7; matrix products, arithmetic and copies ran while one was open for 2% -> 31% of each run, Pallas kernels for 0% -> 0%
where the time goes in v1:
time: 101 us
  waiting for transfers between devices  39.8 us (39%)
  starting transfers between devices  25.7 us (25%)
  matrix products  21.5 us (21%)
  local copies, waits for them, and re-layouts  6.28 us (6%)
  other arithmetic  5.43 us (5%)
  between operations  2.16 us (2%)
    ppermute x16, waiting for transfers between devices, local(): move = lambda v, name: lax.ppermute(v, AXES, way[name])  39.8 us
    ppermute x16, starting transfers between devices, local(): move = lambda v, name: lax.ppermute(v, AXES, way[name])  25.7 us
    dot_general x5, matrix products, nn(): return jnp.dot(a, b, preferred_element_type=F32)  8.05 us
    dot_general x5, matrix products, tn(): lax.dot_general(a, b, (((0,), (0,)), ((), ())), preferred_element_type=F32)  7.86 us
    dot_general x5, matrix products, nt(): lax.dot_general(a, b, (((1,), (1,)), ((), ())), preferred_element_type=F32)  5.59 us
    unnamed x15, local copies, waits for them, and re-layouts  3.63 us
    select_n x2, other arithmetic, local(): jnp.where(upper, t, text[p])  3.19 us
  transfers between devices with their start and end apart: 16, of which 7 were waited for; matrix products, arithmetic and copies ran while one was open for 31% of the time, Pallas kernels for 0%

profile of v1, /device:TPU:1, one launch (start us, length us, event | category | flops | bytes accessed | tf_op | source)
XLA Modules:
  0.0 100.8 jit_solution(6698482641431450278)
XLA Ops:
  1.7 2.1 %collective-permute-start.5 = (bf16[160,1152]{1,0:T(8,128)(2,1)S(1)}, bf16[160,1152]{1,0:T(8,128)(2,1)S(1)}, u32[]{:S(2)}, u32[]{:S(2)}) collective-permute-start(bf16[160,1152]{1,0:T(8,128)(2,1)S(1)} %slice.22), channel_id=1, source_target_pairs={{0,8},{1,9},{2,10},{3,11},{4,12},{5,13},{6,14},{7,15},{8,16},{9,17... | collective-permute-start | bytes 1105928 | tf_op jit(solution)/shard_map/ppermute | solution.py:46
  3.8 1.3 %collective-permute-start.3 = (s32[320]{0:T(512)}, s32[320]{0:T(512)S(1)}, u32[]{:S(2)}, u32[]{:S(2)}) collective-permute-start(s32[320]{0:T(512)} %param.7), channel_id=1, source_target_pairs={{0,1},{1,0},{2,3},{3,2},{4,5},{5,4},{6,7},{7,6},{8,9},{9,8},{10,11... | collective-permute-start | bytes 3848 | tf_op jit(solution)/shard_map/ppermute | solution.py:46
  7.8 10.8 %collective-permute-done.5 = bf16[160,1152]{1,0:T(8,128)(2,1)S(1)} collective-permute-done((bf16[160,1152]{1,0:T(8,128)(2,1)S(1)}, bf16[160,1152]{1,0:T(8,128)(2,1)S(1)}, u32[]{:S(2)}, u32[]{:S(2)}) %collective-permute-start.5) | collective-permute-done | bytes 368672 | tf_op jit(solution)/shard_map/ppermute | solution.py:46
  18.7 2.2 %broadcast_select_fusion.1 = (bf16[160,1152]{1,0:T(8,128)(2,1)}, bf16[160,1152]{1,0:T(8,128)(2,1)}) fusion(bf16[160,1152]{1,0:T(8,128)(2,1)S(1)} %collective-permute-done.5, pred[]{:T(512)S(6)} %eq.21, bf16[320,1152]{1,0:T(8,128)(2,1)} %param.6), kind=kLoop, calls=%fused_computation.60 | loop fusion | flops 184320 | bytes 1843201 | tf_op jit(solution)/shard_map/jit(_where)/select_n | solution.py:59
  20.8 1.2 %constant_dynamic-update-slice_fusion.3 = bf16[1280,1152]{1,0:T(8,128)(2,1)S(1)} fusion(bf16[320,1152]{1,0:T(8,128)(2,1)} %param.5), kind=kLoop, calls=%fused_computation.64 | loop fusion | bytes 1474560
  23.4 2.8 %collective-permute-start.7 = (bf16[160,1152]{1,0:T(8,128)(2,1)}, bf16[160,1152]{1,0:T(8,128)(2,1)S(1)}, u32[]{:S(2)}, u32[]{:S(2)}) collective-permute-start(bf16[160,1152]{1,0:T(8,128)(2,1)} %get-tuple-element.4), channel_id=1, source_target_pairs={{0,6},{1,7},{2,4},{3,5},{4,2},{5,3},{6,0},{7,1},{8,14},{9,15},{10,... | collective-permute-start | bytes 1105928 | tf_op jit(solution)/shard_map/ppermute | solution.py:46
  26.2 1.5 %collective-permute-start.2 = (bf16[320,1152]{1,0:T(8,128)(2,1)}, bf16[320,1152]{1,0:T(8,128)(2,1)S(1)}, u32[]{:S(2)}, u32[]{:S(2)}) collective-permute-start(bf16[320,1152]{1,0:T(8,128)(2,1)} %collective-permute-done.1), channel_id=1, source_target_pairs={{0,1},{1,0},{2,3},{3,2},{4,5},{5,4},{6,7},{7,6},{8,9},{9,8},{10,11... | collective-permute-start | bytes 2211848 | tf_op jit(solution)/shard_map/ppermute | solution.py:46
  27.7 5.5 %collective-permute-done.6 = bf16[160,1152]{1,0:T(8,128)(2,1)S(1)} collective-permute-done((bf16[160,1152]{1,0:T(8,128)(2,1)}, bf16[160,1152]{1,0:T(8,128)(2,1)S(1)}, u32[]{:S(2)}, u32[]{:S(2)}) %collective-permute-start.6) | collective-permute-done | bytes 368672 | tf_op jit(solution)/shard_map/ppermute | solution.py:46
  34.2 2.8 %collective-permute-start.8 = (bf16[160,1152]{1,0:T(8,128)(2,1)S(1)}, bf16[160,1152]{1,0:T(8,128)(2,1)S(1)}, u32[]{:S(2)}, u32[]{:S(2)}) collective-permute-start(bf16[160,1152]{1,0:T(8,128)(2,1)S(1)} %broadcast_select_fusion), channel_id=1, source_target_pairs={{0,6},{1,7},{2,4},{3,5},{4,2},{5,3},{6,0},{7,1},{8,14},{9,15},{10,... | collective-permute-start | bytes 1105928 | tf_op jit(solution)/shard_map/ppermute | solution.py:46
  37.1 1.2 %constant_dynamic-update-slice_fusion.2 = bf16[1280,1152]{1,0:T(8,128)(2,1)S(1)} fusion(bf16[1280,1152]{1,0:T(8,128)(2,1)S(1)} %constant_dynamic-update-slice_fusion.3, bf16[320,1152]{1,0:T(8,128)(2,1)} %collective-permute-done), kind=kLoop, calls=%fused_computation.63 | loop fusion | bytes 1474560
  38.3 1.2 %constant_dynamic-update-slice_fusion.1 = bf16[1280,1152]{1,0:T(8,128)(2,1)S(1)} fusion(bf16[1280,1152]{1,0:T(8,128)(2,1)S(1)} %constant_dynamic-update-slice_fusion.2, bf16[320,1152]{1,0:T(8,128)(2,1)} %collective-permute-done.1), kind=kLoop, calls=%fused_computation.62 | loop fusion | bytes 1474560
  39.6 4.0 %collective-permute-done.8 = bf16[160,1152]{1,0:T(8,128)(2,1)S(1)} collective-permute-done((bf16[160,1152]{1,0:T(8,128)(2,1)S(1)}, bf16[160,1152]{1,0:T(8,128)(2,1)S(1)}, u32[]{:S(2)}, u32[]{:S(2)}) %collective-permute-start.8) | collective-permute-done | bytes 368672 | tf_op jit(solution)/shard_map/ppermute | solution.py:46
  43.6 1.1 %fusion.41 = bf16[160,1280]{1,0:T(8,128)(2,1)S(1)} fusion(bf16[160,1152]{1,0:T(8,128)(2,1)S(1)} %collective-permute-done.8, bf16[1280,1152]{1,0:T(8,128)(2,1)S(1)} %constant_dynamic-update-slice_fusion, f32[]{:T(128)} %bitcast.48, f32[]{:T(128)} %bitcast.42), kind=kOutput, calls=%fused_computation.51 | convolution fusion | flops 473292800 | bytes 3727368 | tf_op jit(solution)/shard_map/dot_general | solution.py:32
  44.7 1.5 %convolution_convert_fusion = bf16[160,1152]{1,0:T(8,128)(2,1)} fusion(bf16[160,1280]{1,0:T(8,128)(2,1)S(1)} %fusion.41, bf16[1280,1152]{1,0:T(8,128)(2,1)S(1)} %constant_dynamic-update-slice_fusion), kind=kOutput, calls=%fused_computation.52 | convolution fusion | flops 472043520 | bytes 3727360 | tf_op jit(solution)/shard_map/dot_general | solution.py:40
  46.1 2.6 %collective-permute-start.13 = (bf16[160,1152]{1,0:T(8,128)(2,1)}, bf16[160,1152]{1,0:T(8,128)(2,1)}, u32[]{:S(2)}, u32[]{:S(2)}) collective-permute-start(bf16[160,1152]{1,0:T(8,128)(2,1)} %convolution_convert_fusion), channel_id=1, source_target_pairs={{0,6},{1,7},{2,4},{3,5},{4,2},{5,3},{6,0},{7,1},{8,14},{9,15},{10,... | collective-permute-start | bytes 1105928 | tf_op jit(solution)/shard_map/ppermute | solution.py:46
  48.8 1.4 %fusion.11 = bf16[320,1280]{1,0:T(8,128)(2,1)S(1)} fusion(bf16[1280,1152]{1,0:T(8,128)(2,1)S(1)} %constant_dynamic-update-slice_fusion, bf16[320,1152]{1,0:T(8,128)(2,1)S(1)} %copy-done, s32[1280]{0:T(1024)S(1)} %broadcast_subtract_fusion, f32[]{:T(128)} %bitcast.45, f32[]{:T(128)} %bitcast.41), kind=kOutput, calls=%fused_computation.15 | convolution fusion | flops 947814400 | bytes 4510728 | tf_op jit(solution)/shard_map/dot_general | solution.py:32
  50.2 1.8 %fusion.46 = f32[1280,1152]{1,0:T(8,128)S(1)} fusion(bf16[320,1280]{1,0:T(8,128)(2,1)S(1)} %fusion.11, bf16[320,1152]{1,0:T(8,128)(2,1)S(1)} %copy-done), kind=kOutput, calls=%fused_computation.69 | convolution fusion | flops 943718400 | bytes 7454720 | tf_op jit(solution)/shard_map/dot_general | solution.py:36
  52.1 1.1 %fusion.48 = f32[1280,1152]{1,0:T(8,128)S(1)} fusion(bf16[160,1280]{1,0:T(8,128)(2,1)S(1)} %fusion.41, bf16[160,1152]{1,0:T(8,128)(2,1)S(1)} %collective-permute-done.8), kind=kOutput, calls=%fused_computation.71 | convolution fusion | flops 471859200 | bytes 6676480 | tf_op jit(solution)/shard_map/dot_general | solution.py:36
  54.2 1.0 %fusion.38 = bf16[1280,160]{0,1:T(8,128)(2,1)S(1)} fusion(bf16[1280,1152]{1,0:T(8,128)(2,1)S(1)} %constant_dynamic-update-slice_fusion, bf16[160,1152]{1,0:T(8,128)(2,1)S(1)} %copy-done.2, f32[]{:T(128)} %bitcast.40, f32[]{:T(128)} %bitcast.46), kind=kOutput, calls=%fused_computation.48 | convolution fusion | flops 473292800 | bytes 3727368 | tf_op jit(solution)/shard_map/dot_general | solution.py:32
  55.2 1.1 %fusion.47 = f32[1280,1152]{1,0:T(8,128)S(1)} fusion(bf16[1280,160]{0,1:T(8,128)(2,1)S(1)} %fusion.39, bf16[160,1152]{1,0:T(8,128)(2,1)S(1)} %collective-permute-done.6), kind=kOutput, calls=%fused_computation.70 | convolution fusion | flops 471859200 | bytes 6676480 | tf_op jit(solution)/shard_map/dot_general | solution.py:36
  57.4 1.1 %convolution_add_fusion = f32[1280,1152]{1,0:T(8,128)S(1)} fusion(f32[1280,1152]{1,0:T(8,128)S(1)} %fusion.48, bf16[160,1280]{1,0:T(8,128)(2,1)S(1)} %fusion.40, bf16[160,1152]{1,0:T(8,128)(2,1)S(1)} %collective-permute-done.7), kind=kOutput, calls=%fused_computation | convolution fusion | flops 473333760 | bytes 12574720 | tf_op jit(solution)/shard_map/dot_general | solution.py:36
  58.5 2.8 %fusion.45 = (bf16[1280,1152]{1,0:T(8,128)(2,1)}, f32[1280,1152]{1,0:T(8,128)S(1)}) fusion(f32[1280,1152]{1,0:T(8,128)S(1)} %convolution_add_fusion, f32[1280,1152]{1,0:T(8,128)S(1)} %fusion.46, f32[1280,1152]{1,0:T(8,128)S(1)} %fusion.47, bf16[1280,160]{0,1:T(8,128)(2,1)S(1)} %fusion.38, bf16[160,1152]{1,0:T(8,128)(2,1)S(1)} %copy-done.2), kind=kOutput, calls=%fused_computation.68 | convolution fusion | flops 477757440 | bytes 27320320 | tf_op jit(solution)/shard_map/dot_general | solution.py:36
  61.3 1.5 %fusion.44 = (bf16[320,1152]{1,0:T(8,128)(2,1)S(1)}, bf16[320,1152]{1,0:T(8,128)(2,1)S(1)}) fusion(bf16[1280,1152]{1,0:T(8,128)(2,1)} %get-tuple-element.6), kind=kLoop, calls=%fused_computation.67 | loop fusion | bytes 2949120 | tf_op jit(solution)/shard_map/slice | solution.py:83
  62.7 3.4 %collective-permute-start.10 = (bf16[320,1152]{1,0:T(8,128)(2,1)S(1)}, bf16[320,1152]{1,0:T(8,128)(2,1)S(1)}, u32[]{:S(2)}, u32[]{:S(2)}) collective-permute-start(bf16[320,1152]{1,0:T(8,128)(2,1)S(1)} %get-tuple-element.3), channel_id=1, source_target_pairs={{0,1},{1,0},{2,3},{3,2},{4,5},{5,4},{6,7},{7,6},{8,9},{9,8},{10,11... | collective-permute-start | bytes 2211848 | tf_op jit(solution)/shard_map/ppermute | solution.py:46
  67.3 1.7 %fusion.37 = bf16[160,1152]{1,0:T(8,128)(2,1)S(1)} fusion(bf16[1280,160]{0,1:T(8,128)(2,1)S(1)} %fusion.39, bf16[1280,1152]{1,0:T(8,128)(2,1)S(1)} %constant_dynamic-update-slice_fusion, bf16[160,1152]{1,0:T(8,128)(2,1)} %collective-permute-done.13, pred[]{:T(512)S(6)} %eq.21), kind=kOutput, calls=%fused_computation.47 | convolution fusion | flops 472596480 | bytes 4096001 | tf_op jit(solution)/shard_map/dot_general | solution.py:40
  69.0 3.5 %collective-permute-start.15 = (bf16[160,1152]{1,0:T(8,128)(2,1)S(1)}, bf16[160,1152]{1,0:T(8,128)(2,1)S(1)}, u32[]{:S(2)}, u32[]{:S(2)}) collective-permute-start(bf16[160,1152]{1,0:T(8,128)(2,1)S(1)} %fusion.37), channel_id=1, source_target_pairs={{0,248},{1,249},{2,250},{3,251},{4,252},{5,253},{6,254},{7,255},{8... | collective-permute-start | bytes 1105928 | tf_op jit(solution)/shard_map/ppermute | solution.py:46
  72.5 5.9 %collective-permute-done.12 = bf16[160,1152]{1,0:T(8,128)(2,1)S(1)} collective-permute-done((bf16[160,1152]{1,0:T(8,128)(2,1)S(1)}, bf16[160,1152]{1,0:T(8,128)(2,1)S(1)}, u32[]{:S(2)}, u32[]{:S(2)}) %collective-permute-start.12) | collective-permute-done | bytes 368672 | tf_op jit(solution)/shard_map/ppermute | solution.py:46
  79.1 3.2 %collective-permute-start.14 = (bf16[160,1152]{1,0:T(8,128)(2,1)S(1)}, bf16[160,1152]{1,0:T(8,128)(2,1)S(1)}, u32[]{:S(2)}, u32[]{:S(2)}) collective-permute-start(bf16[160,1152]{1,0:T(8,128)(2,1)S(1)} %fusion.36), channel_id=1, source_target_pairs={{0,248},{1,249},{2,250},{3,251},{4,252},{5,253},{6,254},{7,255},{8... | collective-permute-start | bytes 1105928 | tf_op jit(solution)/shard_map/ppermute | solution.py:46
  82.6 6.8 %collective-permute-done.14 = bf16[160,1152]{1,0:T(8,128)(2,1)S(1)} collective-permute-done((bf16[160,1152]{1,0:T(8,128)(2,1)S(1)}, bf16[160,1152]{1,0:T(8,128)(2,1)S(1)}, u32[]{:S(2)}, u32[]{:S(2)}) %collective-permute-start.14) | collective-permute-done | bytes 368672 | tf_op jit(solution)/shard_map/ppermute | solution.py:46
  89.5 3.4 %fusion.2 = f32[320,1152]{1,0:T(8,128)} fusion(bf16[320,1280]{1,0:T(8,128)(2,1)S(1)} %copy-done.4, bf16[1280,1152]{1,0:T(8,128)(2,1)S(1)} %constant_dynamic-update-slice_fusion, bf16[160,1152]{1,0:T(8,128)(2,1)} %collective-permute-done.13, bf16[160,1152]{1,0:T(8,128)(2,1)S(1)} %collective-permute-done.12, ...), kind=kOutput, calls=%fused_computation.6 | convolution fusion | flops 947773440 | bytes 6717441 | tf_op jit(solution)/shard_map/dot_general | solution.py:40
  92.9 6.6 %collective-permute-done.11 = bf16[320,1152]{1,0:T(8,128)(2,1)S(1)} collective-permute-done((bf16[320,1152]{1,0:T(8,128)(2,1)S(1)}, bf16[320,1152]{1,0:T(8,128)(2,1)S(1)}, u32[]{:S(2)}, u32[]{:S(2)}) %collective-permute-start.11) | collective-permute-done | bytes 737312 | tf_op jit(solution)/shard_map/ppermute | solution.py:46
  99.5 1.3 %fusion.43 = f32[320,1152]{1,0:T(8,128)} fusion(f32[1280,1152]{1,0:T(8,128)S(1)} %get-tuple-element.7, bf16[320,1152]{1,0:T(8,128)(2,1)S(1)} %collective-permute-done.11, bf16[320,1152]{1,0:T(8,128)(2,1)S(1)} %collective-permute-done.9), kind=kLoop, calls=%fused_computation.58 | loop fusion | flops 1474560 | bytes 4423680 | tf_op jit(solution)/shard_map/add | solution.py:84
  (40 shorter events, 9.2 us)
Async XLA Ops:
  0.6 22.7 %copy-start.5 = (s32[320]{0:T(512)S(1)}, s32[320]{0:T(512)}, u32[]{:S(2)}) copy-start(s32[320]{0:T(512)} %param.7) | copy-start | bytes 3844
  1.7 17.0 %collective-permute-start.5 = (bf16[160,1152]{1,0:T(8,128)(2,1)S(1)}, bf16[160,1152]{1,0:T(8,128)(2,1)S(1)}, u32[]{:S(2)}, u32[]{:S(2)}) collective-permute-start(bf16[160,1152]{1,0:T(8,128)(2,1)S(1)} %slice.22), channel_id=1, source_target_pairs={{0,8},{1,9},{2,10},{3,11},{4,12},{5,13},{6,14},{7,15},{8,16},{9,17... | collective-permute-start | bytes 1105928 | tf_op jit(solution)/shard_map/ppermute | solution.py:46
  3.8 2.3 %collective-permute-start.3 = (s32[320]{0:T(512)}, s32[320]{0:T(512)S(1)}, u32[]{:S(2)}, u32[]{:S(2)}) collective-permute-start(s32[320]{0:T(512)} %param.7), channel_id=1, source_target_pairs={{0,1},{1,0},{2,3},{3,2},{4,5},{5,4},{6,7},{7,6},{8,9},{9,8},{10,11... | collective-permute-start | bytes 3848 | tf_op jit(solution)/shard_map/ppermute | solution.py:46
  5.1 32.0 %collective-permute-start = (bf16[320,1152]{1,0:T(8,128)(2,1)}, bf16[320,1152]{1,0:T(8,128)(2,1)}, u32[]{:S(2)}, u32[]{:S(2)}) collective-permute-start(bf16[320,1152]{1,0:T(8,128)(2,1)} %param.5), channel_id=1, source_target_pairs={{0,1},{1,0},{2,3},{3,2},{4,5},{5,4},{6,7},{7,6},{8,9},{9,8},{10,11... | collective-permute-start | bytes 2211848 | tf_op jit(solution)/shard_map/ppermute | solution.py:46
  5.2 21.0 %collective-permute-start.1 = (bf16[320,1152]{1,0:T(8,128)(2,1)}, bf16[320,1152]{1,0:T(8,128)(2,1)}, u32[]{:S(2)}, u32[]{:S(2)}) collective-permute-start(bf16[320,1152]{1,0:T(8,128)(2,1)} %param.5), channel_id=1, source_target_pairs={{0,2},{1,3},{2,0},{3,1},{4,6},{5,7},{6,4},{7,5},{8,10},{9,11},{10,... | collective-permute-start | bytes 2211848 | tf_op jit(solution)/shard_map/ppermute | solution.py:46
  6.9 16.4 %collective-permute-start.4 = (s32[640]{0:T(1024)S(1)}, s32[640]{0:T(1024)S(1)}, u32[]{:S(2)}, u32[]{:S(2)}) collective-permute-start(s32[640]{0:T(1024)S(1)} %pad_add_fusion), channel_id=1, source_target_pairs={{0,2},{1,3},{2,0},{3,1},{4,6},{5,7},{6,4},{7,5},{8,10},{9,11},{10,... | collective-permute-start | bytes 7688 | tf_op jit(solution)/shard_map/ppermute | solution.py:46
  18.7 2.2 %copy-start.1 = (bf16[160,1152]{1,0:T(8,128)(2,1)}, bf16[160,1152]{1,0:T(8,128)(2,1)S(1)}, u32[]{:S(2)}) copy-start(bf16[160,1152]{1,0:T(8,128)(2,1)S(1)} %collective-permute-done.5) | copy-start | bytes 1105924
  20.8 12.4 %collective-permute-start.6 = (bf16[160,1152]{1,0:T(8,128)(2,1)}, bf16[160,1152]{1,0:T(8,128)(2,1)S(1)}, u32[]{:S(2)}, u32[]{:S(2)}) collective-permute-start(bf16[160,1152]{1,0:T(8,128)(2,1)} %get-tuple-element.5), channel_id=1, source_target_pairs={{0,8},{1,9},{2,10},{3,11},{4,12},{5,13},{6,14},{7,15},{8,16},{9,17... | collective-permute-start | bytes 1105928 | tf_op jit(solution)/shard_map/ppermute | solution.py:46
  23.4 32.9 %collective-permute-start.7 = (bf16[160,1152]{1,0:T(8,128)(2,1)}, bf16[160,1152]{1,0:T(8,128)(2,1)S(1)}, u32[]{:S(2)}, u32[]{:S(2)}) collective-permute-start(bf16[160,1152]{1,0:T(8,128)(2,1)} %get-tuple-element.4), channel_id=1, source_target_pairs={{0,6},{1,7},{2,4},{3,5},{4,2},{5,3},{6,0},{7,1},{8,14},{9,15},{10,... | collective-permute-start | bytes 1105928 | tf_op jit(solution)/shard_map/ppermute | solution.py:46
  26.2 13.3 %collective-permute-start.2 = (bf16[320,1152]{1,0:T(8,128)(2,1)}, bf16[320,1152]{1,0:T(8,128)(2,1)S(1)}, u32[]{:S(2)}, u32[]{:S(2)}) collective-permute-start(bf16[320,1152]{1,0:T(8,128)(2,1)} %collective-permute-done.1), channel_id=1, source_target_pairs={{0,1},{1,0},{2,3},{3,2},{4,5},{5,4},{6,7},{7,6},{8,9},{9,8},{10,11... | collective-permute-start | bytes 2211848 | tf_op jit(solution)/shard_map/ppermute | solution.py:46
  34.2 9.4 %collective-permute-start.8 = (bf16[160,1152]{1,0:T(8,128)(2,1)S(1)}, bf16[160,1152]{1,0:T(8,128)(2,1)S(1)}, u32[]{:S(2)}, u32[]{:S(2)}) collective-permute-start(bf16[160,1152]{1,0:T(8,128)(2,1)S(1)} %broadcast_select_fusion), channel_id=1, source_target_pairs={{0,6},{1,7},{2,4},{3,5},{4,2},{5,3},{6,0},{7,1},{8,14},{9,15},{10,... | collective-permute-start | bytes 1105928 | tf_op jit(solution)/shard_map/ppermute | solution.py:46
  44.7 4.1 %copy-start = (bf16[320,1152]{1,0:T(8,128)(2,1)S(1)}, bf16[320,1152]{1,0:T(8,128)(2,1)}, u32[]{:S(2)}) copy-start(bf16[320,1152]{1,0:T(8,128)(2,1)} %param.6) | copy-start | bytes 2211844
  46.1 21.1 %collective-permute-start.13 = (bf16[160,1152]{1,0:T(8,128)(2,1)}, bf16[160,1152]{1,0:T(8,128)(2,1)}, u32[]{:S(2)}, u32[]{:S(2)}) collective-permute-start(bf16[160,1152]{1,0:T(8,128)(2,1)} %convolution_convert_fusion), channel_id=1, source_target_pairs={{0,6},{1,7},{2,4},{3,5},{4,2},{5,3},{6,0},{7,1},{8,14},{9,15},{10,... | collective-permute-start | bytes 1105928 | tf_op jit(solution)/shard_map/ppermute | solution.py:46
  50.2 1.9 %copy-start.3 = (bf16[320,1280]{1,0:T(8,128)(2,1)}, bf16[320,1280]{1,0:T(8,128)(2,1)S(1)}, u32[]{:S(2)}) copy-start(bf16[320,1280]{1,0:T(8,128)(2,1)S(1)} %fusion.11) | copy-start | bytes 2457604
  53.1 1.1 %copy-start.2 = (bf16[160,1152]{1,0:T(8,128)(2,1)S(1)}, bf16[160,1152]{1,0:T(8,128)(2,1)}, u32[]{:S(2)}) copy-start(bf16[160,1152]{1,0:T(8,128)(2,1)} %copy-done.1) | copy-start | bytes 1105924
  62.7 19.6 %collective-permute-start.10 = (bf16[320,1152]{1,0:T(8,128)(2,1)S(1)}, bf16[320,1152]{1,0:T(8,128)(2,1)S(1)}, u32[]{:S(2)}, u32[]{:S(2)}) collective-permute-start(bf16[320,1152]{1,0:T(8,128)(2,1)S(1)} %get-tuple-element.3), channel_id=1, source_target_pairs={{0,1},{1,0},{2,3},{3,2},{4,5},{5,4},{6,7},{7,6},{8,9},{9,8},{10,11... | collective-permute-start | bytes 2211848 | tf_op jit(solution)/shard_map/ppermute | solution.py:46
  66.9 11.5 %collective-permute-start.12 = (bf16[160,1152]{1,0:T(8,128)(2,1)S(1)}, bf16[160,1152]{1,0:T(8,128)(2,1)S(1)}, u32[]{:S(2)}, u32[]{:S(2)}) collective-permute-start(bf16[160,1152]{1,0:T(8,128)(2,1)S(1)} %convolution_convert_fusion.1), channel_id=1, source_target_pairs={{0,6},{1,7},{2,4},{3,5},{4,2},{5,3},{6,0},{7,1},{8,14},{9,15},{10,... | collective-permute-start | bytes 1105928 | tf_op jit(solution)/shard_map/ppermute | solution.py:46
  67.0 25.9 %collective-permute-start.9 = (bf16[320,1152]{1,0:T(8,128)(2,1)S(1)}, bf16[320,1152]{1,0:T(8,128)(2,1)S(1)}, u32[]{:S(2)}, u32[]{:S(2)}) collective-permute-start(bf16[320,1152]{1,0:T(8,128)(2,1)S(1)} %get-tuple-element.2), channel_id=1, source_target_pairs={{0,1},{1,0},{2,3},{3,2},{4,5},{5,4},{6,7},{7,6},{8,9},{9,8},{10,11... | collective-permute-start | bytes 2211848 | tf_op jit(solution)/shard_map/ppermute | solution.py:46
  69.0 20.5 %copy-start.4 = (bf16[320,1280]{1,0:T(8,128)(2,1)S(1)}, bf16[320,1280]{1,0:T(8,128)(2,1)}, u32[]{:S(2)}) copy-start(bf16[320,1280]{1,0:T(8,128)(2,1)} %copy-done.3) | copy-start | bytes 2457604
  69.0 13.6 %collective-permute-start.15 = (bf16[160,1152]{1,0:T(8,128)(2,1)S(1)}, bf16[160,1152]{1,0:T(8,128)(2,1)S(1)}, u32[]{:S(2)}, u32[]{:S(2)}) collective-permute-start(bf16[160,1152]{1,0:T(8,128)(2,1)S(1)} %fusion.37), channel_id=1, source_target_pairs={{0,248},{1,249},{2,250},{3,251},{4,252},{5,253},{6,254},{7,255},{8... | collective-permute-start | bytes 1105928 | tf_op jit(solution)/shard_map/ppermute | solution.py:46
  79.1 10.4 %collective-permute-start.14 = (bf16[160,1152]{1,0:T(8,128)(2,1)S(1)}, bf16[160,1152]{1,0:T(8,128)(2,1)S(1)}, u32[]{:S(2)}, u32[]{:S(2)}) collective-permute-start(bf16[160,1152]{1,0:T(8,128)(2,1)S(1)} %fusion.36), channel_id=1, source_target_pairs={{0,248},{1,249},{2,250},{3,251},{4,252},{5,253},{6,254},{7,255},{8... | collective-permute-start | bytes 1105928 | tf_op jit(solution)/shard_map/ppermute | solution.py:46
  82.5 17.0 %collective-permute-start.11 = (bf16[320,1152]{1,0:T(8,128)(2,1)S(1)}, bf16[320,1152]{1,0:T(8,128)(2,1)S(1)}, u32[]{:S(2)}, u32[]{:S(2)}) collective-permute-start(bf16[320,1152]{1,0:T(8,128)(2,1)S(1)} %fusion.42), channel_id=1, source_target_pairs={{0,2},{1,3},{2,0},{3,1},{4,6},{5,7},{6,4},{7,5},{8,10},{9,11},{10,... | collective-permute-start | bytes 2211848 | tf_op jit(solution)/shard_map/ppermute | solution.py:46

commit v2 on v1

v2 whole, which is shorter than its diff:
```python
import jax
import jax.numpy as jnp
from jax import lax
from jax.experimental import pallas as pl
from jax.experimental.pallas import tpu as pltpu
from jax.sharding import PartitionSpec as P

AXES = ("blk", "inner")
BF = jnp.bfloat16
F32 = jnp.float32
CUTS = 3
LATE = 1
PAD = 16
PICK_US = 6
SEND_US = 8
GATE_US = 8
VMEM = pl.BlockSpec(memory_space=pltpu.VMEM)
SMEM = pl.BlockSpec(memory_space=pltpu.SMEM)
ANY = pl.BlockSpec(memory_space=pl.ANY)
HBM = pl.BlockSpec(memory_space=pltpu.HBM)


def routes(nblk, ninner):
    def route(place):
        out = []
        for blk in range(nblk):
            for inner in range(ninner):
                c, h, l, k = place(blk // 2, blk % 2, inner // 2, inner % 2)
                out.append((blk * ninner + inner, ((c % (nblk // 2)) * 2 + h) * ninner + l * 2 + k))
        return out

    return {
        "core": route(lambda c, h, l, k: (c, h, l, 1 - k)),
        "pair": route(lambda c, h, l, k: (c, h, 1 - l, k)),
        "mirror": route(lambda c, h, l, k: (c, 1 - h, 1 - l, k)),
        "next": route(lambda c, h, l, k: (c + 1, h, l, k)),
        "prev": route(lambda c, h, l, k: (c - 1, h, l, k)),
    }


def pieces(n, cuts):
    size = -(-n // (cuts * 16)) * 16
    return [slice(a, min(a + size, n)) for a in range(0, n, size)]


def nt(a, b):
    return lax.dot_general(a, b, (((1,), (1,)), ((), ())), preferred_element_type=F32)


def tn(a, b):
    return lax.dot_general(a, b, (((0,), (0,)), ((), ())), preferred_element_type=F32)


def nn(a, b):
    return jnp.dot(a, b, preferred_element_type=F32)


def call(body, name, outs, ins, scalars=(), aliases=None, after=(), us=0):
    shapes = tuple(jax.ShapeDtypeStruct(s, d) for s, d in outs)
    ns, ni, na = len(scalars), len(ins), len(after)

    def run(*refs):
        body(*refs[: ns + ni], *refs[ns + ni + na :])

    return pl.pallas_call(
        run,
        out_shape=shapes,
        in_specs=[SMEM] * ns + [VMEM] * ni + [ANY] * na,
        out_specs=tuple(VMEM for _ in shapes),
        input_output_aliases={k + ns: v for k, v in (aliases or {}).items()},
        compiler_params=pltpu.CompilerParams(vmem_limit_bytes=16 * 2**20),
        cost_estimate=pl.CostEstimate(flops=int(us * 1e9), bytes_accessed=0, transcendentals=0),
        name=name,
    )(*scalars, *ins, *after)


def gate(value, name, after, us=0):
    spec = [(value.shape, value.dtype)]
    return call(lambda a, b: None, name, spec, [value], aliases={0: 0}, after=after, us=us)[0]


def is_upper():
    return lax.rem(lax.axis_index("blk"), 2) == 1


def k_pack(image, pos, out):
    n, d = image.shape
    out[:n, :] = image[...]
    row = lax.broadcasted_iota(jnp.int32, (PAD, n), 0)
    p = jnp.broadcast_to(pos[...].reshape(1, n), (PAD, n))
    code = jnp.where(row == 0, p // 8, jnp.where(row == 1, p % 8, 0))
    out[n:, :] = jnp.zeros((PAD, d), BF)
    out[n:, :n] = code.astype(F32).astype(BF)


def pos_of(block):
    n = block.shape[0] - PAD
    code = block[n:, :n].astype(F32)
    return (code[0:1, :] * 8 + code[1:2, :]).astype(jnp.int32)


def tile_of(scale, bias, texts, images, pos=None):
    s = jax.nn.sigmoid(scale[0] * nt(texts, images) + bias[0])
    if pos is not None:
        first = lax.axis_index("inner") * texts.shape[0]
        at = lax.broadcasted_iota(jnp.int32, s.shape, 0) + first
        s = s - (at == pos).astype(F32)
    return (scale[0] * s).astype(BF)


def local(image, text, positive, logit_scale, logit_bias):
    nblk, ninner = lax.axis_size("blk"), lax.axis_size("inner")
    way = routes(nblk, ninner)
    move = lambda v, name: lax.ppermute(v, AXES, way[name])
    sc = (logit_scale, logit_bias)
    n, d = text.shape
    m = ninner * n
    parts = pieces(n, CUTS)
    size = [p.stop - p.start for p in parts]
    cuts = len(parts)
    early = cuts - LATE
    base = 2 * n
    done = base + parts[early].start
    blocks = [slice(j * n, (j + 1) * n) for j in range(ninner)]

    cut = []
    for p, s in zip(parts, size):

        def k_cut(text, out, p=p):
            out[...] = text[p, :]

        cut += call(k_cut, f"cut_{p.start}", [((s, d), BF)], [text], after=cut[-1:])
    (packed,) = call(k_pack, "pack", [((n + PAD, d), BF)], [image, positive], after=cut[:1])
    text_x = [move(t, "next") for t in cut]
    image_n = move(packed, "pair")
    image_c = move(packed, "core")

    text_m = []
    picked = []
    for i, (p, s, c, x) in enumerate(zip(parts, size, cut, text_x)):

        def k_pick(own, x, out):
            out[...] = jnp.where(is_upper(), x[...], own[...])

        after = picked[-1:] + (text_m[:1] if i == 2 else []) + ([image_c] if i == 0 else [])
        (t,) = call(k_pick, f"pick_{p.start}", [((s, d), BF)], [c, x], after=after, us=PICK_US)
        picked.append(t)
        text_m.append(move(t, "mirror"))
    text_m = [gate(t, f"gate_m_{i}", picked[-1:], us=GATE_US) for i, t in enumerate(text_m[:early])] + text_m[early:]
    image_n = gate(image_n, "gate_pair", picked[-1:])
    image_nc = move(image_n, "core")

    def k_tiles(scale, bias, i0, i_n, i_c, i_nc, *refs):
        own, xs, ms = refs[:cuts], refs[cuts : 2 * cuts], refs[2 * cuts : 2 * cuts + early]
        images, texts, tiles, pos = refs[2 * cuts + early :]
        for rows, ref in zip(blocks, (i_nc, i_n, i_c, i0)):
            images[rows, :] = ref[:n, :]
            pos[0:1, rows] = pos_of(ref)
        for k, group in enumerate((own, xs, ms)):
            for p, ref in zip(parts, group):
                texts[k * n + p.start : k * n + p.stop, :] = ref[...]
        tiles[:n, :] = tile_of(scale, bias, texts[:n, :], images[...], pos[0:1, :])
        tiles[n:base, :] = tile_of(scale, bias, texts[n:base, :], images[...])
        tiles[base:done, :] = tile_of(scale, bias, texts[base:done, :], images[...])

    images, texts, tiles, _ = call(
        k_tiles, "tiles", [((m, d), BF), ((3 * n, d), BF), ((3 * n, m), BF), ((8, m), jnp.int32)],
        [packed, image_n, image_c, image_nc, *cut, *text_x, *text_m[:early]], sc, us=2,
    )

    def k_last(scale, bias, images, *refs):
        got, (_, _, texts, tiles, to_nc, gi_n) = refs[:LATE], refs[LATE:]
        for p, t in zip(parts[early:], got):
            texts[base + p.start : base + p.stop, :] = t[...]
        tiles[done:, :] = tile_of(scale, bias, texts[done:, :], images[...])
        g = tn(tiles[:, : 2 * n], texts[...])
        to_nc[...] = g[:n, :].astype(BF)
        gi_n[...] = g[n:, :]

    texts, tiles, to_nc, gi_n = call(
        k_last, "mirror_last", [((3 * n, d), BF), ((3 * n, m), BF), ((n, d), BF), ((n, d), F32)],
        [images, *text_m[early:], texts, tiles], sc, aliases={1 + LATE: 0, 2 + LATE: 1},
    )
    got_nc = move(to_nc, "core")

    def k_mirror_grad(tiles, images, *grads):
        g = nn(tiles[base:, :], images[...]).astype(BF)
        for p, ref in zip(parts, grads):
            ref[...] = g[p, :]

    grad_m = list(call(k_mirror_grad, "mirror_grad", [((s, d), BF) for s in size], [tiles, images]))
    for i in range(1, cuts):
        grad_m[i] = gate(grad_m[i], f"gate_g_{i}", [grad_m[i - 1]])
    back_m = [move(g, "mirror") for g in grad_m]

    def k_pair(gi, got_nc, out):
        out[...] = (gi[...] + got_nc[...].astype(F32)).astype(BF)

    (send_n,) = call(k_pair, "to_pair", [((n, d), BF)], [gi_n, got_nc])
    got_n = move(send_n, "pair")

    def k_images(tiles, texts, to_c, gi_own):
        g = tn(tiles[:, 2 * n :], texts[...])
        to_c[...] = g[:n, :].astype(BF)
        gi_own[...] = g[n:, :]

    to_c, gi_own = call(k_images, "image_grads", [((n, d), BF), ((n, d), F32)], [tiles, texts], after=[send_n])

    def k_own_images(gi, got_c, out):
        out[...] = gi[...] + got_c[...].astype(F32)

    got_c = move(to_c, "core")
    (gi_own,) = call(k_own_images, "own_images", [((n, d), F32)], [gi_own, got_c])

    def k_texts(tiles, images, gt):
        gt[...] = nn(tiles[:base, :], images[...])

    (gt,) = call(k_texts, "text_grads", [((2 * n, d), F32)], [tiles, images], after=[to_c])

    back_x = []
    sent = []
    for p, s, back in zip(parts, size, back_m):

        def k_send(gt, back, out, p=p):
            b = jnp.where(is_upper(), back[...].astype(F32), 0.0)
            out[...] = (gt[n + p.start : n + p.stop, :] + b).astype(BF)

        (t,) = call(k_send, f"to_prev_{p.start}", [((s, d), BF)], [gt, back], after=sent[-1:], us=SEND_US)
        sent.append(t)
        back_x.append(move(t, "prev"))

    def k_end_images(gi, got_n, out):
        out[...] = gi[...] + got_n[...].astype(F32)

    def k_end_texts(gt, *refs):
        ms, xs, out = refs[:cuts], refs[cuts : 2 * cuts], refs[-1]
        up = is_upper()
        for p, a, b in zip(parts, ms, xs):
            out[p, :] = gt[p, :] + jnp.where(up, 0.0, a[...].astype(F32)) + b[...].astype(F32)

    (grad_images,) = call(k_end_images, "end_images", [((n, d), F32)], [gi_own, got_n])
    (grad_texts,) = call(k_end_texts, "end_texts", [((n, d), F32)], [gt, *back_m, *back_x])
    return grad_images, grad_texts


def solution(mesh):
    rows, flat = P(AXES, None), P(AXES)
    return jax.shard_map(
        local,
        mesh=mesh,
        in_specs=(rows, rows, flat, P(), P()),
        out_specs=(rows, rows),
        check_vma=False,
    )
```

time: 101 us -> 76 us (0.75)
  matrix products: 21.5 us -> 0 us
  Pallas kernels: 0 us -> 14.9 us
  waiting for transfers between devices: 39.8 us -> 28.4 us
  other arithmetic: 5.43 us -> 0 us
  local copies, waits for them, and re-layouts: 6.28 us -> 2.97 us
  starting transfers between devices: 25.7 us -> 27.6 us
    dot_general x15 -> x0, matrix products: 21.5 us -> none  [the longest x5 8.05 us: nn(): return jnp.dot(a, b, preferred_element_type=F32)]
    pallas_call x0 -> x24, Pallas kernels: none -> 14.9 us  [call(): pl.pallas_call(run, out_shape=shapes, in_specs=[SMEM] * ns + [VMEM] * ni...]
    ppermute x16 -> x18, waiting for transfers between devices: 39.8 us -> 28.4 us  [local(): move = lambda v, name: lax.ppermute(v, AXES, way[name])]
    select_n x2 -> x0, other arithmetic: 3.19 us -> none  [local(): jnp.where(upper, t, text[p])]
    slice x2 -> x0, local copies, waits for them, and re-layouts: 2.47 us -> none  [the longest x1 1.45 us: local(): core_c = move(grad_i[rows:2 * rows].astype(BF), 'core')]
    ppermute x16 -> x18, starting transfers between devices: 25.7 us -> 27.6 us  [local(): move = lambda v, name: lax.ppermute(v, AXES, way[name])]
    add x1 -> x0, other arithmetic: 1.32 us -> none  [local(): grad_images = grad_i[:rows] + core_c.astype(F32) + pair_n.astype(F32)]
    unnamed x15 -> x8, local copies, waits for them, and re-layouts: 3.63 us -> 2.97 us
  transfers between devices with their start and end apart: 16 -> 18, of which waited for: 7 -> 7; matrix products, arithmetic and copies ran while one was open for 31% -> 0% of each run, Pallas kernels for 0% -> 14%
where the time goes in v2:
time: 76 us; the launch traced here: 75.9 us
  waiting for transfers between devices  28.4 us (37%)
  starting transfers between devices  27.6 us (36%)
  Pallas kernels  14.9 us (20%)
  local copies, waits for them, and re-layouts  2.97 us (4%)
  between operations  2.06 us (3%)
    ppermute x18, waiting for transfers between devices, local(): move = lambda v, name: lax.ppermute(v, AXES, way[name])  28.4 us
    ppermute x18, starting transfers between devices, local(): move = lambda v, name: lax.ppermute(v, AXES, way[name])  27.6 us
    pallas_call x24, Pallas kernels, call(): pl.pallas_call(run, out_shape=shapes, in_specs=[SMEM] * ns + [VMEM] * ni...  14.9 us
    unnamed x8, local copies, waits for them, and re-layouts  2.97 us
  transfers between devices with their start and end apart: 18, of which 7 were waited for; matrix products, arithmetic and copies ran while one was open for 0% of the time, Pallas kernels for 14%

profile of v2, /device:TPU:1, one launch (start us, length us, event | category | flops | bytes accessed | tf_op | source)
XLA Modules:
  0.0 75.9 jit_solution(11295845185883178714)
XLA Ops:
  0.6 1.1 %copy-done = bf16[320,1152]{1,0:T(8,128)(2,1)S(1)} copy-done((bf16[320,1152]{1,0:T(8,128)(2,1)S(1)}, bf16[320,1152]{1,0:T(8,128)(2,1)}, u32[]{:S(2)}) %copy-start) | copy-done | bytes 737304
  1.8 1.2 %copy-done.2 = bf16[320,1152]{1,0:T(8,128)(2,1)S(1)} copy-done((bf16[320,1152]{1,0:T(8,128)(2,1)S(1)}, bf16[320,1152]{1,0:T(8,128)(2,1)}, u32[]{:S(2)}) %copy-start.2) | copy-done | bytes 737304
  3.0 0.7 copy-done.3
  3.7 3.3 %collective-permute-start.4 = (bf16[336,1152]{1,0:T(8,128)(2,1)S(1)}, bf16[336,1152]{1,0:T(8,128)(2,1)S(1)}, u32[]{:S(2)}, u32[]{:S(2)}) collective-permute-start(bf16[336,1152]{1,0:T(8,128)(2,1)S(1)} %pack.1.refs_2_), channel_id=1, source_target_pairs={{0,1},{1,0},{2,3},{3,2},{4,5},{5,4},{6,7},{7,6},{8,9},{9,8},{10,11... | collective-permute-start | bytes 2322440 | tf_op jit(solution)/shard_map/ppermute | solution.py:114
  7.0 0.8 %collective-permute-start = (bf16[336,1152]{1,0:T(8,128)(2,1)S(1)}, bf16[336,1152]{1,0:T(8,128)(2,1)S(1)}, u32[]{:S(2)}, u32[]{:S(2)}) collective-permute-start(bf16[336,1152]{1,0:T(8,128)(2,1)S(1)} %pack.1.refs_2_), channel_id=1, source_target_pairs={{0,2},{1,3},{2,0},{3,1},{4,6},{5,7},{6,4},{7,5},{8,10},{9,11},{10,... | collective-permute-start | bytes 2322440 | tf_op jit(solution)/shard_map/ppermute | solution.py:114
  7.8 1.3 %collective-permute-start.2 = (bf16[112,1152]{1,0:T(8,128)(2,1)S(1)}, bf16[112,1152]{1,0:T(8,128)(2,1)S(1)}, u32[]{:S(2)}, u32[]{:S(2)}) collective-permute-start(bf16[112,1152]{1,0:T(8,128)(2,1)S(1)} %cut_112.1.refs_1_.refs_0_.refs_7_), channel_id=1, source_target_pairs={{0,8},{1,9},{2,10},{3,11},{4,12},{5,13},{6,14},{7,15},{8,16},{9,17... | collective-permute-start | bytes 774152 | tf_op jit(solution)/shard_map/ppermute | solution.py:114
  9.2 1.0 %collective-permute-start.1 = (bf16[96,1152]{1,0:T(8,128)(2,1)S(1)}, bf16[96,1152]{1,0:T(8,128)(2,1)S(1)}, u32[]{:S(2)}, u32[]{:S(2)}) collective-permute-start(bf16[96,1152]{1,0:T(8,128)(2,1)S(1)} %cut_224.1.refs_0_.refs_8_), channel_id=1, source_target_pairs={{0,8},{1,9},{2,10},{3,11},{4,12},{5,13},{6,14},{7,15},{8,16},{9,17... | collective-permute-start | bytes 663560 | tf_op jit(solution)/shard_map/ppermute | solution.py:114
  11.5 8.1 %collective-permute-done.3.refs_1_.refs_9_ = bf16[112,1152]{1,0:T(8,128)(2,1)S(1)} collective-permute-done((bf16[112,1152]{1,0:T(8,128)(2,1)S(1)}, bf16[112,1152]{1,0:T(8,128)(2,1)S(1)}, u32[]{:S(2)}, u32[]{:S(2)}) %collective-permute-start.3) | collective-permute-done | bytes 258080 | tf_op jit(solution)/shard_map/ppermute | solution.py:114
  19.6 2.8 %collective-permute-start.5 = (bf16[112,1152]{1,0:T(8,128)(2,1)S(1)}, bf16[112,1152]{1,0:T(8,128)(2,1)S(1)}, u32[]{:S(2)}, u32[]{:S(2)}) collective-permute-start(bf16[112,1152]{1,0:T(8,128)(2,1)S(1)} %pick_0.1.refs_2_), channel_id=1, source_target_pairs={{0,6},{1,7},{2,4},{3,5},{4,2},{5,3},{6,0},{7,1},{8,14},{9,15},{10,... | collective-permute-start | bytes 774152 | tf_op jit(solution)/shard_map/ppermute | solution.py:114
  22.4 2.7 %collective-permute-done.2.refs_1_.refs_10_ = bf16[112,1152]{1,0:T(8,128)(2,1)S(1)} collective-permute-done((bf16[112,1152]{1,0:T(8,128)(2,1)S(1)}, bf16[112,1152]{1,0:T(8,128)(2,1)S(1)}, u32[]{:S(2)}, u32[]{:S(2)}) %collective-permute-start.2) | collective-permute-done | bytes 258080 | tf_op jit(solution)/shard_map/ppermute | solution.py:114
  25.1 2.8 %collective-permute-start.7 = (bf16[112,1152]{1,0:T(8,128)(2,1)S(1)}, bf16[112,1152]{1,0:T(8,128)(2,1)S(1)}, u32[]{:S(2)}, u32[]{:S(2)}) collective-permute-start(bf16[112,1152]{1,0:T(8,128)(2,1)S(1)} %pick_112.1.refs_2_), channel_id=1, source_target_pairs={{0,6},{1,7},{2,4},{3,5},{4,2},{5,3},{6,0},{7,1},{8,14},{9,15},{10,... | collective-permute-start | bytes 774152 | tf_op jit(solution)/shard_map/ppermute | solution.py:114
  28.0 1.9 %collective-permute-done.1.refs_1_.refs_11_ = bf16[96,1152]{1,0:T(8,128)(2,1)S(1)} collective-permute-done((bf16[96,1152]{1,0:T(8,128)(2,1)S(1)}, bf16[96,1152]{1,0:T(8,128)(2,1)S(1)}, u32[]{:S(2)}, u32[]{:S(2)}) %collective-permute-start.1) | collective-permute-done | bytes 221216 | tf_op jit(solution)/shard_map/ppermute | solution.py:114
  29.9 2.8 %collective-permute-start.8 = (bf16[96,1152]{1,0:T(8,128)(2,1)S(1)}, bf16[96,1152]{1,0:T(8,128)(2,1)S(1)}, u32[]{:S(2)}, u32[]{:S(2)}) collective-permute-start(bf16[96,1152]{1,0:T(8,128)(2,1)S(1)} %pick_224.1.refs_1_), channel_id=1, source_target_pairs={{0,6},{1,7},{2,4},{3,5},{4,2},{5,3},{6,0},{7,1},{8,14},{9,15},{10,... | collective-permute-start | bytes 663560 | tf_op jit(solution)/shard_map/ppermute | solution.py:114
  32.7 0.9 %collective-permute-start.6 = (bf16[336,1152]{1,0:T(8,128)(2,1)S(1)}, bf16[336,1152]{1,0:T(8,128)(2,1)S(1)}, u32[]{:S(2)}, u32[]{:S(2)}) collective-permute-start(bf16[336,1152]{1,0:T(8,128)(2,1)S(1)} %gate_pair.1.refs_3_), channel_id=1, source_target_pairs={{0,1},{1,0},{2,3},{3,2},{4,5},{5,4},{6,7},{7,6},{8,9},{9,8},{10,11... | collective-permute-start | bytes 2322440 | tf_op jit(solution)/shard_map/ppermute | solution.py:114
  33.7 1.9 %collective-permute-done.6.refs_5_ = bf16[336,1152]{1,0:T(8,128)(2,1)S(1)} collective-permute-done((bf16[336,1152]{1,0:T(8,128)(2,1)S(1)}, bf16[336,1152]{1,0:T(8,128)(2,1)S(1)}, u32[]{:S(2)}, u32[]{:S(2)}) %collective-permute-start.6) | collective-permute-done | bytes 774176 | tf_op jit(solution)/shard_map/ppermute | solution.py:114
  35.6 3.3 %tiles.1 = (bf16[1280,1152]{1,0:T(8,128)(2,1)S(1)}, bf16[960,1152]{1,0:T(8,128)(2,1)S(1)}, bf16[960,1280]{1,0:T(8,128)(2,1)S(1)}, s32[8,1280]{1,0:T(8,128)}) custom-call(f32[1]{0:T(128)S(6)} %copy.21.refs_0_, f32[1]{0:T(128)S(6)} %copy.22.refs_1_, bf16[336,1152]{1,0:T(8,128)(2,1)S(1)} %pack.1.refs_2_, bf16[336,1152]{1,0:T(8,128)(2,1)S(1)} %gate_pair.1.refs_3_, ...), custom_call_target="tpu_custom_call" | custom-call | flops 2000000000 | tf_op jit(solution)/shard_map/tiles/pallas_call | solution.py:65
  38.8 2.8 %mirror_last.1 = (bf16[960,1152]{1,0:T(8,128)(2,1)S(1)}, bf16[960,1280]{1,0:T(8,128)(2,1)S(1)}, bf16[320,1152]{1,0:T(8,128)(2,1)S(1)}, f32[320,1152]{1,0:T(8,128)S(1)}) custom-call(f32[1]{0:T(128)S(6)} %copy.21.refs_0_, f32[1]{0:T(128)S(6)} %copy.22.refs_1_, ...), custom_call_target="tpu_custom_call", output_to_operand_aliasing={{0}: (4, {}), {1}: (5, {})} | custom-call | tf_op jit(solution)/shard_map/mirror_last/pallas_call | solution.py:65
  41.6 1.3 %collective-permute-start.9 = (bf16[320,1152]{1,0:T(8,128)(2,1)S(1)}, bf16[320,1152]{1,0:T(8,128)(2,1)S(1)}, u32[]{:S(2)}, u32[]{:S(2)}) collective-permute-start(bf16[320,1152]{1,0:T(8,128)(2,1)S(1)} %get-tuple-element.20), channel_id=1, source_target_pairs={{0,1},{1,0},{2,3},{3,2},{4,5},{5,4},{6,7},{7,6},{8,9},{9,8},{10,11... | collective-permute-start | bytes 2211848 | tf_op jit(solution)/shard_map/ppermute | solution.py:114
  42.9 1.2 %mirror_grad.1 = (bf16[112,1152]{1,0:T(8,128)(2,1)S(1)}, bf16[112,1152]{1,0:T(8,128)(2,1)S(1)}, bf16[96,1152]{1,0:T(8,128)(2,1)S(1)}) custom-call(bf16[960,1280]{1,0:T(8,128)(2,1)S(1)} %get-tuple-element.17.refs_0_, bf16[1280,1152]{1,0:T(8,128)(2,1)S(1)} %get-tuple-element.14.refs_2_.refs_1_), custom_call_target="tpu_custom_call" | custom-call | tf_op jit(solution)/shard_map/mirror_grad/pallas_call | solution.py:65
  44.2 2.8 %collective-permute-start.12 = (bf16[112,1152]{1,0:T(8,128)(2,1)S(1)}, bf16[112,1152]{1,0:T(8,128)(2,1)S(1)}, u32[]{:S(2)}, u32[]{:S(2)}) collective-permute-start(bf16[112,1152]{1,0:T(8,128)(2,1)S(1)} %get-tuple-element.23.refs_1_), channel_id=1, source_target_pairs={{0,6},{1,7},{2,4},{3,5},{4,2},{5,3},{6,0},{7,1},{8,14},{9,15},{10,... | collective-permute-start | bytes 774152 | tf_op jit(solution)/shard_map/ppermute | solution.py:114
  47.0 2.6 %collective-permute-start.14 = (bf16[96,1152]{1,0:T(8,128)(2,1)S(1)}, bf16[96,1152]{1,0:T(8,128)(2,1)S(1)}, u32[]{:S(2)}, u32[]{:S(2)}) collective-permute-start(bf16[96,1152]{1,0:T(8,128)(2,1)S(1)} %gate_g_2.1), channel_id=1, source_target_pairs={{0,6},{1,7},{2,4},{3,5},{4,2},{5,3},{6,0},{7,1},{8,14},{9,15},{10,... | collective-permute-start | bytes 663560 | tf_op jit(solution)/shard_map/ppermute | solution.py:114
  49.8 1.9 %image_grads.1 = (bf16[320,1152]{1,0:T(8,128)(2,1)S(1)}, f32[320,1152]{1,0:T(8,128)S(1)}) custom-call(bf16[960,1280]{1,0:T(8,128)(2,1)S(1)} %get-tuple-element.17.refs_0_, bf16[960,1152]{1,0:T(8,128)(2,1)S(1)} %get-tuple-element.18.refs_1_, bf16[320,1152]{1,0:T(8,128)(2,1)S(1)} %to_pair.1.refs_2_), custom_call_target="tpu_custom_call" | custom-call | tf_op jit(solution)/shard_map/image_grads/pallas_call | solution.py:65
  51.7 2.3 %text_grads.1.refs_0_ = f32[640,1152]{1,0:T(8,128)S(1)} custom-call(bf16[960,1280]{1,0:T(8,128)(2,1)S(1)} %get-tuple-element.17.refs_0_, bf16[1280,1152]{1,0:T(8,128)(2,1)S(1)} %get-tuple-element.14.refs_2_.refs_1_, bf16[320,1152]{1,0:T(8,128)(2,1)S(1)} %get-tuple-element.22.refs_2_), custom_call_target="tpu_custom_call" | custom-call | tf_op jit(solution)/shard_map/text_grads/pallas_call | solution.py:65
  54.0 0.9 %collective-permute-start.10 = (bf16[320,1152]{1,0:T(8,128)(2,1)S(1)}, bf16[320,1152]{1,0:T(8,128)(2,1)S(1)}, u32[]{:S(2)}, u32[]{:S(2)}) collective-permute-start(bf16[320,1152]{1,0:T(8,128)(2,1)S(1)} %get-tuple-element.22.refs_2_), channel_id=1, source_target_pairs={{0,1},{1,0},{2,3},{3,2},{4,5},{5,4},{6,7},{7,6},{8,9},{9,8},{10,11... | collective-permute-start | bytes 2211848 | tf_op jit(solution)/shard_map/ppermute | solution.py:114
  55.1 1.4 %collective-permute-start.15 = (bf16[112,1152]{1,0:T(8,128)(2,1)S(1)}, bf16[112,1152]{1,0:T(8,128)(2,1)S(1)}, u32[]{:S(2)}, u32[]{:S(2)}) collective-permute-start(bf16[112,1152]{1,0:T(8,128)(2,1)S(1)} %to_prev_0.1.refs_2_), channel_id=1, source_target_pairs={{0,248},{1,249},{2,250},{3,251},{4,252},{5,253},{6,254},{7,255},{8... | collective-permute-start | bytes 774152 | tf_op jit(solution)/shard_map/ppermute | solution.py:114
  56.4 2.4 %collective-permute-done.13.refs_1_.refs_2_ = bf16[112,1152]{1,0:T(8,128)(2,1)S(1)} collective-permute-done((bf16[112,1152]{1,0:T(8,128)(2,1)S(1)}, bf16[112,1152]{1,0:T(8,128)(2,1)S(1)}, u32[]{:S(2)}, u32[]{:S(2)}) %collective-permute-start.13) | collective-permute-done | bytes 258080 | tf_op jit(solution)/shard_map/ppermute | solution.py:114
  58.9 1.4 %collective-permute-start.16 = (bf16[112,1152]{1,0:T(8,128)(2,1)S(1)}, bf16[112,1152]{1,0:T(8,128)(2,1)S(1)}, u32[]{:S(2)}, u32[]{:S(2)}) collective-permute-start(bf16[112,1152]{1,0:T(8,128)(2,1)S(1)} %to_prev_112.1.refs_2_), channel_id=1, source_target_pairs={{0,248},{1,249},{2,250},{3,251},{4,252},{5,253},{6,254},{7,255},{8... | collective-permute-start | bytes 774152 | tf_op jit(solution)/shard_map/ppermute | solution.py:114
  60.3 3.3 %collective-permute-done.14.refs_1_.refs_3_ = bf16[96,1152]{1,0:T(8,128)(2,1)S(1)} collective-permute-done((bf16[96,1152]{1,0:T(8,128)(2,1)S(1)}, bf16[96,1152]{1,0:T(8,128)(2,1)S(1)}, u32[]{:S(2)}, u32[]{:S(2)}) %collective-permute-start.14) | collective-permute-done | bytes 221216 | tf_op jit(solution)/shard_map/ppermute | solution.py:114
  63.7 1.4 %collective-permute-start.17 = (bf16[96,1152]{1,0:T(8,128)(2,1)S(1)}, bf16[96,1152]{1,0:T(8,128)(2,1)S(1)}, u32[]{:S(2)}, u32[]{:S(2)}) collective-permute-start(bf16[96,1152]{1,0:T(8,128)(2,1)S(1)} %to_prev_224.1), channel_id=1, source_target_pairs={{0,248},{1,249},{2,250},{3,251},{4,252},{5,253},{6,254},{7,255},{8... | collective-permute-start | bytes 663560 | tf_op jit(solution)/shard_map/ppermute | solution.py:114
  65.0 8.1 %collective-permute-done.17.refs_6_ = bf16[96,1152]{1,0:T(8,128)(2,1)S(1)} collective-permute-done((bf16[96,1152]{1,0:T(8,128)(2,1)S(1)}, bf16[96,1152]{1,0:T(8,128)(2,1)S(1)}, u32[]{:S(2)}, u32[]{:S(2)}) %collective-permute-start.17) | collective-permute-done | bytes 221216 | tf_op jit(solution)/shard_map/ppermute | solution.py:114
  73.1 1.4 %end_texts.1 = f32[320,1152]{1,0:T(8,128)} custom-call(f32[640,1152]{1,0:T(8,128)S(1)} %text_grads.1.refs_0_, bf16[112,1152]{1,0:T(8,128)(2,1)S(1)} %collective-permute-done.12.refs_1_, bf16[112,1152]{1,0:T(8,128)(2,1)S(1)} %collective-permute-done.13.refs_1_.refs_2_, bf16[96,1152]{1,0:T(8,128)(2,1)S(1)} %collective-permute-done.14.refs_1_.refs_3_, ...), custom_call_target="tpu_custom_call" | custom-call | tf_op jit(solution)/shard_map/end_texts/pallas_call | solution.py:65
  74.6 1.2 %end_images.1 = f32[320,1152]{1,0:T(8,128)} custom-call(f32[320,1152]{1,0:T(8,128)S(1)} %own_images.1.refs_0_, bf16[320,1152]{1,0:T(8,128)(2,1)S(1)} %collective-permute-done.11.refs_1_), custom_call_target="tpu_custom_call" | custom-call | tf_op jit(solution)/shard_map/end_images/pallas_call | solution.py:65
  (36 shorter events, 0.9 us)
Async XLA Ops:
  0.6 1.1 %copy-start = (bf16[320,1152]{1,0:T(8,128)(2,1)S(1)}, bf16[320,1152]{1,0:T(8,128)(2,1)}, u32[]{:S(2)}) copy-start(bf16[320,1152]{1,0:T(8,128)(2,1)} %refs_0_.9) | copy-start | bytes 2211844
  1.7 6.1 %copy-start.1 = (bf16[320,1152]{1,0:T(8,128)(2,1)S(1)}, bf16[320,1152]{1,0:T(8,128)(2,1)}, u32[]{:S(2)}) copy-start(bf16[320,1152]{1,0:T(8,128)(2,1)} %refs_0_.9) | copy-start | bytes 2211844
  1.8 1.2 %copy-start.2 = (bf16[320,1152]{1,0:T(8,128)(2,1)S(1)}, bf16[320,1152]{1,0:T(8,128)(2,1)}, u32[]{:S(2)}) copy-start(bf16[320,1152]{1,0:T(8,128)(2,1)} %refs_0_.7) | copy-start | bytes 2211844
  3.0 0.7 copy-start.3
  3.7 15.9 %collective-permute-start.4 = (bf16[336,1152]{1,0:T(8,128)(2,1)S(1)}, bf16[336,1152]{1,0:T(8,128)(2,1)S(1)}, u32[]{:S(2)}, u32[]{:S(2)}) collective-permute-start(bf16[336,1152]{1,0:T(8,128)(2,1)S(1)} %pack.1.refs_2_), channel_id=1, source_target_pairs={{0,1},{1,0},{2,3},{3,2},{4,5},{5,4},{6,7},{7,6},{8,9},{9,8},{10,11... | collective-permute-start | bytes 2322440 | tf_op jit(solution)/shard_map/ppermute | solution.py:114
  7.0 12.5 %collective-permute-start.3 = (bf16[112,1152]{1,0:T(8,128)(2,1)S(1)}, bf16[112,1152]{1,0:T(8,128)(2,1)S(1)}, u32[]{:S(2)}, u32[]{:S(2)}) collective-permute-start(bf16[112,1152]{1,0:T(8,128)(2,1)S(1)} %cut_0.1.refs_2_.refs_1_.refs_0_.refs_6_), channel_id=1, source_target_pairs={{0,8},{1,9},{2,10},{3,11},{4,12},{5,13},{6,14},{7,15},{8,16},{9,17... | collective-permute-start | bytes 774152 | tf_op jit(solution)/shard_map/ppermute | solution.py:114
  7.0 25.7 %collective-permute-start = (bf16[336,1152]{1,0:T(8,128)(2,1)S(1)}, bf16[336,1152]{1,0:T(8,128)(2,1)S(1)}, u32[]{:S(2)}, u32[]{:S(2)}) collective-permute-start(bf16[336,1152]{1,0:T(8,128)(2,1)S(1)} %pack.1.refs_2_), channel_id=1, source_target_pairs={{0,2},{1,3},{2,0},{3,1},{4,6},{5,7},{6,4},{7,5},{8,10},{9,11},{10,... | collective-permute-start | bytes 2322440 | tf_op jit(solution)/shard_map/ppermute | solution.py:114
  7.8 17.3 %collective-permute-start.2 = (bf16[112,1152]{1,0:T(8,128)(2,1)S(1)}, bf16[112,1152]{1,0:T(8,128)(2,1)S(1)}, u32[]{:S(2)}, u32[]{:S(2)}) collective-permute-start(bf16[112,1152]{1,0:T(8,128)(2,1)S(1)} %cut_112.1.refs_1_.refs_0_.refs_7_), channel_id=1, source_target_pairs={{0,8},{1,9},{2,10},{3,11},{4,12},{5,13},{6,14},{7,15},{8,16},{9,17... | collective-permute-start | bytes 774152 | tf_op jit(solution)/shard_map/ppermute | solution.py:114
  9.2 20.7 %collective-permute-start.1 = (bf16[96,1152]{1,0:T(8,128)(2,1)S(1)}, bf16[96,1152]{1,0:T(8,128)(2,1)S(1)}, u32[]{:S(2)}, u32[]{:S(2)}) collective-permute-start(bf16[96,1152]{1,0:T(8,128)(2,1)S(1)} %cut_224.1.refs_0_.refs_8_), channel_id=1, source_target_pairs={{0,8},{1,9},{2,10},{3,11},{4,12},{5,13},{6,14},{7,15},{8,16},{9,17... | collective-permute-start | bytes 663560 | tf_op jit(solution)/shard_map/ppermute | solution.py:114
  19.6 10.2 %collective-permute-start.5 = (bf16[112,1152]{1,0:T(8,128)(2,1)S(1)}, bf16[112,1152]{1,0:T(8,128)(2,1)S(1)}, u32[]{:S(2)}, u32[]{:S(2)}) collective-permute-start(bf16[112,1152]{1,0:T(8,128)(2,1)S(1)} %pick_0.1.refs_2_), channel_id=1, source_target_pairs={{0,6},{1,7},{2,4},{3,5},{4,2},{5,3},{6,0},{7,1},{8,14},{9,15},{10,... | collective-permute-start | bytes 774152 | tf_op jit(solution)/shard_map/ppermute | solution.py:114
  25.1 8.5 %collective-permute-start.7 = (bf16[112,1152]{1,0:T(8,128)(2,1)S(1)}, bf16[112,1152]{1,0:T(8,128)(2,1)S(1)}, u32[]{:S(2)}, u32[]{:S(2)}) collective-permute-start(bf16[112,1152]{1,0:T(8,128)(2,1)S(1)} %pick_112.1.refs_2_), channel_id=1, source_target_pairs={{0,6},{1,7},{2,4},{3,5},{4,2},{5,3},{6,0},{7,1},{8,14},{9,15},{10,... | collective-permute-start | bytes 774152 | tf_op jit(solution)/shard_map/ppermute | solution.py:114
  29.9 9.0 %collective-permute-start.8 = (bf16[96,1152]{1,0:T(8,128)(2,1)S(1)}, bf16[96,1152]{1,0:T(8,128)(2,1)S(1)}, u32[]{:S(2)}, u32[]{:S(2)}) collective-permute-start(bf16[96,1152]{1,0:T(8,128)(2,1)S(1)} %pick_224.1.refs_1_), channel_id=1, source_target_pairs={{0,6},{1,7},{2,4},{3,5},{4,2},{5,3},{6,0},{7,1},{8,14},{9,15},{10,... | collective-permute-start | bytes 663560 | tf_op jit(solution)/shard_map/ppermute | solution.py:114
  32.7 2.8 %collective-permute-start.6 = (bf16[336,1152]{1,0:T(8,128)(2,1)S(1)}, bf16[336,1152]{1,0:T(8,128)(2,1)S(1)}, u32[]{:S(2)}, u32[]{:S(2)}) collective-permute-start(bf16[336,1152]{1,0:T(8,128)(2,1)S(1)} %gate_pair.1.refs_3_), channel_id=1, source_target_pairs={{0,1},{1,0},{2,3},{3,2},{4,5},{5,4},{6,7},{7,6},{8,9},{9,8},{10,11... | collective-permute-start | bytes 2322440 | tf_op jit(solution)/shard_map/ppermute | solution.py:114
  41.6 8.0 %collective-permute-start.9 = (bf16[320,1152]{1,0:T(8,128)(2,1)S(1)}, bf16[320,1152]{1,0:T(8,128)(2,1)S(1)}, u32[]{:S(2)}, u32[]{:S(2)}) collective-permute-start(bf16[320,1152]{1,0:T(8,128)(2,1)S(1)} %get-tuple-element.20), channel_id=1, source_target_pairs={{0,1},{1,0},{2,3},{3,2},{4,5},{5,4},{6,7},{7,6},{8,9},{9,8},{10,11... | collective-permute-start | bytes 2211848 | tf_op jit(solution)/shard_map/ppermute | solution.py:114
  44.2 10.8 %collective-permute-start.12 = (bf16[112,1152]{1,0:T(8,128)(2,1)S(1)}, bf16[112,1152]{1,0:T(8,128)(2,1)S(1)}, u32[]{:S(2)}, u32[]{:S(2)}) collective-permute-start(bf16[112,1152]{1,0:T(8,128)(2,1)S(1)} %get-tuple-element.23.refs_1_), channel_id=1, source_target_pairs={{0,6},{1,7},{2,4},{3,5},{4,2},{5,3},{6,0},{7,1},{8,14},{9,15},{10,... | collective-permute-start | bytes 774152 | tf_op jit(solution)/shard_map/ppermute | solution.py:114
  46.9 11.9 %collective-permute-start.13 = (bf16[112,1152]{1,0:T(8,128)(2,1)S(1)}, bf16[112,1152]{1,0:T(8,128)(2,1)S(1)}, u32[]{:S(2)}, u32[]{:S(2)}) collective-permute-start(bf16[112,1152]{1,0:T(8,128)(2,1)S(1)} %gate_g_1.1.refs_1_), channel_id=1, source_target_pairs={{0,6},{1,7},{2,4},{3,5},{4,2},{5,3},{6,0},{7,1},{8,14},{9,15},{10,... | collective-permute-start | bytes 774152 | tf_op jit(solution)/shard_map/ppermute | solution.py:114
  47.0 16.5 %collective-permute-start.14 = (bf16[96,1152]{1,0:T(8,128)(2,1)S(1)}, bf16[96,1152]{1,0:T(8,128)(2,1)S(1)}, u32[]{:S(2)}, u32[]{:S(2)}) collective-permute-start(bf16[96,1152]{1,0:T(8,128)(2,1)S(1)} %gate_g_2.1), channel_id=1, source_target_pairs={{0,6},{1,7},{2,4},{3,5},{4,2},{5,3},{6,0},{7,1},{8,14},{9,15},{10,... | collective-permute-start | bytes 663560 | tf_op jit(solution)/shard_map/ppermute | solution.py:114
  54.0 20.5 %collective-permute-start.10 = (bf16[320,1152]{1,0:T(8,128)(2,1)S(1)}, bf16[320,1152]{1,0:T(8,128)(2,1)S(1)}, u32[]{:S(2)}, u32[]{:S(2)}) collective-permute-start(bf16[320,1152]{1,0:T(8,128)(2,1)S(1)} %get-tuple-element.22.refs_2_), channel_id=1, source_target_pairs={{0,1},{1,0},{2,3},{3,2},{4,5},{5,4},{6,7},{7,6},{8,9},{9,8},{10,11... | collective-permute-start | bytes 2211848 | tf_op jit(solution)/shard_map/ppermute | solution.py:114
  55.0 19.6 %collective-permute-start.11 = (bf16[320,1152]{1,0:T(8,128)(2,1)S(1)}, bf16[320,1152]{1,0:T(8,128)(2,1)S(1)}, u32[]{:S(2)}, u32[]{:S(2)}) collective-permute-start(bf16[320,1152]{1,0:T(8,128)(2,1)S(1)} %to_pair.1.refs_2_), channel_id=1, source_target_pairs={{0,2},{1,3},{2,0},{3,1},{4,6},{5,7},{6,4},{7,5},{8,10},{9,11},{10,... | collective-permute-start | bytes 2211848 | tf_op jit(solution)/shard_map/ppermute | solution.py:114
  55.1 18.0 %collective-permute-start.15 = (bf16[112,1152]{1,0:T(8,128)(2,1)S(1)}, bf16[112,1152]{1,0:T(8,128)(2,1)S(1)}, u32[]{:S(2)}, u32[]{:S(2)}) collective-permute-start(bf16[112,1152]{1,0:T(8,128)(2,1)S(1)} %to_prev_0.1.refs_2_), channel_id=1, source_target_pairs={{0,248},{1,249},{2,250},{3,251},{4,252},{5,253},{6,254},{7,255},{8... | collective-permute-start | bytes 774152 | tf_op jit(solution)/shard_map/ppermute | solution.py:114
  58.9 14.2 %collective-permute-start.16 = (bf16[112,1152]{1,0:T(8,128)(2,1)S(1)}, bf16[112,1152]{1,0:T(8,128)(2,1)S(1)}, u32[]{:S(2)}, u32[]{:S(2)}) collective-permute-start(bf16[112,1152]{1,0:T(8,128)(2,1)S(1)} %to_prev_112.1.refs_2_), channel_id=1, source_target_pairs={{0,248},{1,249},{2,250},{3,251},{4,252},{5,253},{6,254},{7,255},{8... | collective-permute-start | bytes 774152 | tf_op jit(solution)/shard_map/ppermute | solution.py:114
  63.7 9.4 %collective-permute-start.17 = (bf16[96,1152]{1,0:T(8,128)(2,1)S(1)}, bf16[96,1152]{1,0:T(8,128)(2,1)S(1)}, u32[]{:S(2)}, u32[]{:S(2)}) collective-permute-start(bf16[96,1152]{1,0:T(8,128)(2,1)S(1)} %to_prev_224.1), channel_id=1, source_target_pairs={{0,248},{1,249},{2,250},{3,251},{4,252},{5,253},{6,254},{7,255},{8... | collective-permute-start | bytes 663560 | tf_op jit(solution)/shard_map/ppermute | solution.py:114

commit v3 on v2

v3 whole, which is shorter than its diff:
```python
import jax
import jax.numpy as jnp
from jax import lax
from jax.experimental import pallas as pl
from jax.experimental.pallas import tpu as pltpu
from jax.sharding import PartitionSpec as P

AXES = ("blk", "inner")
BF = jnp.bfloat16
F32 = jnp.float32
CUTS = 3
LATE = 1
PICK_US = 6
SEND_US = (8, 8, 0)
GATE_US = 0
END_US = 0
GATE_X = (16, 0)
BACK_US = 14
LAST_US = 16
PAIR_US = 0
VMEM = pl.BlockSpec(memory_space=pltpu.VMEM)
SMEM = pl.BlockSpec(memory_space=pltpu.SMEM)
ANY = pl.BlockSpec(memory_space=pl.ANY)
HBM = pl.BlockSpec(memory_space=pltpu.HBM)


def routes(nblk, ninner):
    def route(place):
        out = []
        for blk in range(nblk):
            for inner in range(ninner):
                c, h, l, k = place(blk // 2, blk % 2, inner // 2, inner % 2)
                out.append((blk * ninner + inner, ((c % (nblk // 2)) * 2 + h) * ninner + l * 2 + k))
        return out

    return {
        "core": route(lambda c, h, l, k: (c, h, l, 1 - k)),
        "pair": route(lambda c, h, l, k: (c, h, 1 - l, k)),
        "mirror": route(lambda c, h, l, k: (c, 1 - h, 1 - l, k)),
        "next": route(lambda c, h, l, k: (c + 1, h, l, k)),
        "prev": route(lambda c, h, l, k: (c - 1, h, l, k)),
    }


def pieces(n, cuts):
    size = -(-n // (cuts * 16)) * 16
    return [slice(a, min(a + size, n)) for a in range(0, n, size)]


def nt(a, b):
    return lax.dot_general(a, b, (((1,), (1,)), ((), ())), preferred_element_type=F32)


def tn(a, b):
    return lax.dot_general(a, b, (((0,), (0,)), ((), ())), preferred_element_type=F32)


def nn(a, b):
    return jnp.dot(a, b, preferred_element_type=F32)


def call(body, name, outs, ins, scalars=(), aliases=None, after=(), us=0):
    shapes = tuple(jax.ShapeDtypeStruct(s, d) for s, d in outs)
    ns, ni, na = len(scalars), len(ins), len(after)

    def run(*refs):
        body(*refs[: ns + ni], *refs[ns + ni + na :])

    return pl.pallas_call(
        run,
        out_shape=shapes,
        in_specs=[SMEM] * ns + [VMEM] * ni + [ANY] * na,
        out_specs=tuple(VMEM for _ in shapes),
        input_output_aliases={k + ns: v for k, v in (aliases or {}).items()},
        compiler_params=pltpu.CompilerParams(vmem_limit_bytes=16 * 2**20),
        cost_estimate=pl.CostEstimate(flops=int(us * 1e9), bytes_accessed=0, transcendentals=0),
        name=name,
    )(*scalars, *ins, *after)


def gate(value, name, after=(), us=0):
    spec = [(value.shape, value.dtype)]
    return call(lambda a, b: None, name, spec, [value], aliases={0: 0}, after=after, us=us)[0]


def is_upper():
    return lax.rem(lax.axis_index("blk"), 2) == 1


def k_positives(own, other, image, out, kept):
    n = own.shape[0]
    kept[...] = image[...]
    out[...] = jnp.zeros(out.shape, out.dtype)
    out[0:1, :n] = own[...].reshape(1, n)
    out[0:1, n:] = other[...].reshape(1, n)


def tile_of(scale, bias, texts, images, pos=None):
    s = jax.nn.sigmoid(scale[0] * nt(texts, images) + bias[0])
    if pos is not None:
        first = lax.axis_index("inner") * texts.shape[0]
        at = lax.broadcasted_iota(jnp.int32, s.shape, 0) + first
        s = s - (at == pos).astype(F32)
    return (scale[0] * s).astype(BF)


def local(image, text, positive, logit_scale, logit_bias):
    nblk, ninner = lax.axis_size("blk"), lax.axis_size("inner")
    way = routes(nblk, ninner)
    move = lambda v, name: lax.ppermute(v, AXES, way[name])
    sc = (logit_scale, logit_bias)
    n, d = text.shape
    m = ninner * n
    parts = pieces(n, CUTS)
    size = [p.stop - p.start for p in parts]
    cuts = len(parts)
    early = cuts - LATE
    base = 2 * n
    done = base + parts[early].start
    blocks = [slice(j * n, (j + 1) * n) for j in range(ninner)]

    cut = []
    for p, s in zip(parts, size):

        def k_cut(text, out, p=p):
            out[...] = text[p, :]

        cut += call(k_cut, f"cut_{p.start}", [((s, d), BF)], [text], after=cut[-1:])
    text_x = [move(t, "next") for t in cut]
    image_n = move(image, "pair")
    image_c = move(image, "core")
    pos_c = move(positive, "core")

    text_m = []
    picked = []
    pos_n = ()
    for i, (p, s, c, x) in enumerate(zip(parts, size, cut, text_x)):

        def k_pick(own, x, out):
            out[...] = jnp.where(is_upper(), x[...], own[...])

        after = picked[-1:] + [[image_c, pos_c], [], [*text_m[:1], *pos_n]][min(i, 2)]
        (t,) = call(k_pick, f"pick_{p.start}", [((s, d), BF)], [c, x], after=after, us=PICK_US)
        picked.append(t)
        text_m.append(move(t, "mirror"))
        if i == 0:
            pos_own, kept = call(
                k_positives, "positives", [((8, 2 * n), jnp.int32), ((n, d), BF)], [positive, pos_c, image], after=[t]
            )
            pos_n = [move(pos_own, "pair")]
            picked.append(pos_own)
        if i == cuts - 2:
            image_n = gate(image_n, "gate_pair", [t], us=PAIR_US)
            image_nc = move(image_n, "core")
            picked.append(image_n)

    def k_tiles(scale, bias, i0, i_n, i_c, i_nc, pos_own, pos_n, *refs):
        own, xs = refs[:cuts], refs[cuts : 2 * cuts]
        images, texts, tiles, pos = refs[2 * cuts :]
        for rows, ref in zip(blocks, (i_nc, i_c, i_n, i0)):
            images[rows, :] = ref[...]
        for j, ref, at in ((0, pos_n, n), (1, pos_own, n), (2, pos_n, 0), (3, pos_own, 0)):
            pos[0:1, blocks[j]] = ref[0:1, at : at + n]
        for k, group in enumerate((own, xs)):
            for p, ref in zip(parts, group):
                texts[k * n + p.start : k * n + p.stop, :] = ref[...]
        tiles[:n, :] = tile_of(scale, bias, texts[:n, :], images[...], pos[0:1, :])
        tiles[n:base, :] = tile_of(scale, bias, texts[n:base, :], images[...])

    images, texts, tiles, _ = call(
        k_tiles, "tiles", [((m, d), BF), ((3 * n, d), BF), ((3 * n, m), BF), ((8, m), jnp.int32)],
        [kept, image_n, image_c, image_nc, pos_own, *pos_n, *cut, *text_x], sc,
    )

    for i in range(early):
        text_m[i] = gate(text_m[i], f"gate_m_{i}", [tiles, *text_m[:i]], us=GATE_US)

    def k_next_grads(tiles, images, out):
        out[...] = nn(tiles[n:base, :], images[...])

    def k_mirror_first(scale, bias, images, *refs):
        got, (_, _, texts, tiles, grad) = refs[:early], refs[early:]
        for p, t in zip(parts, got):
            texts[base + p.start : base + p.stop, :] = t[...]
        tiles[base:done, :] = tile_of(scale, bias, texts[base:done, :], images[...])
        grad[...] = nn(tiles[base : base + parts[0].stop, :], images[...]).astype(BF)

    texts, tiles, *grad_m = call(
        k_mirror_first, "mirror_first", [((3 * n, d), BF), ((3 * n, m), BF), ((size[0], d), BF)],
        [images, *text_m[:early], texts, tiles], sc, aliases={1 + early: 0, 2 + early: 1},
    )
    back_m = [move(grad_m[0], "mirror")]
    text_m[early] = gate(text_m[early], "gate_m_last", grad_m, us=LAST_US)

    def k_last(scale, bias, images, *refs):
        got, (_, _, texts, tiles, to_core) = refs[:LATE], refs[LATE:]
        for p, t in zip(parts[early:], got):
            texts[base + p.start : base + p.stop, :] = t[...]
        tiles[done:, :] = tile_of(scale, bias, texts[done:, :], images[...])
        to_core[...] = tn(tiles[:, : 2 * n], texts[...]).astype(BF)

    texts, tiles, to_core = call(
        k_last, "mirror_last", [((3 * n, d), BF), ((3 * n, m), BF), ((2 * n, d), BF)],
        [images, *text_m[early:], texts, tiles], sc, aliases={1 + LATE: 0, 2 + LATE: 1}, after=grad_m[-1:],
    )
    got_core = move(to_core, "core")

    def k_rest_grads(tiles, images, *grads):
        g = nn(tiles[base + parts[1].start :, :], images[...]).astype(BF)
        for p, ref in zip(parts[1:], grads):
            ref[...] = g[p.start - parts[1].start : p.stop - parts[1].start, :]

    grad_m += call(k_rest_grads, "mirror_rest_grads", [((s, d), BF) for s in size[1:]], [tiles, images])
    back_m.append(move(grad_m[1], "mirror"))
    (gx,) = call(k_next_grads, "next_text_grads", [((n, d), F32)], [tiles, images], after=[grad_m[1]])

    def k_pair(tiles, texts, got_core, out):
        g = tn(tiles[:, 2 * n : 3 * n], texts[...])
        out[...] = (g + got_core[:n, :].astype(F32)).astype(BF)

    back_m[0] = gate(back_m[0], "gate_back_0", [gx], us=BACK_US)
    (send_n,) = call(k_pair, "to_pair", [((n, d), BF)], [tiles, texts, got_core], after=[back_m[0]])
    got_n = move(send_n, "pair")
    def k_own_grads(tiles, images, out):
        out[...] = nn(tiles[:n, :], images[...])

    def k_own_images(tiles, texts, got_core, out):
        skip = n % 128
        g = tn(tiles[:, 3 * n - skip :], texts[...])[skip:, :]
        out[...] = g + got_core[n:, :].astype(F32)

    back_x = []
    sent = []
    for i, (p, s) in enumerate(zip(parts, size)):

        def k_send(gx, back, out, p=p):
            b = jnp.where(is_upper(), back[...].astype(F32), 0.0)
            out[...] = (gx[p, :] + b).astype(BF)

        after = sent[-1:] or [send_n]
        (t,) = call(k_send, f"to_prev_{p.start}", [((s, d), BF)], [gx, back_m[i]], after=after, us=SEND_US[i])
        sent.append(t)
        back_x.append(move(t, "prev"))
        if i == 0:
            for j in range(2, cuts):
                back_m.append(move(gate(grad_m[j], f"gate_g_{j}", [t]), "mirror"))
        if i == 2:
            back_x[0] = gate(back_x[0], "gate_x_0", [t], us=GATE_X[0])
            (gt,) = call(k_own_grads, "own_text_grads", [((n, d), F32)], [tiles, images], after=back_x[:1])
            (gi_own,) = call(k_own_images, "own_images", [((n, d), F32)], [tiles, texts, got_core], after=[gt])

    back_x[1] = gate(back_x[1], "gate_x_1", [], us=GATE_X[1])

    def k_end_images(gi, got_n, out, token):
        out[...] = gi[...] + got_n[...].astype(F32)
        token[...] = jnp.zeros(token.shape, F32)

    grad_images, token = call(k_end_images, "end_images", [((n, d), F32), ((8, 128), F32)], [gi_own, got_n])

    grad_texts = None
    for name, a, b in (("end_texts_first", 0, cuts - 1), ("end_texts_last", cuts - 1, cuts)):
        at, rows = parts[a].start, parts[b - 1].stop - parts[a].start

        def k_end_texts(gt, *refs, a=a, b=b, at=at, rows=rows):
            ms, xs, (out, block, sem) = refs[: b - a], refs[b - a : 2 * (b - a)], refs[-3:]
            up = is_upper()
            for p, m_ref, x_ref in zip(parts[a:b], ms, xs):
                g = gt[p, :] + jnp.where(up, 0.0, m_ref[...].astype(F32)) + x_ref[...].astype(F32)
                block[p.start - at : p.stop - at, :] = g
            copy = pltpu.make_async_copy(block, out.at[pl.ds(at, rows), :], sem)
            copy.start()
            copy.wait()

        ins = [gt, *back_m[a:b], *back_x[a:b]]
        old = [] if grad_texts is None else [grad_texts]
        after = [token] if old else []
        grad_texts = pl.pallas_call(
            k_end_texts,
            out_shape=jax.ShapeDtypeStruct((n, d), F32),
            in_specs=[VMEM] * len(ins) + [HBM] * len(old) + [ANY] * len(after),
            out_specs=HBM,
            input_output_aliases={len(ins): 0} if old else {},
            scratch_shapes=[pltpu.VMEM((rows, d), F32), pltpu.SemaphoreType.DMA],
            compiler_params=pltpu.CompilerParams(vmem_limit_bytes=16 * 2**20),
            cost_estimate=pl.CostEstimate(flops=0 if old else int(END_US * 1e9), bytes_accessed=0, transcendentals=0),
            name=name,
        )(*ins, *old, *after)
    return grad_images, grad_texts


def solution(mesh):
    rows, flat = P(AXES, None), P(AXES)
    return jax.shard_map(
        local,
        mesh=mesh,
        in_specs=(rows, rows, flat, P(), P()),
        out_specs=(rows, rows),
        check_vma=False,
    )
```

time: 76 us -> 67.7 us (0.89); the launches traced: 75.9 us -> 66.6 us
  waiting for transfers between devices: 28.4 us -> 18.7 us
  Pallas kernels: 14.9 us -> 16.8 us
  local copies, waits for them, and re-layouts: 2.97 us -> 1.13 us
    ppermute x18 -> x19, waiting for transfers between devices: 28.4 us -> 18.7 us  [local(): move = lambda v, name: lax.ppermute(v, AXES, way[name])]
    pallas_call x0 -> x2, Pallas kernels: none -> 2.04 us  [local(): pl.pallas_call(k_end_texts, out_shape=jax.ShapeDtypeStruct((n, d), F32),...]
    unnamed x8 -> x6, local copies, waits for them, and re-layouts: 2.97 us -> 1.13 us
    pallas_call x24 -> x27, Pallas kernels: 14.9 us -> 14.7 us  [call(): pl.pallas_call(run, out_shape=shapes, in_specs=[SMEM] * ns + [VMEM] * ni...]
    ppermute x18 -> x19, starting transfers between devices: 27.6 us -> 27.7 us  [local(): move = lambda v, name: lax.ppermute(v, AXES, way[name])]
  transfers between devices with their start and end apart: 18 -> 19, of which waited for: 7 -> 7; matrix products, arithmetic and copies ran while one was open for 0% -> 0% of each run, Pallas kernels for 14% -> 24%
where the time goes in v3:
time: 67.7 us; the launch traced here: 66.6 us
  starting transfers between devices  27.7 us (41%)
  waiting for transfers between devices  18.7 us (28%)
  Pallas kernels  16.8 us (25%)
  between operations  2.31 us (3%)
  local copies, waits for them, and re-layouts  1.13 us (2%)
    ppermute x19, starting transfers between devices, local(): move = lambda v, name: lax.ppermute(v, AXES, way[name])  27.7 us
    ppermute x19, waiting for transfers between devices, local(): move = lambda v, name: lax.ppermute(v, AXES, way[name])  18.7 us
    pallas_call x27, Pallas kernels, call(): pl.pallas_call(run, out_shape=shapes, in_specs=[SMEM] * ns + [VMEM] * ni...  14.7 us
    pallas_call x2, Pallas kernels, local(): pl.pallas_call(k_end_texts, out_shape=jax.ShapeDtypeStruct((n, d), F32),...  2.04 us
  transfers between devices with their start and end apart: 19, of which 7 were waited for; matrix products, arithmetic and copies ran while one was open for 0% of the time, Pallas kernels for 24%

profile of v3, /device:TPU:1, one launch (start us, length us, event | category | flops | bytes accessed | tf_op | source)
XLA Modules:
  0.0 66.6 jit_solution(3230525064751436268)
XLA Ops:
  0.6 3.3 %collective-permute-start.2 = (bf16[320,1152]{1,0:T(8,128)(2,1)}, bf16[320,1152]{1,0:T(8,128)(2,1)S(1)}, u32[]{:S(2)}, u32[]{:S(2)}) collective-permute-start(bf16[320,1152]{1,0:T(8,128)(2,1)} %refs_2_.1), channel_id=1, source_target_pairs={{0,1},{1,0},{2,3},{3,2},{4,5},{5,4},{6,7},{7,6},{8,9},{9,8},{10,11... | collective-permute-start | bytes 2211848 | tf_op jit(solution)/shard_map/ppermute | solution.py:110
  4.0 1.1 %copy-done = bf16[320,1152]{1,0:T(8,128)(2,1)S(1)} copy-done((bf16[320,1152]{1,0:T(8,128)(2,1)S(1)}, bf16[320,1152]{1,0:T(8,128)(2,1)}, u32[]{:S(2)}) %copy-start) | copy-done | bytes 737304
  5.3 1.0 %collective-permute-start.3 = (bf16[320,1152]{1,0:T(8,128)(2,1)}, bf16[320,1152]{1,0:T(8,128)(2,1)S(1)}, u32[]{:S(2)}, u32[]{:S(2)}) collective-permute-start(bf16[320,1152]{1,0:T(8,128)(2,1)} %refs_2_.1), channel_id=1, source_target_pairs={{0,2},{1,3},{2,0},{3,1},{4,6},{5,7},{6,4},{7,5},{8,10},{9,11},{10,... | collective-permute-start | bytes 2211848 | tf_op jit(solution)/shard_map/ppermute | solution.py:110
  6.3 1.3 %collective-permute-start.4 = (bf16[112,1152]{1,0:T(8,128)(2,1)S(1)}, bf16[112,1152]{1,0:T(8,128)(2,1)S(1)}, u32[]{:S(2)}, u32[]{:S(2)}) collective-permute-start(bf16[112,1152]{1,0:T(8,128)(2,1)S(1)} %cut_112.1.refs_0_.refs_1_.refs_9_), channel_id=1, source_target_pairs={{0,8},{1,9},{2,10},{3,11},{4,12},{5,13},{6,14},{7,15},{8,16},{9,17... | collective-permute-start | bytes 774152 | tf_op jit(solution)/shard_map/ppermute | solution.py:110
  7.6 1.0 %collective-permute-start.7 = (bf16[96,1152]{1,0:T(8,128)(2,1)S(1)}, bf16[96,1152]{1,0:T(8,128)(2,1)S(1)}, u32[]{:S(2)}, u32[]{:S(2)}) collective-permute-start(bf16[96,1152]{1,0:T(8,128)(2,1)S(1)} %cut_224.1.refs_10_.refs_0_), channel_id=1, source_target_pairs={{0,8},{1,9},{2,10},{3,11},{4,12},{5,13},{6,14},{7,15},{8,16},{9,17... | collective-permute-start | bytes 663560 | tf_op jit(solution)/shard_map/ppermute | solution.py:110
  8.6 9.2 %collective-permute-done.1.refs_1_.refs_11_ = bf16[112,1152]{1,0:T(8,128)(2,1)S(1)} collective-permute-done((bf16[112,1152]{1,0:T(8,128)(2,1)S(1)}, bf16[112,1152]{1,0:T(8,128)(2,1)S(1)}, u32[]{:S(2)}, u32[]{:S(2)}) %collective-permute-start.1) | collective-permute-done | bytes 258080 | tf_op jit(solution)/shard_map/ppermute | solution.py:110
  17.8 2.8 %collective-permute-start.8 = (bf16[112,1152]{1,0:T(8,128)(2,1)S(1)}, bf16[112,1152]{1,0:T(8,128)(2,1)S(1)}, u32[]{:S(2)}, u32[]{:S(2)}) collective-permute-start(bf16[112,1152]{1,0:T(8,128)(2,1)S(1)} %pick_0.1.refs_3_), channel_id=1, source_target_pairs={{0,6},{1,7},{2,4},{3,5},{4,2},{5,3},{6,0},{7,1},{8,14},{9,15},{10,... | collective-permute-start | bytes 774152 | tf_op jit(solution)/shard_map/ppermute | solution.py:110
  20.8 2.5 %collective-permute-done.4.refs_1_.refs_12_ = bf16[112,1152]{1,0:T(8,128)(2,1)S(1)} collective-permute-done((bf16[112,1152]{1,0:T(8,128)(2,1)S(1)}, bf16[112,1152]{1,0:T(8,128)(2,1)S(1)}, u32[]{:S(2)}, u32[]{:S(2)}) %collective-permute-start.4) | collective-permute-done | bytes 258080 | tf_op jit(solution)/shard_map/ppermute | solution.py:110
  23.4 2.8 %collective-permute-start.10 = (bf16[112,1152]{1,0:T(8,128)(2,1)S(1)}, bf16[112,1152]{1,0:T(8,128)(2,1)S(1)}, u32[]{:S(2)}, u32[]{:S(2)}) collective-permute-start(bf16[112,1152]{1,0:T(8,128)(2,1)S(1)} %pick_112.1.refs_1_), channel_id=1, source_target_pairs={{0,6},{1,7},{2,4},{3,5},{4,2},{5,3},{6,0},{7,1},{8,14},{9,15},{10,... | collective-permute-start | bytes 774152 | tf_op jit(solution)/shard_map/ppermute | solution.py:110
  26.2 1.1 %collective-permute-start.5 = (bf16[320,1152]{1,0:T(8,128)(2,1)S(1)}, bf16[320,1152]{1,0:T(8,128)(2,1)S(1)}, u32[]{:S(2)}, u32[]{:S(2)}) collective-permute-start(bf16[320,1152]{1,0:T(8,128)(2,1)S(1)} %gate_pair.1.refs_3_.refs_2_), channel_id=1, source_target_pairs={{0,1},{1,0},{2,3},{3,2},{4,5},{5,4},{6,7},{7,6},{8,9},{9,8},{10,11... | collective-permute-start | bytes 2211848 | tf_op jit(solution)/shard_map/ppermute | solution.py:110
  27.3 0.8 %collective-permute-done.7.refs_13_.refs_1_ = bf16[96,1152]{1,0:T(8,128)(2,1)S(1)} collective-permute-done((bf16[96,1152]{1,0:T(8,128)(2,1)S(1)}, bf16[96,1152]{1,0:T(8,128)(2,1)S(1)}, u32[]{:S(2)}, u32[]{:S(2)}) %collective-permute-start.7) | collective-permute-done | bytes 221216 | tf_op jit(solution)/shard_map/ppermute | solution.py:110
  28.1 2.8 %collective-permute-start.9 = (bf16[96,1152]{1,0:T(8,128)(2,1)S(1)}, bf16[96,1152]{1,0:T(8,128)(2,1)S(1)}, u32[]{:S(2)}, u32[]{:S(2)}) collective-permute-start(bf16[96,1152]{1,0:T(8,128)(2,1)S(1)} %pick_224.1), channel_id=1, source_target_pairs={{0,6},{1,7},{2,4},{3,5},{4,2},{5,3},{6,0},{7,1},{8,14},{9,15},{10,... | collective-permute-start | bytes 663560 | tf_op jit(solution)/shard_map/ppermute | solution.py:110
  32.2 2.6 %tiles.1 = (bf16[1280,1152]{1,0:T(8,128)(2,1)S(1)}, bf16[960,1152]{1,0:T(8,128)(2,1)S(1)}, bf16[960,1280]{1,0:T(8,128)(2,1)S(1)}, s32[8,1280]{1,0:T(8,128)}) custom-call(f32[1]{0:T(128)S(6)} %copy.33.refs_0_, f32[1]{0:T(128)S(6)} %copy.34.refs_1_, bf16[320,1152]{1,0:T(8,128)(2,1)S(1)} %get-tuple-element.17.refs_2_, ...), custom_call_target="tpu_custom_call" | custom-call | tf_op jit(solution)/shard_map/tiles/pallas_call | solution.py:69
  34.9 1.8 %mirror_first.1 = (bf16[960,1152]{1,0:T(8,128)(2,1)S(1)}, bf16[960,1280]{1,0:T(8,128)(2,1)S(1)}, bf16[112,1152]{1,0:T(8,128)(2,1)S(1)}) custom-call(f32[1]{0:T(128)S(6)} %copy.33.refs_0_, f32[1]{0:T(128)S(6)} %copy.34.refs_1_, bf16[1280,1152]{1,0:T(8,128)(2,1)S(1)} %get-tuple-element.19.refs_2_.refs_1_, ...), custom_call_target="tpu_custom_call", output_to_operand_aliasing={{0}: (5, {}), {1}: (6, {})} | custom-call | tf_op jit(solution)/shard_map/mirror_first/pallas_call | solution.py:69
  37.0 2.8 %mirror_last.1 = (bf16[960,1152]{1,0:T(8,128)(2,1)S(1)}, bf16[960,1280]{1,0:T(8,128)(2,1)S(1)}, bf16[640,1152]{1,0:T(8,128)(2,1)S(1)}) custom-call(f32[1]{0:T(128)S(6)} %copy.33.refs_0_, f32[1]{0:T(128)S(6)} %copy.34.refs_1_, bf16[1280,1152]{1,0:T(8,128)(2,1)S(1)} %get-tuple-element.19.refs_2_.refs_1_, ...), custom_call_target="tpu_custom_call", output_to_operand_aliasing={{0}: (4, {}), {1}: (5, {})} | custom-call | tf_op jit(solution)/shard_map/mirror_last/pallas_call | solution.py:69
  39.8 2.2 %collective-permute-start.11 = (bf16[640,1152]{1,0:T(8,128)(2,1)S(1)}, bf16[640,1152]{1,0:T(8,128)(2,1)S(1)}, u32[]{:S(2)}, u32[]{:S(2)}) collective-permute-start(bf16[640,1152]{1,0:T(8,128)(2,1)S(1)} %get-tuple-element.27), channel_id=1, source_target_pairs={{0,1},{1,0},{2,3},{3,2},{4,5},{5,4},{6,7},{7,6},{8,9},{9,8},{10,11... | collective-permute-start | bytes 4423688 | tf_op jit(solution)/shard_map/ppermute | solution.py:110
  41.9 0.9 %mirror_rest_grads.1 = (bf16[112,1152]{1,0:T(8,128)(2,1)S(1)}, bf16[96,1152]{1,0:T(8,128)(2,1)S(1)}) custom-call(bf16[960,1280]{1,0:T(8,128)(2,1)S(1)} %get-tuple-element.25.refs_0_, bf16[1280,1152]{1,0:T(8,128)(2,1)S(1)} %get-tuple-element.19.refs_2_.refs_1_), custom_call_target="tpu_custom_call" | custom-call | tf_op jit(solution)/shard_map/mirror_rest_grads/pallas_call | solution.py:69
  42.8 1.2 %next_text_grads.1.refs_1_.refs_0_ = f32[320,1152]{1,0:T(8,128)S(1)} custom-call(bf16[960,1280]{1,0:T(8,128)(2,1)S(1)} %get-tuple-element.25.refs_0_, bf16[1280,1152]{1,0:T(8,128)(2,1)S(1)} %get-tuple-element.19.refs_2_.refs_1_, bf16[112,1152]{1,0:T(8,128)(2,1)S(1)} %get-tuple-element.28.refs_2_), custom_call_target="tpu_custom_call" | custom-call | tf_op jit(solution)/shard_map/next_text_grads/pallas_call | solution.py:69
  44.1 1.8 %collective-permute-start.15 = (bf16[112,1152]{1,0:T(8,128)(2,1)S(1)}, bf16[112,1152]{1,0:T(8,128)(2,1)S(1)}, u32[]{:S(2)}, u32[]{:S(2)}) collective-permute-start(bf16[112,1152]{1,0:T(8,128)(2,1)S(1)} %get-tuple-element.28.refs_2_), channel_id=1, source_target_pairs={{0,6},{1,7},{2,4},{3,5},{4,2},{5,3},{6,0},{7,1},{8,14},{9,15},{10,... | collective-permute-start | bytes 774152 | tf_op jit(solution)/shard_map/ppermute | solution.py:110
  45.9 1.1 %to_pair.1.refs_2_ = bf16[320,1152]{1,0:T(8,128)(2,1)S(1)} custom-call(bf16[960,1280]{1,0:T(8,128)(2,1)S(1)} %get-tuple-element.25.refs_0_, bf16[960,1152]{1,0:T(8,128)(2,1)S(1)} %get-tuple-element.26.refs_1_, bf16[640,1152]{1,0:T(8,128)(2,1)S(1)} %collective-permute-done.11.refs_2_, bf16[112,1152]{1,0:T(8,128)(2,1)S(1)} %gate_back_0.1.refs_3_.refs_1_.refs_0_), custom_call_target="tpu_custom_call" | custom-call | tf_op jit(solution)/shard_map/to_pair/pallas_call | solution.py:69
  47.2 2.4 %collective-permute-start.13 = (bf16[112,1152]{1,0:T(8,128)(2,1)S(1)}, bf16[112,1152]{1,0:T(8,128)(2,1)S(1)}, u32[]{:S(2)}, u32[]{:S(2)}) collective-permute-start(bf16[112,1152]{1,0:T(8,128)(2,1)S(1)} %to_prev_0.1.refs_1_.refs_2_), channel_id=1, source_target_pairs={{0,248},{1,249},{2,250},{3,251},{4,252},{5,253},{6,254},{7,255},{8... | collective-permute-start | bytes 774152 | tf_op jit(solution)/shard_map/ppermute | solution.py:110
  49.6 0.6 collective-permute-start.14
  50.2 3.0 %collective-permute-done.15.refs_1_ = bf16[112,1152]{1,0:T(8,128)(2,1)S(1)} collective-permute-done((bf16[112,1152]{1,0:T(8,128)(2,1)S(1)}, bf16[112,1152]{1,0:T(8,128)(2,1)S(1)}, u32[]{:S(2)}, u32[]{:S(2)}) %collective-permute-start.15) | collective-permute-done | bytes 258080 | tf_op jit(solution)/shard_map/ppermute | solution.py:110
  53.3 1.7 %collective-permute-start.18 = (bf16[112,1152]{1,0:T(8,128)(2,1)S(1)}, bf16[112,1152]{1,0:T(8,128)(2,1)S(1)}, u32[]{:S(2)}, u32[]{:S(2)}) collective-permute-start(bf16[112,1152]{1,0:T(8,128)(2,1)S(1)} %to_prev_112.1.refs_2_), channel_id=1, source_target_pairs={{0,248},{1,249},{2,250},{3,251},{4,252},{5,253},{6,254},{7,255},{8... | collective-permute-start | bytes 774152 | tf_op jit(solution)/shard_map/ppermute | solution.py:110
  55.0 1.4 %collective-permute-done.14.refs_1_.refs_0_ = bf16[96,1152]{1,0:T(8,128)(2,1)S(1)} collective-permute-done((bf16[96,1152]{1,0:T(8,128)(2,1)S(1)}, bf16[96,1152]{1,0:T(8,128)(2,1)S(1)}, u32[]{:S(2)}, u32[]{:S(2)}) %collective-permute-start.14) | collective-permute-done | bytes 221216 | tf_op jit(solution)/shard_map/ppermute | solution.py:110
  56.5 2.3 %collective-permute-start.17 = (bf16[96,1152]{1,0:T(8,128)(2,1)S(1)}, bf16[96,1152]{1,0:T(8,128)(2,1)S(1)}, u32[]{:S(2)}, u32[]{:S(2)}) collective-permute-start(bf16[96,1152]{1,0:T(8,128)(2,1)S(1)} %to_prev_224.1.refs_1_), channel_id=1, source_target_pairs={{0,248},{1,249},{2,250},{3,251},{4,252},{5,253},{6,254},{7,255},{8... | collective-permute-start | bytes 663560 | tf_op jit(solution)/shard_map/ppermute | solution.py:110
  58.7 1.2 %own_text_grads.1.refs_3_.gt = f32[320,1152]{1,0:T(8,128)S(1)} custom-call(bf16[960,1280]{1,0:T(8,128)(2,1)S(1)} %get-tuple-element.25.refs_0_, bf16[1280,1152]{1,0:T(8,128)(2,1)S(1)} %get-tuple-element.19.refs_2_.refs_1_, bf16[112,1152]{1,0:T(8,128)(2,1)S(1)} %gate_x_0.1.refs_2_), custom_call_target="tpu_custom_call" | custom-call | tf_op jit(solution)/shard_map/own_text_grads/pallas_call | solution.py:69
  60.3 1.2 %own_images.1.refs_0_ = f32[320,1152]{1,0:T(8,128)S(1)} custom-call(bf16[960,1280]{1,0:T(8,128)(2,1)S(1)} %get-tuple-element.25.refs_0_, bf16[960,1152]{1,0:T(8,128)(2,1)S(1)} %get-tuple-element.26.refs_1_, bf16[640,1152]{1,0:T(8,128)(2,1)S(1)} %collective-permute-done.11.refs_2_, f32[320,1152]{1,0:T(8,128)S(1)} %own_text_grads.1.refs_3_.gt), custom_call_target="tpu_custom_call" | custom-call | tf_op jit(solution)/shard_map/own_images/pallas_call | solution.py:69
  61.5 1.2 %end_texts_first.1.refs_2_ = f32[320,1152]{1,0:T(8,128)} custom-call(f32[320,1152]{1,0:T(8,128)S(1)} %own_text_grads.1.refs_3_.gt, bf16[112,1152]{1,0:T(8,128)(2,1)S(1)} %gate_back_0.1.refs_3_.refs_1_.refs_0_, bf16[112,1152]{1,0:T(8,128)(2,1)S(1)} %collective-permute-done.15.refs_1_, bf16[112,1152]{1,0:T(8,128)(2,1)S(1)} %gate_x_0.1.refs_2_, ...), custom_call_target="tpu_custom_call" | custom-call | tf_op jit(solution)/shard_map/end_texts_first/pallas_call | solution.py:277
  62.7 1.6 %collective-permute-done.16.refs_1_ = bf16[320,1152]{1,0:T(8,128)(2,1)S(1)} collective-permute-done((bf16[320,1152]{1,0:T(8,128)(2,1)S(1)}, bf16[320,1152]{1,0:T(8,128)(2,1)S(1)}, u32[]{:S(2)}, u32[]{:S(2)}) %collective-permute-start.16) | collective-permute-done | bytes 737312 | tf_op jit(solution)/shard_map/ppermute | solution.py:110
  64.3 1.3 %end_images.1 = (f32[320,1152]{1,0:T(8,128)}, f32[8,128]{1,0:T(8,128)S(1)}) custom-call(f32[320,1152]{1,0:T(8,128)S(1)} %own_images.1.refs_0_, bf16[320,1152]{1,0:T(8,128)(2,1)S(1)} %collective-permute-done.16.refs_1_), custom_call_target="tpu_custom_call" | custom-call | tf_op jit(solution)/shard_map/end_images/pallas_call | solution.py:69
  65.6 0.9 %end_texts_last.1 = f32[320,1152]{1,0:T(8,128)} custom-call(f32[320,1152]{1,0:T(8,128)S(1)} %own_text_grads.1.refs_3_.gt, bf16[96,1152]{1,0:T(8,128)(2,1)S(1)} %collective-permute-done.14.refs_1_.refs_0_, bf16[96,1152]{1,0:T(8,128)(2,1)S(1)} %collective-permute-done.17.refs_1_, f32[320,1152]{1,0:T(8,128)} %end_texts_first.1.refs_2_, ...), custom_call_target="tpu_custom_call", output_to_operand_aliasing={{}: (3, {})} | custom-call | tf_op jit(solution)/shard_map/end_texts_last/pallas_call | solution.py:277
  (41 shorter events, 1.4 us)
Async XLA Ops:
  0.6 17.2 %collective-permute-start.2 = (bf16[320,1152]{1,0:T(8,128)(2,1)}, bf16[320,1152]{1,0:T(8,128)(2,1)S(1)}, u32[]{:S(2)}, u32[]{:S(2)}) collective-permute-start(bf16[320,1152]{1,0:T(8,128)(2,1)} %refs_2_.1), channel_id=1, source_target_pairs={{0,1},{1,0},{2,3},{3,2},{4,5},{5,4},{6,7},{7,6},{8,9},{9,8},{10,11... | collective-permute-start | bytes 2211848 | tf_op jit(solution)/shard_map/ppermute | solution.py:110
  4.0 1.1 %copy-start = (bf16[320,1152]{1,0:T(8,128)(2,1)S(1)}, bf16[320,1152]{1,0:T(8,128)(2,1)}, u32[]{:S(2)}) copy-start(bf16[320,1152]{1,0:T(8,128)(2,1)} %refs_0_.10) | copy-start | bytes 2211844
  5.1 12.7 %collective-permute-start.1 = (bf16[112,1152]{1,0:T(8,128)(2,1)S(1)}, bf16[112,1152]{1,0:T(8,128)(2,1)S(1)}, u32[]{:S(2)}, u32[]{:S(2)}) collective-permute-start(bf16[112,1152]{1,0:T(8,128)(2,1)S(1)} %cut_0.1.refs_0_.refs_1_.refs_8_), channel_id=1, source_target_pairs={{0,8},{1,9},{2,10},{3,11},{4,12},{5,13},{6,14},{7,15},{8,16},{9,17... | collective-permute-start | bytes 774152 | tf_op jit(solution)/shard_map/ppermute | solution.py:110
  5.2 2.4 %collective-permute-start = (s32[320]{0:T(512)}, s32[320]{0:T(512)S(1)}, u32[]{:S(2)}, u32[]{:S(2)}) collective-permute-start(s32[320]{0:T(512)} %refs_0_.8), channel_id=1, source_target_pairs={{0,1},{1,0},{2,3},{3,2},{4,5},{5,4},{6,7},{7,6},{8,9},{9,8},{10,11... | collective-permute-start | bytes 3848 | tf_op jit(solution)/shard_map/ppermute | solution.py:110
  5.3 20.9 %collective-permute-start.3 = (bf16[320,1152]{1,0:T(8,128)(2,1)}, bf16[320,1152]{1,0:T(8,128)(2,1)S(1)}, u32[]{:S(2)}, u32[]{:S(2)}) collective-permute-start(bf16[320,1152]{1,0:T(8,128)(2,1)} %refs_2_.1), channel_id=1, source_target_pairs={{0,2},{1,3},{2,0},{3,1},{4,6},{5,7},{6,4},{7,5},{8,10},{9,11},{10,... | collective-permute-start | bytes 2211848 | tf_op jit(solution)/shard_map/ppermute | solution.py:110
  6.3 17.1 %collective-permute-start.4 = (bf16[112,1152]{1,0:T(8,128)(2,1)S(1)}, bf16[112,1152]{1,0:T(8,128)(2,1)S(1)}, u32[]{:S(2)}, u32[]{:S(2)}) collective-permute-start(bf16[112,1152]{1,0:T(8,128)(2,1)S(1)} %cut_112.1.refs_0_.refs_1_.refs_9_), channel_id=1, source_target_pairs={{0,8},{1,9},{2,10},{3,11},{4,12},{5,13},{6,14},{7,15},{8,16},{9,17... | collective-permute-start | bytes 774152 | tf_op jit(solution)/shard_map/ppermute | solution.py:110
  7.6 13.1 %copy-start.1 = (bf16[320,1152]{1,0:T(8,128)(2,1)S(1)}, bf16[320,1152]{1,0:T(8,128)(2,1)}, u32[]{:S(2)}) copy-start(bf16[320,1152]{1,0:T(8,128)(2,1)} %refs_2_.1) | copy-start | bytes 2211844
  7.6 13.1 %copy-start.2 = (s32[320]{0:T(512)S(1)}, s32[320]{0:T(512)}, u32[]{:S(2)}) copy-start(s32[320]{0:T(512)} %refs_0_.8) | copy-start | bytes 3844
  7.6 20.4 %collective-permute-start.7 = (bf16[96,1152]{1,0:T(8,128)(2,1)S(1)}, bf16[96,1152]{1,0:T(8,128)(2,1)S(1)}, u32[]{:S(2)}, u32[]{:S(2)}) collective-permute-start(bf16[96,1152]{1,0:T(8,128)(2,1)S(1)} %cut_224.1.refs_10_.refs_0_), channel_id=1, source_target_pairs={{0,8},{1,9},{2,10},{3,11},{4,12},{5,13},{6,14},{7,15},{8,16},{9,17... | collective-permute-start | bytes 663560 | tf_op jit(solution)/shard_map/ppermute | solution.py:110
  17.8 10.2 %collective-permute-start.8 = (bf16[112,1152]{1,0:T(8,128)(2,1)S(1)}, bf16[112,1152]{1,0:T(8,128)(2,1)S(1)}, u32[]{:S(2)}, u32[]{:S(2)}) collective-permute-start(bf16[112,1152]{1,0:T(8,128)(2,1)S(1)} %pick_0.1.refs_3_), channel_id=1, source_target_pairs={{0,6},{1,7},{2,4},{3,5},{4,2},{5,3},{6,0},{7,1},{8,14},{9,15},{10,... | collective-permute-start | bytes 774152 | tf_op jit(solution)/shard_map/ppermute | solution.py:110
  20.8 7.3 %collective-permute-start.6 = (s32[8,640]{1,0:T(8,128)S(1)}, s32[8,640]{1,0:T(8,128)S(1)}, u32[]{:S(2)}, u32[]{:S(2)}) collective-permute-start(s32[8,640]{1,0:T(8,128)S(1)} %get-tuple-element.18.refs_2_.refs_6_), channel_id=1, source_target_pairs={{0,2},{1,3},{2,0},{3,1},{4,6},{5,7},{6,4},{7,5},{8,10},{9,11},{10,... | collective-permute-start | bytes 61448 | tf_op jit(solution)/shard_map/ppermute | solution.py:110
  23.4 11.5 %collective-permute-start.10 = (bf16[112,1152]{1,0:T(8,128)(2,1)S(1)}, bf16[112,1152]{1,0:T(8,128)(2,1)S(1)}, u32[]{:S(2)}, u32[]{:S(2)}) collective-permute-start(bf16[112,1152]{1,0:T(8,128)(2,1)S(1)} %pick_112.1.refs_1_), channel_id=1, source_target_pairs={{0,6},{1,7},{2,4},{3,5},{4,2},{5,3},{6,0},{7,1},{8,14},{9,15},{10,... | collective-permute-start | bytes 774152 | tf_op jit(solution)/shard_map/ppermute | solution.py:110
  26.2 6.0 %collective-permute-start.5 = (bf16[320,1152]{1,0:T(8,128)(2,1)S(1)}, bf16[320,1152]{1,0:T(8,128)(2,1)S(1)}, u32[]{:S(2)}, u32[]{:S(2)}) collective-permute-start(bf16[320,1152]{1,0:T(8,128)(2,1)S(1)} %gate_pair.1.refs_3_.refs_2_), channel_id=1, source_target_pairs={{0,1},{1,0},{2,3},{3,2},{4,5},{5,4},{6,7},{7,6},{8,9},{9,8},{10,11... | collective-permute-start | bytes 2211848 | tf_op jit(solution)/shard_map/ppermute | solution.py:110
  28.1 8.9 %collective-permute-start.9 = (bf16[96,1152]{1,0:T(8,128)(2,1)S(1)}, bf16[96,1152]{1,0:T(8,128)(2,1)S(1)}, u32[]{:S(2)}, u32[]{:S(2)}) collective-permute-start(bf16[96,1152]{1,0:T(8,128)(2,1)S(1)} %pick_224.1), channel_id=1, source_target_pairs={{0,6},{1,7},{2,4},{3,5},{4,2},{5,3},{6,0},{7,1},{8,14},{9,15},{10,... | collective-permute-start | bytes 663560 | tf_op jit(solution)/shard_map/ppermute | solution.py:110
  36.7 9.2 %collective-permute-start.12 = (bf16[112,1152]{1,0:T(8,128)(2,1)S(1)}, bf16[112,1152]{1,0:T(8,128)(2,1)S(1)}, u32[]{:S(2)}, u32[]{:S(2)}) collective-permute-start(bf16[112,1152]{1,0:T(8,128)(2,1)S(1)} %get-tuple-element.22.refs_1_.refs_6_), channel_id=1, source_target_pairs={{0,6},{1,7},{2,4},{3,5},{4,2},{5,3},{6,0},{7,1},{8,14},{9,15},{10,... | collective-permute-start | bytes 774152 | tf_op jit(solution)/shard_map/ppermute | solution.py:110
  39.8 6.1 %collective-permute-start.11 = (bf16[640,1152]{1,0:T(8,128)(2,1)S(1)}, bf16[640,1152]{1,0:T(8,128)(2,1)S(1)}, u32[]{:S(2)}, u32[]{:S(2)}) collective-permute-start(bf16[640,1152]{1,0:T(8,128)(2,1)S(1)} %get-tuple-element.27), channel_id=1, source_target_pairs={{0,1},{1,0},{2,3},{3,2},{4,5},{5,4},{6,7},{7,6},{8,9},{9,8},{10,11... | collective-permute-start | bytes 4423688 | tf_op jit(solution)/shard_map/ppermute | solution.py:110
  44.1 9.1 %collective-permute-start.15 = (bf16[112,1152]{1,0:T(8,128)(2,1)S(1)}, bf16[112,1152]{1,0:T(8,128)(2,1)S(1)}, u32[]{:S(2)}, u32[]{:S(2)}) collective-permute-start(bf16[112,1152]{1,0:T(8,128)(2,1)S(1)} %get-tuple-element.28.refs_2_), channel_id=1, source_target_pairs={{0,6},{1,7},{2,4},{3,5},{4,2},{5,3},{6,0},{7,1},{8,14},{9,15},{10,... | collective-permute-start | bytes 774152 | tf_op jit(solution)/shard_map/ppermute | solution.py:110
  47.1 17.2 %collective-permute-start.16 = (bf16[320,1152]{1,0:T(8,128)(2,1)S(1)}, bf16[320,1152]{1,0:T(8,128)(2,1)S(1)}, u32[]{:S(2)}, u32[]{:S(2)}) collective-permute-start(bf16[320,1152]{1,0:T(8,128)(2,1)S(1)} %to_pair.1.refs_2_), channel_id=1, source_target_pairs={{0,2},{1,3},{2,0},{3,1},{4,6},{5,7},{6,4},{7,5},{8,10},{9,11},{10,... | collective-permute-start | bytes 2211848 | tf_op jit(solution)/shard_map/ppermute | solution.py:110
  47.2 11.5 %collective-permute-start.13 = (bf16[112,1152]{1,0:T(8,128)(2,1)S(1)}, bf16[112,1152]{1,0:T(8,128)(2,1)S(1)}, u32[]{:S(2)}, u32[]{:S(2)}) collective-permute-start(bf16[112,1152]{1,0:T(8,128)(2,1)S(1)} %to_prev_0.1.refs_1_.refs_2_), channel_id=1, source_target_pairs={{0,248},{1,249},{2,250},{3,251},{4,252},{5,253},{6,254},{7,255},{8... | collective-permute-start | bytes 774152 | tf_op jit(solution)/shard_map/ppermute | solution.py:110
  49.6 6.8 %collective-permute-start.14 = (bf16[96,1152]{1,0:T(8,128)(2,1)S(1)}, bf16[96,1152]{1,0:T(8,128)(2,1)S(1)}, u32[]{:S(2)}, u32[]{:S(2)}) collective-permute-start(bf16[96,1152]{1,0:T(8,128)(2,1)S(1)} %gate_g_2.1), channel_id=1, source_target_pairs={{0,6},{1,7},{2,4},{3,5},{4,2},{5,3},{6,0},{7,1},{8,14},{9,15},{10,... | collective-permute-start | bytes 663560 | tf_op jit(solution)/shard_map/ppermute | solution.py:110
  53.3 7.0 %collective-permute-start.18 = (bf16[112,1152]{1,0:T(8,128)(2,1)S(1)}, bf16[112,1152]{1,0:T(8,128)(2,1)S(1)}, u32[]{:S(2)}, u32[]{:S(2)}) collective-permute-start(bf16[112,1152]{1,0:T(8,128)(2,1)S(1)} %to_prev_112.1.refs_2_), channel_id=1, source_target_pairs={{0,248},{1,249},{2,250},{3,251},{4,252},{5,253},{6,254},{7,255},{8... | collective-permute-start | bytes 774152 | tf_op jit(solution)/shard_map/ppermute | solution.py:110
  56.5 9.1 %collective-permute-start.17 = (bf16[96,1152]{1,0:T(8,128)(2,1)S(1)}, bf16[96,1152]{1,0:T(8,128)(2,1)S(1)}, u32[]{:S(2)}, u32[]{:S(2)}) collective-permute-start(bf16[96,1152]{1,0:T(8,128)(2,1)S(1)} %to_prev_224.1.refs_1_), channel_id=1, source_target_pairs={{0,248},{1,249},{2,250},{3,251},{4,252},{5,253},{6,254},{7,255},{8... | collective-permute-start | bytes 663560 | tf_op jit(solution)/shard_map/ppermute | solution.py:110

commit v4 on v3

--- a/solution.py
+++ b/solution.py
@@ -13,11 +13,11 @@
 PICK_US = 6
 SEND_US = (8, 8, 0)
 GATE_US = 0
-END_US = 0
 GATE_X = (16, 0)
-BACK_US = 14
+BACK_US = 6
 LAST_US = 16
 PAIR_US = 0
+FIRST_US = 8
 VMEM = pl.BlockSpec(memory_space=pltpu.VMEM)
 SMEM = pl.BlockSpec(memory_space=pltpu.SMEM)
 ANY = pl.BlockSpec(memory_space=pl.ANY)
@@ -44,7 +44,8 @@
 
 def pieces(n, cuts):
     size = -(-n // (cuts * 16)) * 16
-    return [slice(a, min(a + size, n)) for a in range(0, n, size)]
+    stops = [n - size * i for i in range(cuts) if n - size * i > 0][::-1]
+    return [slice(a, b) for a, b in zip([0] + stops, stops)]
 
 
 def nt(a, b):
@@ -85,14 +86,6 @@
 
 def is_upper():
     return lax.rem(lax.axis_index("blk"), 2) == 1
-
-
-def k_positives(own, other, image, out, kept):
-    n = own.shape[0]
-    kept[...] = image[...]
-    out[...] = jnp.zeros(out.shape, out.dtype)
-    out[0:1, :n] = own[...].reshape(1, n)
-    out[0:1, n:] = other[...].reshape(1, n)
 
 
 def tile_of(scale, bias, texts, images, pos=None):
@@ -144,39 +137,54 @@
         picked.append(t)
         text_m.append(move(t, "mirror"))
         if i == 0:
-            pos_own, kept = call(
-                k_positives, "positives", [((8, 2 * n), jnp.int32), ((n, d), BF)], [positive, pos_c, image], after=[t]
+
+            def k_own(pos, pos_c, image, image_c, *refs):
+                own, (out, images, texts) = refs[:cuts], refs[cuts:]
+                out[...] = jnp.zeros(out.shape, out.dtype)
+                out[0:1, :n] = pos[...].reshape(1, n)
+                out[0:1, n:] = pos_c[...].reshape(1, n)
+                images[blocks[1], :] = image_c[...]
+                images[blocks[3], :] = image[...]
+                for p, ref in zip(parts, own):
+                    texts[p, :] = ref[...]
+
+            pos_own, images, texts = call(
+                k_own, "own_blocks", [((8, 2 * n), jnp.int32), ((m, d), BF), ((3 * n, d), BF)],
+                [positive, pos_c, image, image_c, *cut], after=[t],
             )
             pos_n = [move(pos_own, "pair")]
             picked.append(pos_own)
         if i == cuts - 2:
-            image_n = gate(image_n, "gate_pair", [t], us=PAIR_US)
+            text_m[0] = gate(text_m[0], "gate_first", [t], us=FIRST_US)
+            image_n = gate(image_n, "gate_pair", [t, text_m[0]], us=PAIR_US)
             image_nc = move(image_n, "core")
             picked.append(image_n)
 
-    def k_tiles(scale, bias, i0, i_n, i_c, i_nc, pos_own, pos_n, *refs):
-        own, xs = refs[:cuts], refs[cuts : 2 * cuts]
-        images, texts, tiles, pos = refs[2 * cuts :]
-        for rows, ref in zip(blocks, (i_nc, i_c, i_n, i0)):
-            images[rows, :] = ref[...]
+    def k_tiles(scale, bias, i_n, i_nc, pos_own, pos_n, *refs):
+        xs, (_, _, images, texts, tiles, pos) = refs[:cuts], refs[cuts:]
+        images[blocks[0], :] = i_nc[...]
+        images[blocks[2], :] = i_n[...]
         for j, ref, at in ((0, pos_n, n), (1, pos_own, n), (2, pos_n, 0), (3, pos_own, 0)):
             pos[0:1, blocks[j]] = ref[0:1, at : at + n]
-        for k, group in enumerate((own, xs)):
-            for p, ref in zip(parts, group):
-                texts[k * n + p.start : k * n + p.stop, :] = ref[...]
+        for p, ref in zip(parts, xs):
+            texts[n + p.start : n + p.stop, :] = ref[...]
         tiles[:n, :] = tile_of(scale, bias, texts[:n, :], images[...], pos[0:1, :])
         tiles[n:base, :] = tile_of(scale, bias, texts[n:base, :], images[...])
 
     images, texts, tiles, _ = call(
         k_tiles, "tiles", [((m, d), BF), ((3 * n, d), BF), ((3 * n, m), BF), ((8, m), jnp.int32)],
-        [kept, image_n, image_c, image_nc, pos_own, *pos_n, *cut, *text_x], sc,
+        [image_n, image_nc, pos_own, *pos_n, *text_x, images, texts], sc,
+        aliases={4 + cuts: 0, 5 + cuts: 1},
     )
 
     for i in range(early):
         text_m[i] = gate(text_m[i], f"gate_m_{i}", [tiles, *text_m[:i]], us=GATE_US)
 
-    def k_next_grads(tiles, images, out):
-        out[...] = nn(tiles[n:base, :], images[...])
+    def k_next_first(tiles, images, out):
+        out[...] = nn(tiles[n : n + parts[0].stop, :], images[...])
+
+    def k_next_rest(tiles, images, out):
+        out[...] = nn(tiles[n + parts[0].stop : base, :], images[...])
 
     def k_mirror_first(scale, bias, images, *refs):
         got, (_, _, texts, tiles, grad) = refs[:early], refs[early:]
@@ -197,10 +205,10 @@
         for p, t in zip(parts[early:], got):
             texts[base + p.start : base + p.stop, :] = t[...]
         tiles[done:, :] = tile_of(scale, bias, texts[done:, :], images[...])
-        to_core[...] = tn(tiles[:, : 2 * n], texts[...]).astype(BF)
+        to_core[...] = tn(tiles[:, :n], texts[...]).astype(BF)
 
     texts, tiles, to_core = call(
-        k_last, "mirror_last", [((3 * n, d), BF), ((3 * n, m), BF), ((2 * n, d), BF)],
+        k_last, "mirror_last", [((3 * n, d), BF), ((3 * n, m), BF), ((n, d), BF)],
         [images, *text_m[early:], texts, tiles], sc, aliases={1 + LATE: 0, 2 + LATE: 1}, after=grad_m[-1:],
     )
     got_core = move(to_core, "core")
@@ -212,11 +220,11 @@
 
     grad_m += call(k_rest_grads, "mirror_rest_grads", [((s, d), BF) for s in size[1:]], [tiles, images])
     back_m.append(move(grad_m[1], "mirror"))
-    (gx,) = call(k_next_grads, "next_text_grads", [((n, d), F32)], [tiles, images], after=[grad_m[1]])
+    (gx,) = call(k_next_first, "next_text_first", [((size[0], d), F32)], [tiles, images], after=[grad_m[1]])
 
     def k_pair(tiles, texts, got_core, out):
         g = tn(tiles[:, 2 * n : 3 * n], texts[...])
-        out[...] = (g + got_core[:n, :].astype(F32)).astype(BF)
+        out[...] = (g + got_core[...].astype(F32)).astype(BF)
 
     back_m[0] = gate(back_m[0], "gate_back_0", [gx], us=BACK_US)
     (send_n,) = call(k_pair, "to_pair", [((n, d), BF)], [tiles, texts, got_core], after=[back_m[0]])
@@ -224,10 +232,14 @@
     def k_own_grads(tiles, images, out):
         out[...] = nn(tiles[:n, :], images[...])
 
-    def k_own_images(tiles, texts, got_core, out):
+    def k_core_images(tiles, texts, out):
+        skip = n % 128
+        out[...] = tn(tiles[:, n - skip : 2 * n], texts[...])[skip:, :].astype(BF)
+
+    def k_own_images(tiles, texts, got_c, out):
         skip = n % 128
         g = tn(tiles[:, 3 * n - skip :], texts[...])[skip:, :]
-        out[...] = g + got_core[n:, :].astype(F32)
+        out[...] = g + got_c[...].astype(F32)
 
     back_x = []
     sent = []
@@ -235,7 +247,8 @@
 
         def k_send(gx, back, out, p=p):
             b = jnp.where(is_upper(), back[...].astype(F32), 0.0)
-            out[...] = (gx[p, :] + b).astype(BF)
+            at = p.start if p.start == 0 else p.start - parts[0].stop
+            out[...] = (gx[at : at + p.stop - p.start, :] + b).astype(BF)
 
         after = sent[-1:] or [send_n]
         (t,) = call(k_send, f"to_prev_{p.start}", [((s, d), BF)], [gx, back_m[i]], after=after, us=SEND_US[i])
@@ -244,47 +257,54 @@
         if i == 0:
             for j in range(2, cuts):
                 back_m.append(move(gate(grad_m[j], f"gate_g_{j}", [t]), "mirror"))
+            (gx,) = call(k_next_rest, "next_text_rest", [((n - size[0], d), F32)], [tiles, images], after=[t])
+        if i == 1:
+            (to_c,) = call(k_core_images, "core_images", [((n, d), BF)], [tiles, texts], after=[t])
+            got_c = move(to_c, "core")
         if i == 2:
             back_x[0] = gate(back_x[0], "gate_x_0", [t], us=GATE_X[0])
             (gt,) = call(k_own_grads, "own_text_grads", [((n, d), F32)], [tiles, images], after=back_x[:1])
-            (gi_own,) = call(k_own_images, "own_images", [((n, d), F32)], [tiles, texts, got_core], after=[gt])
-
-    back_x[1] = gate(back_x[1], "gate_x_1", [], us=GATE_X[1])
-
-    def k_end_images(gi, got_n, out, token):
-        out[...] = gi[...] + got_n[...].astype(F32)
-        token[...] = jnp.zeros(token.shape, F32)
-
-    grad_images, token = call(k_end_images, "end_images", [((n, d), F32), ((8, 128), F32)], [gi_own, got_n])
-
-    grad_texts = None
-    for name, a, b in (("end_texts_first", 0, cuts - 1), ("end_texts_last", cuts - 1, cuts)):
+            (gi_own,) = call(k_own_images, "own_images", [((n, d), F32)], [tiles, texts, got_c], after=[gt])
+
+    back_x[1] = gate(back_x[1], "gate_x_1", [gi_own], us=GATE_X[1])
+
+    def write_texts(name, a, b, old, after):
         at, rows = parts[a].start, parts[b - 1].stop - parts[a].start
 
-        def k_end_texts(gt, *refs, a=a, b=b, at=at, rows=rows):
-            ms, xs, (out, block, sem) = refs[: b - a], refs[b - a : 2 * (b - a)], refs[-3:]
+        def k_end_texts(gt, *refs):
+            ms, xs, (out, *token, block, sem) = refs[: b - a], refs[b - a : 2 * (b - a)], refs[-3 if old else -4 :]
             up = is_upper()
             for p, m_ref, x_ref in zip(parts[a:b], ms, xs):
                 g = gt[p, :] + jnp.where(up, 0.0, m_ref[...].astype(F32)) + x_ref[...].astype(F32)
                 block[p.start - at : p.stop - at, :] = g
             copy = pltpu.make_async_copy(block, out.at[pl.ds(at, rows), :], sem)
             copy.start()
+            for ref in token:
+                ref[...] = jnp.zeros(ref.shape, F32)
             copy.wait()
 
         ins = [gt, *back_m[a:b], *back_x[a:b]]
-        old = [] if grad_texts is None else [grad_texts]
-        after = [token] if old else []
-        grad_texts = pl.pallas_call(
+        return pl.pallas_call(
             k_end_texts,
-            out_shape=jax.ShapeDtypeStruct((n, d), F32),
+            out_shape=[jax.ShapeDtypeStruct((n, d), F32), jax.ShapeDtypeStruct((8, 128), F32)][: 1 if old else 2],
             in_specs=[VMEM] * len(ins) + [HBM] * len(old) + [ANY] * len(after),
-            out_specs=HBM,
+            out_specs=[HBM, VMEM][: 1 if old else 2],
             input_output_aliases={len(ins): 0} if old else {},
             scratch_shapes=[pltpu.VMEM((rows, d), F32), pltpu.SemaphoreType.DMA],
             compiler_params=pltpu.CompilerParams(vmem_limit_bytes=16 * 2**20),
-            cost_estimate=pl.CostEstimate(flops=0 if old else int(END_US * 1e9), bytes_accessed=0, transcendentals=0),
+            cost_estimate=pl.CostEstimate(flops=0, bytes_accessed=0, transcendentals=0),
             name=name,
         )(*ins, *old, *after)
+
+    def k_end_images(gi, got_n, out, token):
+        out[...] = gi[...] + got_n[...].astype(F32)
+        token[...] = jnp.zeros(token.shape, F32)
+
+    grad_texts, token = write_texts("end_texts_first", 0, cuts - 1, [], [])
+    grad_images, token = call(
+        k_end_images, "end_images", [((n, d), F32), ((8, 128), F32)], [gi_own, got_n], after=[token]
+    )
+    (grad_texts,) = write_texts("end_texts_last", cuts - 1, cuts, [grad_texts], [token])
     return grad_images, grad_texts
 
 

time: 67.7 us -> 65.7 us (0.970)
  the two profiles are of different devices: /device:TPU:1 before, /device:TPU:102 now
where the time goes in v4:
time: 65.7 us; the launch traced here: 65.6 us
  waiting for transfers between devices  22.5 us (34%)
  starting transfers between devices  22.4 us (34%)
  Pallas kernels  17.2 us (26%)
  between operations  2.38 us (4%)
  local copies, waits for them, and re-layouts  1.12 us (2%)
    ppermute x20, waiting for transfers between devices, local(): move = lambda v, name: lax.ppermute(v, AXES, way[name])  22.5 us
    ppermute x20, starting transfers between devices, local(): move = lambda v, name: lax.ppermute(v, AXES, way[name])  22.4 us
    pallas_call x30, Pallas kernels, call(): pl.pallas_call(run, out_shape=shapes, in_specs=[SMEM] * ns + [VMEM] * ni...  15.2 us
    pallas_call x2, Pallas kernels, write_texts(): pl.pallas_call(k_end_texts, out_shape=[jax.ShapeDtypeStruct((n, d), F32),...  2.03 us
  transfers between devices with their start and end apart: 20, of which 10 were waited for; matrix products, arithmetic and copies ran while one was open for 0% of the time, Pallas kernels for 25%

profile of v4, /device:TPU:102, one launch (start us, length us, event | category | flops | bytes accessed | tf_op | source)
XLA Modules:
  0.0 65.6 jit_solution(1555526820888613734)
XLA Ops:
  0.7 1.1 %copy-done = bf16[320,1152]{1,0:T(8,128)(2,1)S(1)} copy-done((bf16[320,1152]{1,0:T(8,128)(2,1)S(1)}, bf16[320,1152]{1,0:T(8,128)(2,1)}, u32[]{:S(2)}) %copy-start) | copy-done | bytes 737304
  1.9 3.1 %collective-permute-start.4 = (bf16[96,1152]{1,0:T(8,128)(2,1)S(1)}, bf16[96,1152]{1,0:T(8,128)(2,1)S(1)}, u32[]{:S(2)}, u32[]{:S(2)}) collective-permute-start(bf16[96,1152]{1,0:T(8,128)(2,1)S(1)} %cut_0.1.refs_1_.refs_0_.refs_4_), channel_id=1, source_target_pairs={{0,8},{1,9},{2,10},{3,11},{4,12},{5,13},{6,14},{7,15},{8,16},{9,17... | collective-permute-start | bytes 663560 | tf_op jit(solution)/shard_map/ppermute | solution.py:103
  5.2 1.6 %collective-permute-start = (bf16[320,1152]{1,0:T(8,128)(2,1)}, bf16[320,1152]{1,0:T(8,128)(2,1)S(1)}, u32[]{:S(2)}, u32[]{:S(2)}) collective-permute-start(bf16[320,1152]{1,0:T(8,128)(2,1)} %refs_2_.1), channel_id=1, source_target_pairs={{0,2},{1,3},{2,0},{3,1},{4,6},{5,7},{6,4},{7,5},{8,10},{9,11},{10,... | collective-permute-start | bytes 2211848 | tf_op jit(solution)/shard_map/ppermute | solution.py:103
  6.8 1.6 %collective-permute-start.1 = (bf16[112,1152]{1,0:T(8,128)(2,1)S(1)}, bf16[112,1152]{1,0:T(8,128)(2,1)S(1)}, u32[]{:S(2)}, u32[]{:S(2)}) collective-permute-start(bf16[112,1152]{1,0:T(8,128)(2,1)S(1)} %cut_96.1.refs_1_.refs_5_.refs_0_), channel_id=1, source_target_pairs={{0,8},{1,9},{2,10},{3,11},{4,12},{5,13},{6,14},{7,15},{8,16},{9,17... | collective-permute-start | bytes 774152 | tf_op jit(solution)/shard_map/ppermute | solution.py:103
  8.4 1.6 %collective-permute-start.8 = (bf16[112,1152]{1,0:T(8,128)(2,1)S(1)}, bf16[112,1152]{1,0:T(8,128)(2,1)S(1)}, u32[]{:S(2)}, u32[]{:S(2)}) collective-permute-start(bf16[112,1152]{1,0:T(8,128)(2,1)S(1)} %cut_208.1.refs_6_.refs_0_), channel_id=1, source_target_pairs={{0,8},{1,9},{2,10},{3,11},{4,12},{5,13},{6,14},{7,15},{8,16},{9,17... | collective-permute-start | bytes 774152 | tf_op jit(solution)/shard_map/ppermute | solution.py:103
  10.0 0.7 %collective-permute-done.4.refs_1_.refs_6_ = bf16[96,1152]{1,0:T(8,128)(2,1)S(1)} collective-permute-done((bf16[96,1152]{1,0:T(8,128)(2,1)S(1)}, bf16[96,1152]{1,0:T(8,128)(2,1)S(1)}, u32[]{:S(2)}, u32[]{:S(2)}) %collective-permute-start.4) | collective-permute-done | bytes 221216 | tf_op jit(solution)/shard_map/ppermute | solution.py:103
  10.8 3.1 %collective-permute-start.5 = (bf16[96,1152]{1,0:T(8,128)(2,1)S(1)}, bf16[96,1152]{1,0:T(8,128)(2,1)S(1)}, u32[]{:S(2)}, u32[]{:S(2)}) collective-permute-start(bf16[96,1152]{1,0:T(8,128)(2,1)S(1)} %pick_0.1.refs_7_), channel_id=1, source_target_pairs={{0,6},{1,7},{2,4},{3,5},{4,2},{5,3},{6,0},{7,1},{8,14},{9,15},{10,... | collective-permute-start | bytes 663560 | tf_op jit(solution)/shard_map/ppermute | solution.py:103
  14.3 2.0 %collective-permute-done.1.refs_1_.refs_7_ = bf16[112,1152]{1,0:T(8,128)(2,1)S(1)} collective-permute-done((bf16[112,1152]{1,0:T(8,128)(2,1)S(1)}, bf16[112,1152]{1,0:T(8,128)(2,1)S(1)}, u32[]{:S(2)}, u32[]{:S(2)}) %collective-permute-start.1) | collective-permute-done | bytes 258080 | tf_op jit(solution)/shard_map/ppermute | solution.py:103
  16.3 3.1 %collective-permute-start.10 = (bf16[112,1152]{1,0:T(8,128)(2,1)S(1)}, bf16[112,1152]{1,0:T(8,128)(2,1)S(1)}, u32[]{:S(2)}, u32[]{:S(2)}) collective-permute-start(bf16[112,1152]{1,0:T(8,128)(2,1)S(1)} %pick_96.1.refs_1_), channel_id=1, source_target_pairs={{0,6},{1,7},{2,4},{3,5},{4,2},{5,3},{6,0},{7,1},{8,14},{9,15},{10,... | collective-permute-start | bytes 774152 | tf_op jit(solution)/shard_map/ppermute | solution.py:103
  19.4 4.9 %collective-permute-done.refs_0_ = bf16[320,1152]{1,0:T(8,128)(2,1)S(1)} collective-permute-done((bf16[320,1152]{1,0:T(8,128)(2,1)}, bf16[320,1152]{1,0:T(8,128)(2,1)S(1)}, u32[]{:S(2)}, u32[]{:S(2)}) %collective-permute-start) | collective-permute-done | bytes 737312 | tf_op jit(solution)/shard_map/ppermute | solution.py:103
  24.6 3.1 %collective-permute-start.9 = (bf16[112,1152]{1,0:T(8,128)(2,1)S(1)}, bf16[112,1152]{1,0:T(8,128)(2,1)S(1)}, u32[]{:S(2)}, u32[]{:S(2)}) collective-permute-start(bf16[112,1152]{1,0:T(8,128)(2,1)S(1)} %pick_208.1), channel_id=1, source_target_pairs={{0,6},{1,7},{2,4},{3,5},{4,2},{5,3},{6,0},{7,1},{8,14},{9,15},{10,... | collective-permute-start | bytes 774152 | tf_op jit(solution)/shard_map/ppermute | solution.py:103
  29.0 2.5 %tiles.1 = (bf16[1280,1152]{1,0:T(8,128)(2,1)S(1)}, bf16[960,1152]{1,0:T(8,128)(2,1)S(1)}, bf16[960,1280]{1,0:T(8,128)(2,1)S(1)}, s32[8,1280]{1,0:T(8,128)}) custom-call(f32[1]{0:T(128)S(6)} %copy.39.refs_0_, f32[1]{0:T(128)S(6)} %copy.40.refs_1_, bf16[320,1152]{1,0:T(8,128)(2,1)S(1)} %gate_pair.1.refs_2_, ...), custom_call_target="tpu_custom_call", output_to_operand_aliasing={{0}: (9, {}), {1}: (10, {})} | custom-call | tf_op jit(solution)/shard_map/tiles/pallas_call | solution.py:70
  31.6 1.8 %mirror_first.1 = (bf16[960,1152]{1,0:T(8,128)(2,1)S(1)}, bf16[960,1280]{1,0:T(8,128)(2,1)S(1)}, bf16[96,1152]{1,0:T(8,128)(2,1)S(1)}) custom-call(f32[1]{0:T(128)S(6)} %copy.39.refs_0_, f32[1]{0:T(128)S(6)} %copy.40.refs_1_, bf16[1280,1152]{1,0:T(8,128)(2,1)S(1)} %get-tuple-element.23.refs_2_.refs_1_, ...), custom_call_target="tpu_custom_call", output_to_operand_aliasing={{0}: (5, {}), {1}: (6, {})} | custom-call | tf_op jit(solution)/shard_map/mirror_first/pallas_call | solution.py:70
  33.3 0.8 %collective-permute-start.11 = (bf16[96,1152]{1,0:T(8,128)(2,1)S(1)}, bf16[96,1152]{1,0:T(8,128)(2,1)S(1)}, u32[]{:S(2)}, u32[]{:S(2)}) collective-permute-start(bf16[96,1152]{1,0:T(8,128)(2,1)S(1)} %get-tuple-element.26.refs_1_.refs_6_), channel_id=1, source_target_pairs={{0,6},{1,7},{2,4},{3,5},{4,2},{5,3},{6,0},{7,1},{8,14},{9,15},{10,... | collective-permute-start | bytes 663560 | tf_op jit(solution)/shard_map/ppermute | solution.py:103
  34.4 1.9 %mirror_last.1 = (bf16[960,1152]{1,0:T(8,128)(2,1)S(1)}, bf16[960,1280]{1,0:T(8,128)(2,1)S(1)}, bf16[320,1152]{1,0:T(8,128)(2,1)S(1)}) custom-call(f32[1]{0:T(128)S(6)} %copy.39.refs_0_, f32[1]{0:T(128)S(6)} %copy.40.refs_1_, bf16[1280,1152]{1,0:T(8,128)(2,1)S(1)} %get-tuple-element.23.refs_2_.refs_1_, ...), custom_call_target="tpu_custom_call", output_to_operand_aliasing={{0}: (4, {}), {1}: (5, {})} | custom-call | tf_op jit(solution)/shard_map/mirror_last/pallas_call | solution.py:70
  36.4 0.9 %mirror_rest_grads.1 = (bf16[112,1152]{1,0:T(8,128)(2,1)S(1)}, bf16[112,1152]{1,0:T(8,128)(2,1)S(1)}) custom-call(bf16[960,1280]{1,0:T(8,128)(2,1)S(1)} %get-tuple-element.29.refs_0_, bf16[1280,1152]{1,0:T(8,128)(2,1)S(1)} %get-tuple-element.23.refs_2_.refs_1_), custom_call_target="tpu_custom_call" | custom-call | tf_op jit(solution)/shard_map/mirror_rest_grads/pallas_call | solution.py:70
  37.3 3.0 %collective-permute-start.13 = (bf16[112,1152]{1,0:T(8,128)(2,1)S(1)}, bf16[112,1152]{1,0:T(8,128)(2,1)S(1)}, u32[]{:S(2)}, u32[]{:S(2)}) collective-permute-start(bf16[112,1152]{1,0:T(8,128)(2,1)S(1)} %get-tuple-element.31.refs_2_), channel_id=1, source_target_pairs={{0,6},{1,7},{2,4},{3,5},{4,2},{5,3},{6,0},{7,1},{8,14},{9,15},{10,... | collective-permute-start | bytes 774152 | tf_op jit(solution)/shard_map/ppermute | solution.py:103
  40.3 0.6 next_text_first.1.refs_1_.refs_0_
  40.9 1.7 %collective-permute-done.11.refs_0_ = bf16[96,1152]{1,0:T(8,128)(2,1)S(1)} collective-permute-done((bf16[96,1152]{1,0:T(8,128)(2,1)S(1)}, bf16[96,1152]{1,0:T(8,128)(2,1)S(1)}, u32[]{:S(2)}, u32[]{:S(2)}) %collective-permute-start.11) | collective-permute-done | bytes 221216 | tf_op jit(solution)/shard_map/ppermute | solution.py:103
  42.6 1.1 %to_pair.1.refs_2_ = bf16[320,1152]{1,0:T(8,128)(2,1)S(1)} custom-call(bf16[960,1280]{1,0:T(8,128)(2,1)S(1)} %get-tuple-element.29.refs_0_, bf16[960,1152]{1,0:T(8,128)(2,1)S(1)} %get-tuple-element.30.refs_1_, bf16[320,1152]{1,0:T(8,128)(2,1)S(1)} %collective-permute-done.12.refs_2_, bf16[96,1152]{1,0:T(8,128)(2,1)S(1)} %gate_back_0.1.refs_3_.refs_1_.refs_0_), custom_call_target="tpu_custom_call" | custom-call | tf_op jit(solution)/shard_map/to_pair/pallas_call | solution.py:70
  44.0 0.9 %next_text_rest.1.refs_0_ = f32[224,1152]{1,0:T(8,128)S(1)} custom-call(bf16[960,1280]{1,0:T(8,128)(2,1)S(1)} %get-tuple-element.29.refs_0_, bf16[1280,1152]{1,0:T(8,128)(2,1)S(1)} %get-tuple-element.23.refs_2_.refs_1_, bf16[96,1152]{1,0:T(8,128)(2,1)S(1)} %to_prev_0.1.refs_2_.refs_1_), custom_call_target="tpu_custom_call" | custom-call | tf_op jit(solution)/shard_map/next_text_rest/pallas_call | solution.py:70
  44.9 0.3 collective-permute-start.16
  45.2 2.6 %collective-permute-done.13.refs_1_ = bf16[112,1152]{1,0:T(8,128)(2,1)S(1)} collective-permute-done((bf16[112,1152]{1,0:T(8,128)(2,1)S(1)}, bf16[112,1152]{1,0:T(8,128)(2,1)S(1)}, u32[]{:S(2)}, u32[]{:S(2)}) %collective-permute-start.13) | collective-permute-done | bytes 258080 | tf_op jit(solution)/shard_map/ppermute | solution.py:103
  48.0 1.2 %core_images.1 = bf16[320,1152]{1,0:T(8,128)(2,1)S(1)} custom-call(bf16[960,1280]{1,0:T(8,128)(2,1)S(1)} %get-tuple-element.29.refs_0_, bf16[960,1152]{1,0:T(8,128)(2,1)S(1)} %get-tuple-element.30.refs_1_, bf16[112,1152]{1,0:T(8,128)(2,1)S(1)} %to_prev_96.1.refs_2_), custom_call_target="tpu_custom_call" | custom-call | tf_op jit(solution)/shard_map/core_images/pallas_call | solution.py:70
  49.3 3.9 %collective-permute-done.16.refs_1_.refs_0_ = bf16[112,1152]{1,0:T(8,128)(2,1)S(1)} collective-permute-done((bf16[112,1152]{1,0:T(8,128)(2,1)S(1)}, bf16[112,1152]{1,0:T(8,128)(2,1)S(1)}, u32[]{:S(2)}, u32[]{:S(2)}) %collective-permute-start.16) | collective-permute-done | bytes 258080 | tf_op jit(solution)/shard_map/ppermute | solution.py:103
  53.4 1.2 %own_text_grads.1.refs_3_.gt = f32[320,1152]{1,0:T(8,128)S(1)} custom-call(bf16[960,1280]{1,0:T(8,128)(2,1)S(1)} %get-tuple-element.29.refs_0_, bf16[1280,1152]{1,0:T(8,128)(2,1)S(1)} %get-tuple-element.23.refs_2_.refs_1_, bf16[96,1152]{1,0:T(8,128)(2,1)S(1)} %gate_x_0.1.refs_2_), custom_call_target="tpu_custom_call" | custom-call | tf_op jit(solution)/shard_map/own_text_grads/pallas_call | solution.py:70
  54.7 1.2 %own_images.1.refs_1_.refs_0_ = f32[320,1152]{1,0:T(8,128)S(1)} custom-call(bf16[960,1280]{1,0:T(8,128)(2,1)S(1)} %get-tuple-element.29.refs_0_, bf16[960,1152]{1,0:T(8,128)(2,1)S(1)} %get-tuple-element.30.refs_1_, bf16[320,1152]{1,0:T(8,128)(2,1)S(1)} %collective-permute-done.14.refs_2_, f32[320,1152]{1,0:T(8,128)S(1)} %own_text_grads.1.refs_3_.gt), custom_call_target="tpu_custom_call" | custom-call | tf_op jit(solution)/shard_map/own_images/pallas_call | solution.py:70
  55.9 4.2 %collective-permute-done.18.refs_0_ = bf16[112,1152]{1,0:T(8,128)(2,1)S(1)} collective-permute-done((bf16[112,1152]{1,0:T(8,128)(2,1)S(1)}, bf16[112,1152]{1,0:T(8,128)(2,1)S(1)}, u32[]{:S(2)}, u32[]{:S(2)}) %collective-permute-start.18) | collective-permute-done | bytes 258080 | tf_op jit(solution)/shard_map/ppermute | solution.py:103
  60.1 1.1 %end_texts_first.1 = (f32[320,1152]{1,0:T(8,128)}, f32[8,128]{1,0:T(8,128)S(1)}) custom-call(f32[320,1152]{1,0:T(8,128)S(1)} %own_text_grads.1.refs_3_.gt, bf16[96,1152]{1,0:T(8,128)(2,1)S(1)} %gate_back_0.1.refs_3_.refs_1_.refs_0_, bf16[112,1152]{1,0:T(8,128)(2,1)S(1)} %collective-permute-done.13.refs_1_, bf16[96,1152]{1,0:T(8,128)(2,1)S(1)} %gate_x_0.1.refs_2_, ...), custom_call_target="tpu_custom_call" | custom-call | tf_op jit(solution)/shard_map/end_texts_first/pallas_call | solution.py:287
  61.3 1.3 %end_images.1 = (f32[320,1152]{1,0:T(8,128)}, f32[8,128]{1,0:T(8,128)S(1)}) custom-call(f32[320,1152]{1,0:T(8,128)S(1)} %own_images.1.refs_1_.refs_0_, bf16[320,1152]{1,0:T(8,128)(2,1)S(1)} %collective-permute-done.17.refs_1_, f32[8,128]{1,0:T(8,128)S(1)} %get-tuple-element.34.refs_2_), custom_call_target="tpu_custom_call" | custom-call | tf_op jit(solution)/shard_map/end_images/pallas_call | solution.py:70
  62.5 2.0 %collective-permute-done.19.refs_1_ = bf16[112,1152]{1,0:T(8,128)(2,1)S(1)} collective-permute-done((bf16[112,1152]{1,0:T(8,128)(2,1)S(1)}, bf16[112,1152]{1,0:T(8,128)(2,1)S(1)}, u32[]{:S(2)}, u32[]{:S(2)}) %collective-permute-start.19) | collective-permute-done | bytes 258080 | tf_op jit(solution)/shard_map/ppermute | solution.py:103
  64.5 0.9 %end_texts_last.1 = f32[320,1152]{1,0:T(8,128)} custom-call(f32[320,1152]{1,0:T(8,128)S(1)} %own_text_grads.1.refs_3_.gt, bf16[112,1152]{1,0:T(8,128)(2,1)S(1)} %collective-permute-done.16.refs_1_.refs_0_, bf16[112,1152]{1,0:T(8,128)(2,1)S(1)} %collective-permute-done.19.refs_1_, ...), custom_call_target="tpu_custom_call", output_to_operand_aliasing={{}: (3, {})} | custom-call | tf_op jit(solution)/shard_map/end_texts_last/pallas_call | solution.py:287
  (46 shorter events, 2.1 us)
Async XLA Ops:
  0.6 10.1 %collective-permute-start.3 = (bf16[320,1152]{1,0:T(8,128)(2,1)}, bf16[320,1152]{1,0:T(8,128)(2,1)S(1)}, u32[]{:S(2)}, u32[]{:S(2)}) collective-permute-start(bf16[320,1152]{1,0:T(8,128)(2,1)} %refs_2_.1), channel_id=1, source_target_pairs={{0,1},{1,0},{2,3},{3,2},{4,5},{5,4},{6,7},{7,6},{8,9},{9,8},{10,11... | collective-permute-start | bytes 2211848 | tf_op jit(solution)/shard_map/ppermute | solution.py:103
  0.7 1.1 %copy-start = (bf16[320,1152]{1,0:T(8,128)(2,1)S(1)}, bf16[320,1152]{1,0:T(8,128)(2,1)}, u32[]{:S(2)}) copy-start(bf16[320,1152]{1,0:T(8,128)(2,1)} %refs_0_.9) | copy-start | bytes 2211844
  1.9 8.9 %collective-permute-start.4 = (bf16[96,1152]{1,0:T(8,128)(2,1)S(1)}, bf16[96,1152]{1,0:T(8,128)(2,1)S(1)}, u32[]{:S(2)}, u32[]{:S(2)}) collective-permute-start(bf16[96,1152]{1,0:T(8,128)(2,1)S(1)} %cut_0.1.refs_1_.refs_0_.refs_4_), channel_id=1, source_target_pairs={{0,8},{1,9},{2,10},{3,11},{4,12},{5,13},{6,14},{7,15},{8,16},{9,17... | collective-permute-start | bytes 663560 | tf_op jit(solution)/shard_map/ppermute | solution.py:103
  5.0 3.4 %collective-permute-start.2 = (s32[320]{0:T(512)}, s32[320]{0:T(512)S(1)}, u32[]{:S(2)}, u32[]{:S(2)}) collective-permute-start(s32[320]{0:T(512)} %refs_0_.10), channel_id=1, source_target_pairs={{0,1},{1,0},{2,3},{3,2},{4,5},{5,4},{6,7},{7,6},{8,9},{9,8},{10,11... | collective-permute-start | bytes 3848 | tf_op jit(solution)/shard_map/ppermute | solution.py:103
  5.2 19.1 %collective-permute-start = (bf16[320,1152]{1,0:T(8,128)(2,1)}, bf16[320,1152]{1,0:T(8,128)(2,1)S(1)}, u32[]{:S(2)}, u32[]{:S(2)}) collective-permute-start(bf16[320,1152]{1,0:T(8,128)(2,1)} %refs_2_.1), channel_id=1, source_target_pairs={{0,2},{1,3},{2,0},{3,1},{4,6},{5,7},{6,4},{7,5},{8,10},{9,11},{10,... | collective-permute-start | bytes 2211848 | tf_op jit(solution)/shard_map/ppermute | solution.py:103
  6.8 9.5 %collective-permute-start.1 = (bf16[112,1152]{1,0:T(8,128)(2,1)S(1)}, bf16[112,1152]{1,0:T(8,128)(2,1)S(1)}, u32[]{:S(2)}, u32[]{:S(2)}) collective-permute-start(bf16[112,1152]{1,0:T(8,128)(2,1)S(1)} %cut_96.1.refs_1_.refs_5_.refs_0_), channel_id=1, source_target_pairs={{0,8},{1,9},{2,10},{3,11},{4,12},{5,13},{6,14},{7,15},{8,16},{9,17... | collective-permute-start | bytes 774152 | tf_op jit(solution)/shard_map/ppermute | solution.py:103
  8.4 5.5 %copy-start.1 = (bf16[320,1152]{1,0:T(8,128)(2,1)S(1)}, bf16[320,1152]{1,0:T(8,128)(2,1)}, u32[]{:S(2)}) copy-start(bf16[320,1152]{1,0:T(8,128)(2,1)} %refs_2_.1) | copy-start | bytes 2211844
  8.4 5.5 %copy-start.2 = (s32[320]{0:T(512)S(1)}, s32[320]{0:T(512)}, u32[]{:S(2)}) copy-start(s32[320]{0:T(512)} %refs_0_.10) | copy-start | bytes 3844
  8.4 15.9 %collective-permute-start.8 = (bf16[112,1152]{1,0:T(8,128)(2,1)S(1)}, bf16[112,1152]{1,0:T(8,128)(2,1)S(1)}, u32[]{:S(2)}, u32[]{:S(2)}) collective-permute-start(bf16[112,1152]{1,0:T(8,128)(2,1)S(1)} %cut_208.1.refs_6_.refs_0_), channel_id=1, source_target_pairs={{0,8},{1,9},{2,10},{3,11},{4,12},{5,13},{6,14},{7,15},{8,16},{9,17... | collective-permute-start | bytes 774152 | tf_op jit(solution)/shard_map/ppermute | solution.py:103
  10.8 8.6 %collective-permute-start.5 = (bf16[96,1152]{1,0:T(8,128)(2,1)S(1)}, bf16[96,1152]{1,0:T(8,128)(2,1)S(1)}, u32[]{:S(2)}, u32[]{:S(2)}) collective-permute-start(bf16[96,1152]{1,0:T(8,128)(2,1)S(1)} %pick_0.1.refs_7_), channel_id=1, source_target_pairs={{0,6},{1,7},{2,4},{3,5},{4,2},{5,3},{6,0},{7,1},{8,14},{9,15},{10,... | collective-permute-start | bytes 663560 | tf_op jit(solution)/shard_map/ppermute | solution.py:103
  14.0 10.5 %collective-permute-start.7 = (s32[8,640]{1,0:T(8,128)S(1)}, s32[8,640]{1,0:T(8,128)S(1)}, u32[]{:S(2)}, u32[]{:S(2)}) collective-permute-start(s32[8,640]{1,0:T(8,128)S(1)} %get-tuple-element.20.refs_2_.refs_4_), channel_id=1, source_target_pairs={{0,2},{1,3},{2,0},{3,1},{4,6},{5,7},{6,4},{7,5},{8,10},{9,11},{10,... | collective-permute-start | bytes 61448 | tf_op jit(solution)/shard_map/ppermute | solution.py:103
  16.3 15.2 %collective-permute-start.10 = (bf16[112,1152]{1,0:T(8,128)(2,1)S(1)}, bf16[112,1152]{1,0:T(8,128)(2,1)S(1)}, u32[]{:S(2)}, u32[]{:S(2)}) collective-permute-start(bf16[112,1152]{1,0:T(8,128)(2,1)S(1)} %pick_96.1.refs_1_), channel_id=1, source_target_pairs={{0,6},{1,7},{2,4},{3,5},{4,2},{5,3},{6,0},{7,1},{8,14},{9,15},{10,... | collective-permute-start | bytes 774152 | tf_op jit(solution)/shard_map/ppermute | solution.py:103
  24.3 4.7 %collective-permute-start.6 = (bf16[320,1152]{1,0:T(8,128)(2,1)S(1)}, bf16[320,1152]{1,0:T(8,128)(2,1)S(1)}, u32[]{:S(2)}, u32[]{:S(2)}) collective-permute-start(bf16[320,1152]{1,0:T(8,128)(2,1)S(1)} %gate_pair.1.refs_2_), channel_id=1, source_target_pairs={{0,1},{1,0},{2,3},{3,2},{4,5},{5,4},{6,7},{7,6},{8,9},{9,8},{10,11... | collective-permute-start | bytes 2211848 | tf_op jit(solution)/shard_map/ppermute | solution.py:103
  24.6 9.8 %collective-permute-start.9 = (bf16[112,1152]{1,0:T(8,128)(2,1)S(1)}, bf16[112,1152]{1,0:T(8,128)(2,1)S(1)}, u32[]{:S(2)}, u32[]{:S(2)}) collective-permute-start(bf16[112,1152]{1,0:T(8,128)(2,1)S(1)} %pick_208.1), channel_id=1, source_target_pairs={{0,6},{1,7},{2,4},{3,5},{4,2},{5,3},{6,0},{7,1},{8,14},{9,15},{10,... | collective-permute-start | bytes 774152 | tf_op jit(solution)/shard_map/ppermute | solution.py:103
  33.3 9.3 %collective-permute-start.11 = (bf16[96,1152]{1,0:T(8,128)(2,1)S(1)}, bf16[96,1152]{1,0:T(8,128)(2,1)S(1)}, u32[]{:S(2)}, u32[]{:S(2)}) collective-permute-start(bf16[96,1152]{1,0:T(8,128)(2,1)S(1)} %get-tuple-element.26.refs_1_.refs_6_), channel_id=1, source_target_pairs={{0,6},{1,7},{2,4},{3,5},{4,2},{5,3},{6,0},{7,1},{8,14},{9,15},{10,... | collective-permute-start | bytes 663560 | tf_op jit(solution)/shard_map/ppermute | solution.py:103
  36.3 6.3 %collective-permute-start.12 = (bf16[320,1152]{1,0:T(8,128)(2,1)S(1)}, bf16[320,1152]{1,0:T(8,128)(2,1)S(1)}, u32[]{:S(2)}, u32[]{:S(2)}) collective-permute-start(bf16[320,1152]{1,0:T(8,128)(2,1)S(1)} %get-tuple-element.32), channel_id=1, source_target_pairs={{0,1},{1,0},{2,3},{3,2},{4,5},{5,4},{6,7},{7,6},{8,9},{9,8},{10,11... | collective-permute-start | bytes 2211848 | tf_op jit(solution)/shard_map/ppermute | solution.py:103
  37.3 10.5 %collective-permute-start.13 = (bf16[112,1152]{1,0:T(8,128)(2,1)S(1)}, bf16[112,1152]{1,0:T(8,128)(2,1)S(1)}, u32[]{:S(2)}, u32[]{:S(2)}) collective-permute-start(bf16[112,1152]{1,0:T(8,128)(2,1)S(1)} %get-tuple-element.31.refs_2_), channel_id=1, source_target_pairs={{0,6},{1,7},{2,4},{3,5},{4,2},{5,3},{6,0},{7,1},{8,14},{9,15},{10,... | collective-permute-start | bytes 774152 | tf_op jit(solution)/shard_map/ppermute | solution.py:103
  43.8 17.5 %collective-permute-start.17 = (bf16[320,1152]{1,0:T(8,128)(2,1)S(1)}, bf16[320,1152]{1,0:T(8,128)(2,1)S(1)}, u32[]{:S(2)}, u32[]{:S(2)}) collective-permute-start(bf16[320,1152]{1,0:T(8,128)(2,1)S(1)} %to_pair.1.refs_2_), channel_id=1, source_target_pairs={{0,2},{1,3},{2,0},{3,1},{4,6},{5,7},{6,4},{7,5},{8,10},{9,11},{10,... | collective-permute-start | bytes 2211848 | tf_op jit(solution)/shard_map/ppermute | solution.py:103
  43.9 9.5 %collective-permute-start.15 = (bf16[96,1152]{1,0:T(8,128)(2,1)S(1)}, bf16[96,1152]{1,0:T(8,128)(2,1)S(1)}, u32[]{:S(2)}, u32[]{:S(2)}) collective-permute-start(bf16[96,1152]{1,0:T(8,128)(2,1)S(1)} %to_prev_0.1.refs_2_.refs_1_), channel_id=1, source_target_pairs={{0,248},{1,249},{2,250},{3,251},{4,252},{5,253},{6,254},{7,255},{8... | collective-permute-start | bytes 663560 | tf_op jit(solution)/shard_map/ppermute | solution.py:103
  44.9 8.3 %collective-permute-start.16 = (bf16[112,1152]{1,0:T(8,128)(2,1)S(1)}, bf16[112,1152]{1,0:T(8,128)(2,1)S(1)}, u32[]{:S(2)}, u32[]{:S(2)}) collective-permute-start(bf16[112,1152]{1,0:T(8,128)(2,1)S(1)} %gate_g_2.1), channel_id=1, source_target_pairs={{0,6},{1,7},{2,4},{3,5},{4,2},{5,3},{6,0},{7,1},{8,14},{9,15},{10,... | collective-permute-start | bytes 774152 | tf_op jit(solution)/shard_map/ppermute | solution.py:103
  47.9 12.2 %collective-permute-start.18 = (bf16[112,1152]{1,0:T(8,128)(2,1)S(1)}, bf16[112,1152]{1,0:T(8,128)(2,1)S(1)}, u32[]{:S(2)}, u32[]{:S(2)}) collective-permute-start(bf16[112,1152]{1,0:T(8,128)(2,1)S(1)} %to_prev_96.1.refs_2_), channel_id=1, source_target_pairs={{0,248},{1,249},{2,250},{3,251},{4,252},{5,253},{6,254},{7,255},{8... | collective-permute-start | bytes 774152 | tf_op jit(solution)/shard_map/ppermute | solution.py:103
  49.2 5.4 %collective-permute-start.14 = (bf16[320,1152]{1,0:T(8,128)(2,1)S(1)}, bf16[320,1152]{1,0:T(8,128)(2,1)S(1)}, u32[]{:S(2)}, u32[]{:S(2)}) collective-permute-start(bf16[320,1152]{1,0:T(8,128)(2,1)S(1)} %core_images.1), channel_id=1, source_target_pairs={{0,1},{1,0},{2,3},{3,2},{4,5},{5,4},{6,7},{7,6},{8,9},{9,8},{10,11... | collective-permute-start | bytes 2211848 | tf_op jit(solution)/shard_map/ppermute | solution.py:103
  53.3 11.2 %collective-permute-start.19 = (bf16[112,1152]{1,0:T(8,128)(2,1)S(1)}, bf16[112,1152]{1,0:T(8,128)(2,1)S(1)}, u32[]{:S(2)}, u32[]{:S(2)}) collective-permute-start(bf16[112,1152]{1,0:T(8,128)(2,1)S(1)} %to_prev_208.1.refs_1_), channel_id=1, source_target_pairs={{0,248},{1,249},{2,250},{3,251},{4,252},{5,253},{6,254},{7,255},{8... | collective-permute-start | bytes 774152 | tf_op jit(solution)/shard_map/ppermute | solution.py:103

commit v5 on v4

--- a/solution.py
+++ b/solution.py
@@ -256,8 +256,9 @@
         back_x.append(move(t, "prev"))
         if i == 0:
             for j in range(2, cuts):
-                back_m.append(move(gate(grad_m[j], f"gate_g_{j}", [t]), "mirror"))
-            (gx,) = call(k_next_rest, "next_text_rest", [((n - size[0], d), F32)], [tiles, images], after=[t])
+                grad_m[j] = gate(grad_m[j], f"gate_g_{j}", [t])
+                back_m.append(move(grad_m[j], "mirror"))
+            (gx,) = call(k_next_rest, "next_text_rest", [((n - size[0], d), F32)], [tiles, images], after=grad_m[-1:])
         if i == 1:
             (to_c,) = call(k_core_images, "core_images", [((n, d), BF)], [tiles, texts], after=[t])
             got_c = move(to_c, "core")

time: 65.7 us -> 65.7 us (level)
  transfers between devices with their start and end apart: 20 -> 20, of which waited for: 10 -> 11; matrix products, arithmetic and copies ran while one was open for 0% -> 0% of each run, Pallas kernels for 25% -> 25%
where the time goes in v5:
time: 65.7 us; the launch traced here: 65.6 us
  waiting for transfers between devices  22.5 us (34%)
  starting transfers between devices  22.4 us (34%)
  Pallas kernels  17.2 us (26%)
  between operations  2.37 us (4%)
  local copies, waits for them, and re-layouts  1.12 us (2%)
    ppermute x20, waiting for transfers between devices, local(): move = lambda v, name: lax.ppermute(v, AXES, way[name])  22.5 us
    ppermute x20, starting transfers between devices, local(): move = lambda v, name: lax.ppermute(v, AXES, way[name])  22.4 us
    pallas_call x30, Pallas kernels, call(): pl.pallas_call(run, out_shape=shapes, in_specs=[SMEM] * ns + [VMEM] * ni...  15.2 us
    pallas_call x2, Pallas kernels, write_texts(): pl.pallas_call(k_end_texts, out_shape=[jax.ShapeDtypeStruct((n, d), F32),...  2.02 us
  transfers between devices with their start and end apart: 20, of which 11 were waited for; matrix products, arithmetic and copies ran while one was open for 0% of the time, Pallas kernels for 25%

profile of v5, /device:TPU:102, one launch (start us, length us, event | category | flops | bytes accessed | tf_op | source)
XLA Modules:
  0.0 65.6 jit_solution(16596529129360459777)
XLA Ops:
  0.7 1.1 %copy-done = bf16[320,1152]{1,0:T(8,128)(2,1)S(1)} copy-done((bf16[320,1152]{1,0:T(8,128)(2,1)S(1)}, bf16[320,1152]{1,0:T(8,128)(2,1)}, u32[]{:S(2)}) %copy-start) | copy-done | bytes 737304
  1.9 3.1 %collective-permute-start.4 = (bf16[96,1152]{1,0:T(8,128)(2,1)S(1)}, bf16[96,1152]{1,0:T(8,128)(2,1)S(1)}, u32[]{:S(2)}, u32[]{:S(2)}) collective-permute-start(bf16[96,1152]{1,0:T(8,128)(2,1)S(1)} %cut_0.1.refs_1_.refs_0_.refs_4_), channel_id=1, source_target_pairs={{0,8},{1,9},{2,10},{3,11},{4,12},{5,13},{6,14},{7,15},{8,16},{9,17... | collective-permute-start | bytes 663560 | tf_op jit(solution)/shard_map/ppermute | solution.py:103
  5.2 1.6 %collective-permute-start = (bf16[320,1152]{1,0:T(8,128)(2,1)}, bf16[320,1152]{1,0:T(8,128)(2,1)S(1)}, u32[]{:S(2)}, u32[]{:S(2)}) collective-permute-start(bf16[320,1152]{1,0:T(8,128)(2,1)} %refs_2_.1), channel_id=1, source_target_pairs={{0,2},{1,3},{2,0},{3,1},{4,6},{5,7},{6,4},{7,5},{8,10},{9,11},{10,... | collective-permute-start | bytes 2211848 | tf_op jit(solution)/shard_map/ppermute | solution.py:103
  6.8 1.6 %collective-permute-start.1 = (bf16[112,1152]{1,0:T(8,128)(2,1)S(1)}, bf16[112,1152]{1,0:T(8,128)(2,1)S(1)}, u32[]{:S(2)}, u32[]{:S(2)}) collective-permute-start(bf16[112,1152]{1,0:T(8,128)(2,1)S(1)} %cut_96.1.refs_1_.refs_5_.refs_0_), channel_id=1, source_target_pairs={{0,8},{1,9},{2,10},{3,11},{4,12},{5,13},{6,14},{7,15},{8,16},{9,17... | collective-permute-start | bytes 774152 | tf_op jit(solution)/shard_map/ppermute | solution.py:103
  8.4 1.6 %collective-permute-start.8 = (bf16[112,1152]{1,0:T(8,128)(2,1)S(1)}, bf16[112,1152]{1,0:T(8,128)(2,1)S(1)}, u32[]{:S(2)}, u32[]{:S(2)}) collective-permute-start(bf16[112,1152]{1,0:T(8,128)(2,1)S(1)} %cut_208.1.refs_6_.refs_0_), channel_id=1, source_target_pairs={{0,8},{1,9},{2,10},{3,11},{4,12},{5,13},{6,14},{7,15},{8,16},{9,17... | collective-permute-start | bytes 774152 | tf_op jit(solution)/shard_map/ppermute | solution.py:103
  10.0 0.7 %collective-permute-done.4.refs_1_.refs_6_ = bf16[96,1152]{1,0:T(8,128)(2,1)S(1)} collective-permute-done((bf16[96,1152]{1,0:T(8,128)(2,1)S(1)}, bf16[96,1152]{1,0:T(8,128)(2,1)S(1)}, u32[]{:S(2)}, u32[]{:S(2)}) %collective-permute-start.4) | collective-permute-done | bytes 221216 | tf_op jit(solution)/shard_map/ppermute | solution.py:103
  10.8 3.1 %collective-permute-start.5 = (bf16[96,1152]{1,0:T(8,128)(2,1)S(1)}, bf16[96,1152]{1,0:T(8,128)(2,1)S(1)}, u32[]{:S(2)}, u32[]{:S(2)}) collective-permute-start(bf16[96,1152]{1,0:T(8,128)(2,1)S(1)} %pick_0.1.refs_7_), channel_id=1, source_target_pairs={{0,6},{1,7},{2,4},{3,5},{4,2},{5,3},{6,0},{7,1},{8,14},{9,15},{10,... | collective-permute-start | bytes 663560 | tf_op jit(solution)/shard_map/ppermute | solution.py:103
  14.3 2.0 %collective-permute-done.1.refs_1_.refs_7_ = bf16[112,1152]{1,0:T(8,128)(2,1)S(1)} collective-permute-done((bf16[112,1152]{1,0:T(8,128)(2,1)S(1)}, bf16[112,1152]{1,0:T(8,128)(2,1)S(1)}, u32[]{:S(2)}, u32[]{:S(2)}) %collective-permute-start.1) | collective-permute-done | bytes 258080 | tf_op jit(solution)/shard_map/ppermute | solution.py:103
  16.3 3.1 %collective-permute-start.10 = (bf16[112,1152]{1,0:T(8,128)(2,1)S(1)}, bf16[112,1152]{1,0:T(8,128)(2,1)S(1)}, u32[]{:S(2)}, u32[]{:S(2)}) collective-permute-start(bf16[112,1152]{1,0:T(8,128)(2,1)S(1)} %pick_96.1.refs_1_), channel_id=1, source_target_pairs={{0,6},{1,7},{2,4},{3,5},{4,2},{5,3},{6,0},{7,1},{8,14},{9,15},{10,... | collective-permute-start | bytes 774152 | tf_op jit(solution)/shard_map/ppermute | solution.py:103
  19.4 4.9 %collective-permute-done.refs_0_ = bf16[320,1152]{1,0:T(8,128)(2,1)S(1)} collective-permute-done((bf16[320,1152]{1,0:T(8,128)(2,1)}, bf16[320,1152]{1,0:T(8,128)(2,1)S(1)}, u32[]{:S(2)}, u32[]{:S(2)}) %collective-permute-start) | collective-permute-done | bytes 737312 | tf_op jit(solution)/shard_map/ppermute | solution.py:103
  24.6 3.1 %collective-permute-start.9 = (bf16[112,1152]{1,0:T(8,128)(2,1)S(1)}, bf16[112,1152]{1,0:T(8,128)(2,1)S(1)}, u32[]{:S(2)}, u32[]{:S(2)}) collective-permute-start(bf16[112,1152]{1,0:T(8,128)(2,1)S(1)} %pick_208.1), channel_id=1, source_target_pairs={{0,6},{1,7},{2,4},{3,5},{4,2},{5,3},{6,0},{7,1},{8,14},{9,15},{10,... | collective-permute-start | bytes 774152 | tf_op jit(solution)/shard_map/ppermute | solution.py:103
  29.0 2.5 %tiles.1 = (bf16[1280,1152]{1,0:T(8,128)(2,1)S(1)}, bf16[960,1152]{1,0:T(8,128)(2,1)S(1)}, bf16[960,1280]{1,0:T(8,128)(2,1)S(1)}, s32[8,1280]{1,0:T(8,128)}) custom-call(f32[1]{0:T(128)S(6)} %copy.39.refs_0_, f32[1]{0:T(128)S(6)} %copy.40.refs_1_, bf16[320,1152]{1,0:T(8,128)(2,1)S(1)} %gate_pair.1.refs_2_, ...), custom_call_target="tpu_custom_call", output_to_operand_aliasing={{0}: (9, {}), {1}: (10, {})} | custom-call | tf_op jit(solution)/shard_map/tiles/pallas_call | solution.py:70
  31.6 1.8 %mirror_first.1 = (bf16[960,1152]{1,0:T(8,128)(2,1)S(1)}, bf16[960,1280]{1,0:T(8,128)(2,1)S(1)}, bf16[96,1152]{1,0:T(8,128)(2,1)S(1)}) custom-call(f32[1]{0:T(128)S(6)} %copy.39.refs_0_, f32[1]{0:T(128)S(6)} %copy.40.refs_1_, bf16[1280,1152]{1,0:T(8,128)(2,1)S(1)} %get-tuple-element.23.refs_2_.refs_1_, ...), custom_call_target="tpu_custom_call", output_to_operand_aliasing={{0}: (5, {}), {1}: (6, {})} | custom-call | tf_op jit(solution)/shard_map/mirror_first/pallas_call | solution.py:70
  33.3 0.8 %collective-permute-start.11 = (bf16[96,1152]{1,0:T(8,128)(2,1)S(1)}, bf16[96,1152]{1,0:T(8,128)(2,1)S(1)}, u32[]{:S(2)}, u32[]{:S(2)}) collective-permute-start(bf16[96,1152]{1,0:T(8,128)(2,1)S(1)} %get-tuple-element.26.refs_1_.refs_6_), channel_id=1, source_target_pairs={{0,6},{1,7},{2,4},{3,5},{4,2},{5,3},{6,0},{7,1},{8,14},{9,15},{10,... | collective-permute-start | bytes 663560 | tf_op jit(solution)/shard_map/ppermute | solution.py:103
  34.4 1.9 %mirror_last.1 = (bf16[960,1152]{1,0:T(8,128)(2,1)S(1)}, bf16[960,1280]{1,0:T(8,128)(2,1)S(1)}, bf16[320,1152]{1,0:T(8,128)(2,1)S(1)}) custom-call(f32[1]{0:T(128)S(6)} %copy.39.refs_0_, f32[1]{0:T(128)S(6)} %copy.40.refs_1_, bf16[1280,1152]{1,0:T(8,128)(2,1)S(1)} %get-tuple-element.23.refs_2_.refs_1_, ...), custom_call_target="tpu_custom_call", output_to_operand_aliasing={{0}: (4, {}), {1}: (5, {})} | custom-call | tf_op jit(solution)/shard_map/mirror_last/pallas_call | solution.py:70
  36.4 0.9 %mirror_rest_grads.1 = (bf16[112,1152]{1,0:T(8,128)(2,1)S(1)}, bf16[112,1152]{1,0:T(8,128)(2,1)S(1)}) custom-call(bf16[960,1280]{1,0:T(8,128)(2,1)S(1)} %get-tuple-element.29.refs_0_, bf16[1280,1152]{1,0:T(8,128)(2,1)S(1)} %get-tuple-element.23.refs_2_.refs_1_), custom_call_target="tpu_custom_call" | custom-call | tf_op jit(solution)/shard_map/mirror_rest_grads/pallas_call | solution.py:70
  37.3 3.0 %collective-permute-start.13 = (bf16[112,1152]{1,0:T(8,128)(2,1)S(1)}, bf16[112,1152]{1,0:T(8,128)(2,1)S(1)}, u32[]{:S(2)}, u32[]{:S(2)}) collective-permute-start(bf16[112,1152]{1,0:T(8,128)(2,1)S(1)} %get-tuple-element.32.refs_2_), channel_id=1, source_target_pairs={{0,6},{1,7},{2,4},{3,5},{4,2},{5,3},{6,0},{7,1},{8,14},{9,15},{10,... | collective-permute-start | bytes 774152 | tf_op jit(solution)/shard_map/ppermute | solution.py:103
  40.3 0.6 next_text_first.1.refs_1_.refs_0_
  40.9 1.7 %collective-permute-done.11.refs_0_ = bf16[96,1152]{1,0:T(8,128)(2,1)S(1)} collective-permute-done((bf16[96,1152]{1,0:T(8,128)(2,1)S(1)}, bf16[96,1152]{1,0:T(8,128)(2,1)S(1)}, u32[]{:S(2)}, u32[]{:S(2)}) %collective-permute-start.11) | collective-permute-done | bytes 221216 | tf_op jit(solution)/shard_map/ppermute | solution.py:103
  42.6 1.1 %to_pair.1.refs_2_ = bf16[320,1152]{1,0:T(8,128)(2,1)S(1)} custom-call(bf16[960,1280]{1,0:T(8,128)(2,1)S(1)} %get-tuple-element.29.refs_0_, bf16[960,1152]{1,0:T(8,128)(2,1)S(1)} %get-tuple-element.30.refs_1_, bf16[320,1152]{1,0:T(8,128)(2,1)S(1)} %collective-permute-done.12.refs_2_, bf16[96,1152]{1,0:T(8,128)(2,1)S(1)} %gate_back_0.1.refs_3_.refs_1_.refs_0_), custom_call_target="tpu_custom_call" | custom-call | tf_op jit(solution)/shard_map/to_pair/pallas_call | solution.py:70
  44.0 0.3 collective-permute-start.16
  44.3 0.9 %next_text_rest.1.refs_0_ = f32[224,1152]{1,0:T(8,128)S(1)} custom-call(bf16[960,1280]{1,0:T(8,128)(2,1)S(1)} %get-tuple-element.29.refs_0_, bf16[1280,1152]{1,0:T(8,128)(2,1)S(1)} %get-tuple-element.23.refs_2_.refs_1_, bf16[112,1152]{1,0:T(8,128)(2,1)S(1)} %gate_g_2.1.refs_2_), custom_call_target="tpu_custom_call" | custom-call | tf_op jit(solution)/shard_map/next_text_rest/pallas_call | solution.py:70
  45.2 2.9 %collective-permute-done.13.refs_1_ = bf16[112,1152]{1,0:T(8,128)(2,1)S(1)} collective-permute-done((bf16[112,1152]{1,0:T(8,128)(2,1)S(1)}, bf16[112,1152]{1,0:T(8,128)(2,1)S(1)}, u32[]{:S(2)}, u32[]{:S(2)}) %collective-permute-start.13) | collective-permute-done | bytes 258080 | tf_op jit(solution)/shard_map/ppermute | solution.py:103
  48.3 1.2 %core_images.1 = bf16[320,1152]{1,0:T(8,128)(2,1)S(1)} custom-call(bf16[960,1280]{1,0:T(8,128)(2,1)S(1)} %get-tuple-element.29.refs_0_, bf16[960,1152]{1,0:T(8,128)(2,1)S(1)} %get-tuple-element.30.refs_1_, bf16[112,1152]{1,0:T(8,128)(2,1)S(1)} %to_prev_96.1.refs_2_), custom_call_target="tpu_custom_call" | custom-call | tf_op jit(solution)/shard_map/core_images/pallas_call | solution.py:70
  49.6 3.6 %collective-permute-done.16.refs_1_.refs_0_ = bf16[112,1152]{1,0:T(8,128)(2,1)S(1)} collective-permute-done((bf16[112,1152]{1,0:T(8,128)(2,1)S(1)}, bf16[112,1152]{1,0:T(8,128)(2,1)S(1)}, u32[]{:S(2)}, u32[]{:S(2)}) %collective-permute-start.16) | collective-permute-done | bytes 258080 | tf_op jit(solution)/shard_map/ppermute | solution.py:103
  53.4 1.2 %own_text_grads.1.refs_3_.gt = f32[320,1152]{1,0:T(8,128)S(1)} custom-call(bf16[960,1280]{1,0:T(8,128)(2,1)S(1)} %get-tuple-element.29.refs_0_, bf16[1280,1152]{1,0:T(8,128)(2,1)S(1)} %get-tuple-element.23.refs_2_.refs_1_, bf16[96,1152]{1,0:T(8,128)(2,1)S(1)} %gate_x_0.1.refs_2_), custom_call_target="tpu_custom_call" | custom-call | tf_op jit(solution)/shard_map/own_text_grads/pallas_call | solution.py:70
  54.7 1.2 %own_images.1.refs_1_.refs_0_ = f32[320,1152]{1,0:T(8,128)S(1)} custom-call(bf16[960,1280]{1,0:T(8,128)(2,1)S(1)} %get-tuple-element.29.refs_0_, bf16[960,1152]{1,0:T(8,128)(2,1)S(1)} %get-tuple-element.30.refs_1_, bf16[320,1152]{1,0:T(8,128)(2,1)S(1)} %collective-permute-done.14.refs_2_, f32[320,1152]{1,0:T(8,128)S(1)} %own_text_grads.1.refs_3_.gt), custom_call_target="tpu_custom_call" | custom-call | tf_op jit(solution)/shard_map/own_images/pallas_call | solution.py:70
  55.9 3.8 %collective-permute-done.18.refs_0_ = bf16[112,1152]{1,0:T(8,128)(2,1)S(1)} collective-permute-done((bf16[112,1152]{1,0:T(8,128)(2,1)S(1)}, bf16[112,1152]{1,0:T(8,128)(2,1)S(1)}, u32[]{:S(2)}, u32[]{:S(2)}) %collective-permute-start.18) | collective-permute-done | bytes 258080 | tf_op jit(solution)/shard_map/ppermute | solution.py:103
  59.7 1.1 %end_texts_first.1 = (f32[320,1152]{1,0:T(8,128)}, f32[8,128]{1,0:T(8,128)S(1)}) custom-call(f32[320,1152]{1,0:T(8,128)S(1)} %own_text_grads.1.refs_3_.gt, bf16[96,1152]{1,0:T(8,128)(2,1)S(1)} %gate_back_0.1.refs_3_.refs_1_.refs_0_, bf16[112,1152]{1,0:T(8,128)(2,1)S(1)} %collective-permute-done.13.refs_1_, bf16[96,1152]{1,0:T(8,128)(2,1)S(1)} %gate_x_0.1.refs_2_, ...), custom_call_target="tpu_custom_call" | custom-call | tf_op jit(solution)/shard_map/end_texts_first/pallas_call | solution.py:288
  61.0 1.3 %end_images.1 = (f32[320,1152]{1,0:T(8,128)}, f32[8,128]{1,0:T(8,128)S(1)}) custom-call(f32[320,1152]{1,0:T(8,128)S(1)} %own_images.1.refs_1_.refs_0_, bf16[320,1152]{1,0:T(8,128)(2,1)S(1)} %collective-permute-done.17.refs_1_, f32[8,128]{1,0:T(8,128)S(1)} %get-tuple-element.34.refs_2_), custom_call_target="tpu_custom_call" | custom-call | tf_op jit(solution)/shard_map/end_images/pallas_call | solution.py:70
  62.3 2.2 %collective-permute-done.19.refs_1_ = bf16[112,1152]{1,0:T(8,128)(2,1)S(1)} collective-permute-done((bf16[112,1152]{1,0:T(8,128)(2,1)S(1)}, bf16[112,1152]{1,0:T(8,128)(2,1)S(1)}, u32[]{:S(2)}, u32[]{:S(2)}) %collective-permute-start.19) | collective-permute-done | bytes 258080 | tf_op jit(solution)/shard_map/ppermute | solution.py:103
  64.5 0.9 %end_texts_last.1 = f32[320,1152]{1,0:T(8,128)} custom-call(f32[320,1152]{1,0:T(8,128)S(1)} %own_text_grads.1.refs_3_.gt, bf16[112,1152]{1,0:T(8,128)(2,1)S(1)} %collective-permute-done.16.refs_1_.refs_0_, bf16[112,1152]{1,0:T(8,128)(2,1)S(1)} %collective-permute-done.19.refs_1_, ...), custom_call_target="tpu_custom_call", output_to_operand_aliasing={{}: (3, {})} | custom-call | tf_op jit(solution)/shard_map/end_texts_last/pallas_call | solution.py:288
  (46 shorter events, 2.3 us)
Async XLA Ops:
  0.6 10.1 %collective-permute-start.3 = (bf16[320,1152]{1,0:T(8,128)(2,1)}, bf16[320,1152]{1,0:T(8,128)(2,1)S(1)}, u32[]{:S(2)}, u32[]{:S(2)}) collective-permute-start(bf16[320,1152]{1,0:T(8,128)(2,1)} %refs_2_.1), channel_id=1, source_target_pairs={{0,1},{1,0},{2,3},{3,2},{4,5},{5,4},{6,7},{7,6},{8,9},{9,8},{10,11... | collective-permute-start | bytes 2211848 | tf_op jit(solution)/shard_map/ppermute | solution.py:103
  0.7 1.1 %copy-start = (bf16[320,1152]{1,0:T(8,128)(2,1)S(1)}, bf16[320,1152]{1,0:T(8,128)(2,1)}, u32[]{:S(2)}) copy-start(bf16[320,1152]{1,0:T(8,128)(2,1)} %refs_0_.9) | copy-start | bytes 2211844
  1.9 8.9 %collective-permute-start.4 = (bf16[96,1152]{1,0:T(8,128)(2,1)S(1)}, bf16[96,1152]{1,0:T(8,128)(2,1)S(1)}, u32[]{:S(2)}, u32[]{:S(2)}) collective-permute-start(bf16[96,1152]{1,0:T(8,128)(2,1)S(1)} %cut_0.1.refs_1_.refs_0_.refs_4_), channel_id=1, source_target_pairs={{0,8},{1,9},{2,10},{3,11},{4,12},{5,13},{6,14},{7,15},{8,16},{9,17... | collective-permute-start | bytes 663560 | tf_op jit(solution)/shard_map/ppermute | solution.py:103
  5.0 3.4 %collective-permute-start.2 = (s32[320]{0:T(512)}, s32[320]{0:T(512)S(1)}, u32[]{:S(2)}, u32[]{:S(2)}) collective-permute-start(s32[320]{0:T(512)} %refs_0_.10), channel_id=1, source_target_pairs={{0,1},{1,0},{2,3},{3,2},{4,5},{5,4},{6,7},{7,6},{8,9},{9,8},{10,11... | collective-permute-start | bytes 3848 | tf_op jit(solution)/shard_map/ppermute | solution.py:103
  5.2 19.1 %collective-permute-start = (bf16[320,1152]{1,0:T(8,128)(2,1)}, bf16[320,1152]{1,0:T(8,128)(2,1)S(1)}, u32[]{:S(2)}, u32[]{:S(2)}) collective-permute-start(bf16[320,1152]{1,0:T(8,128)(2,1)} %refs_2_.1), channel_id=1, source_target_pairs={{0,2},{1,3},{2,0},{3,1},{4,6},{5,7},{6,4},{7,5},{8,10},{9,11},{10,... | collective-permute-start | bytes 2211848 | tf_op jit(solution)/shard_map/ppermute | solution.py:103
  6.8 9.5 %collective-permute-start.1 = (bf16[112,1152]{1,0:T(8,128)(2,1)S(1)}, bf16[112,1152]{1,0:T(8,128)(2,1)S(1)}, u32[]{:S(2)}, u32[]{:S(2)}) collective-permute-start(bf16[112,1152]{1,0:T(8,128)(2,1)S(1)} %cut_96.1.refs_1_.refs_5_.refs_0_), channel_id=1, source_target_pairs={{0,8},{1,9},{2,10},{3,11},{4,12},{5,13},{6,14},{7,15},{8,16},{9,17... | collective-permute-start | bytes 774152 | tf_op jit(solution)/shard_map/ppermute | solution.py:103
  8.4 5.5 %copy-start.1 = (bf16[320,1152]{1,0:T(8,128)(2,1)S(1)}, bf16[320,1152]{1,0:T(8,128)(2,1)}, u32[]{:S(2)}) copy-start(bf16[320,1152]{1,0:T(8,128)(2,1)} %refs_2_.1) | copy-start | bytes 2211844
  8.4 5.5 %copy-start.2 = (s32[320]{0:T(512)S(1)}, s32[320]{0:T(512)}, u32[]{:S(2)}) copy-start(s32[320]{0:T(512)} %refs_0_.10) | copy-start | bytes 3844
  8.4 15.9 %collective-permute-start.8 = (bf16[112,1152]{1,0:T(8,128)(2,1)S(1)}, bf16[112,1152]{1,0:T(8,128)(2,1)S(1)}, u32[]{:S(2)}, u32[]{:S(2)}) collective-permute-start(bf16[112,1152]{1,0:T(8,128)(2,1)S(1)} %cut_208.1.refs_6_.refs_0_), channel_id=1, source_target_pairs={{0,8},{1,9},{2,10},{3,11},{4,12},{5,13},{6,14},{7,15},{8,16},{9,17... | collective-permute-start | bytes 774152 | tf_op jit(solution)/shard_map/ppermute | solution.py:103
  10.8 8.6 %collective-permute-start.5 = (bf16[96,1152]{1,0:T(8,128)(2,1)S(1)}, bf16[96,1152]{1,0:T(8,128)(2,1)S(1)}, u32[]{:S(2)}, u32[]{:S(2)}) collective-permute-start(bf16[96,1152]{1,0:T(8,128)(2,1)S(1)} %pick_0.1.refs_7_), channel_id=1, source_target_pairs={{0,6},{1,7},{2,4},{3,5},{4,2},{5,3},{6,0},{7,1},{8,14},{9,15},{10,... | collective-permute-start | bytes 663560 | tf_op jit(solution)/shard_map/ppermute | solution.py:103
  14.0 10.5 %collective-permute-start.7 = (s32[8,640]{1,0:T(8,128)S(1)}, s32[8,640]{1,0:T(8,128)S(1)}, u32[]{:S(2)}, u32[]{:S(2)}) collective-permute-start(s32[8,640]{1,0:T(8,128)S(1)} %get-tuple-element.20.refs_2_.refs_4_), channel_id=1, source_target_pairs={{0,2},{1,3},{2,0},{3,1},{4,6},{5,7},{6,4},{7,5},{8,10},{9,11},{10,... | collective-permute-start | bytes 61448 | tf_op jit(solution)/shard_map/ppermute | solution.py:103
  16.3 15.2 %collective-permute-start.10 = (bf16[112,1152]{1,0:T(8,128)(2,1)S(1)}, bf16[112,1152]{1,0:T(8,128)(2,1)S(1)}, u32[]{:S(2)}, u32[]{:S(2)}) collective-permute-start(bf16[112,1152]{1,0:T(8,128)(2,1)S(1)} %pick_96.1.refs_1_), channel_id=1, source_target_pairs={{0,6},{1,7},{2,4},{3,5},{4,2},{5,3},{6,0},{7,1},{8,14},{9,15},{10,... | collective-permute-start | bytes 774152 | tf_op jit(solution)/shard_map/ppermute | solution.py:103
  24.3 4.7 %collective-permute-start.6 = (bf16[320,1152]{1,0:T(8,128)(2,1)S(1)}, bf16[320,1152]{1,0:T(8,128)(2,1)S(1)}, u32[]{:S(2)}, u32[]{:S(2)}) collective-permute-start(bf16[320,1152]{1,0:T(8,128)(2,1)S(1)} %gate_pair.1.refs_2_), channel_id=1, source_target_pairs={{0,1},{1,0},{2,3},{3,2},{4,5},{5,4},{6,7},{7,6},{8,9},{9,8},{10,11... | collective-permute-start | bytes 2211848 | tf_op jit(solution)/shard_map/ppermute | solution.py:103
  24.6 9.8 %collective-permute-start.9 = (bf16[112,1152]{1,0:T(8,128)(2,1)S(1)}, bf16[112,1152]{1,0:T(8,128)(2,1)S(1)}, u32[]{:S(2)}, u32[]{:S(2)}) collective-permute-start(bf16[112,1152]{1,0:T(8,128)(2,1)S(1)} %pick_208.1), channel_id=1, source_target_pairs={{0,6},{1,7},{2,4},{3,5},{4,2},{5,3},{6,0},{7,1},{8,14},{9,15},{10,... | collective-permute-start | bytes 774152 | tf_op jit(solution)/shard_map/ppermute | solution.py:103
  33.3 9.3 %collective-permute-start.11 = (bf16[96,1152]{1,0:T(8,128)(2,1)S(1)}, bf16[96,1152]{1,0:T(8,128)(2,1)S(1)}, u32[]{:S(2)}, u32[]{:S(2)}) collective-permute-start(bf16[96,1152]{1,0:T(8,128)(2,1)S(1)} %get-tuple-element.26.refs_1_.refs_6_), channel_id=1, source_target_pairs={{0,6},{1,7},{2,4},{3,5},{4,2},{5,3},{6,0},{7,1},{8,14},{9,15},{10,... | collective-permute-start | bytes 663560 | tf_op jit(solution)/shard_map/ppermute | solution.py:103
  36.3 6.3 %collective-permute-start.12 = (bf16[320,1152]{1,0:T(8,128)(2,1)S(1)}, bf16[320,1152]{1,0:T(8,128)(2,1)S(1)}, u32[]{:S(2)}, u32[]{:S(2)}) collective-permute-start(bf16[320,1152]{1,0:T(8,128)(2,1)S(1)} %get-tuple-element.33), channel_id=1, source_target_pairs={{0,1},{1,0},{2,3},{3,2},{4,5},{5,4},{6,7},{7,6},{8,9},{9,8},{10,11... | collective-permute-start | bytes 2211848 | tf_op jit(solution)/shard_map/ppermute | solution.py:103
  37.3 10.8 %collective-permute-start.13 = (bf16[112,1152]{1,0:T(8,128)(2,1)S(1)}, bf16[112,1152]{1,0:T(8,128)(2,1)S(1)}, u32[]{:S(2)}, u32[]{:S(2)}) collective-permute-start(bf16[112,1152]{1,0:T(8,128)(2,1)S(1)} %get-tuple-element.32.refs_2_), channel_id=1, source_target_pairs={{0,6},{1,7},{2,4},{3,5},{4,2},{5,3},{6,0},{7,1},{8,14},{9,15},{10,... | collective-permute-start | bytes 774152 | tf_op jit(solution)/shard_map/ppermute | solution.py:103
  43.8 17.2 %collective-permute-start.17 = (bf16[320,1152]{1,0:T(8,128)(2,1)S(1)}, bf16[320,1152]{1,0:T(8,128)(2,1)S(1)}, u32[]{:S(2)}, u32[]{:S(2)}) collective-permute-start(bf16[320,1152]{1,0:T(8,128)(2,1)S(1)} %to_pair.1.refs_2_), channel_id=1, source_target_pairs={{0,2},{1,3},{2,0},{3,1},{4,6},{5,7},{6,4},{7,5},{8,10},{9,11},{10,... | collective-permute-start | bytes 2211848 | tf_op jit(solution)/shard_map/ppermute | solution.py:103
  43.9 9.5 %collective-permute-start.15 = (bf16[96,1152]{1,0:T(8,128)(2,1)S(1)}, bf16[96,1152]{1,0:T(8,128)(2,1)S(1)}, u32[]{:S(2)}, u32[]{:S(2)}) collective-permute-start(bf16[96,1152]{1,0:T(8,128)(2,1)S(1)} %to_prev_0.1.refs_1_.refs_2_), channel_id=1, source_target_pairs={{0,248},{1,249},{2,250},{3,251},{4,252},{5,253},{6,254},{7,255},{8... | collective-permute-start | bytes 663560 | tf_op jit(solution)/shard_map/ppermute | solution.py:103
  44.0 9.3 %collective-permute-start.16 = (bf16[112,1152]{1,0:T(8,128)(2,1)S(1)}, bf16[112,1152]{1,0:T(8,128)(2,1)S(1)}, u32[]{:S(2)}, u32[]{:S(2)}) collective-permute-start(bf16[112,1152]{1,0:T(8,128)(2,1)S(1)} %gate_g_2.1.refs_2_), channel_id=1, source_target_pairs={{0,6},{1,7},{2,4},{3,5},{4,2},{5,3},{6,0},{7,1},{8,14},{9,15},{10,... | collective-permute-start | bytes 774152 | tf_op jit(solution)/shard_map/ppermute | solution.py:103
  48.2 11.5 %collective-permute-start.18 = (bf16[112,1152]{1,0:T(8,128)(2,1)S(1)}, bf16[112,1152]{1,0:T(8,128)(2,1)S(1)}, u32[]{:S(2)}, u32[]{:S(2)}) collective-permute-start(bf16[112,1152]{1,0:T(8,128)(2,1)S(1)} %to_prev_96.1.refs_2_), channel_id=1, source_target_pairs={{0,248},{1,249},{2,250},{3,251},{4,252},{5,253},{6,254},{7,255},{8... | collective-permute-start | bytes 774152 | tf_op jit(solution)/shard_map/ppermute | solution.py:103
  49.5 5.1 %collective-permute-start.14 = (bf16[320,1152]{1,0:T(8,128)(2,1)S(1)}, bf16[320,1152]{1,0:T(8,128)(2,1)S(1)}, u32[]{:S(2)}, u32[]{:S(2)}) collective-permute-start(bf16[320,1152]{1,0:T(8,128)(2,1)S(1)} %core_images.1), channel_id=1, source_target_pairs={{0,1},{1,0},{2,3},{3,2},{4,5},{5,4},{6,7},{7,6},{8,9},{9,8},{10,11... | collective-permute-start | bytes 2211848 | tf_op jit(solution)/shard_map/ppermute | solution.py:103
  53.3 11.2 %collective-permute-start.19 = (bf16[112,1152]{1,0:T(8,128)(2,1)S(1)}, bf16[112,1152]{1,0:T(8,128)(2,1)S(1)}, u32[]{:S(2)}, u32[]{:S(2)}) collective-permute-start(bf16[112,1152]{1,0:T(8,128)(2,1)S(1)} %to_prev_208.1.refs_1_), channel_id=1, source_target_pairs={{0,248},{1,249},{2,250},{3,251},{4,252},{5,253},{6,254},{7,255},{8... | collective-permute-start | bytes 774152 | tf_op jit(solution)/shard_map/ppermute | solution.py:103
